TPU v7x, 128 devices: a whole 4x4x4 slice. The times are simulated.
128 devices in a mesh: nodes: 32 (over z, x, core), batch: 4 (over y).
Axes of the slice: x: 4, y: 4, z: 4, core: 2. Of those that a mesh axis runs over, the one named last changes fastest.
Arguments:
- node_latents: bfloat16 [4, 8192, 512], P('batch', 'nodes'), may hold values from -6 to 6
- edge_latents: bfloat16 [4, 65536, 512], P('batch', 'nodes'), may hold values from -6 to 6
- node_cotangent: bfloat16 [4, 8192, 512], P('batch', 'nodes'), may hold values from -6 to 6
- edge_cotangent: bfloat16 [4, 65536, 512], P('batch', 'nodes'), may hold values from -6 to 6
- senders: int32 [65536], P('nodes'), may hold values from 0 to 767, as said below
- receivers: int32 [65536], P('nodes'), may hold values from 0 to 255, as said below
- send_rows: int32 [32, 32, 16], P('nodes'), may hold values from 0 to 255, as said below
- edge_weight_in: bfloat16 [1536, 512], replicated, may hold values from -0.15625 to 0.15625
- edge_bias: float32 [512], replicated, may hold values from -3 to 3
- edge_weight_out: bfloat16 [512, 512], replicated, may hold values from -0.25 to 0.25
- edge_gain: float32 [512], replicated, may hold values from 0.5 to 1.5
- node_weight_in: bfloat16 [1024, 512], replicated, may hold values from -0.1875 to 0.1875
- node_bias: float32 [512], replicated, may hold values from -3 to 3
- node_weight_out: bfloat16 [512, 512], replicated, may hold values from -0.25 to 0.25
- node_gain: float32 [512], replicated, may hold values from 0.5 to 1.5
Outputs:
- grad_nodes: bfloat16 [4, 8192, 512], P('batch', 'nodes')
- grad_edges: bfloat16 [4, 65536, 512], P('batch', 'nodes')
- grad_edge_weight_in: float32 [1536, 512], P(('nodes', 'batch'))
- grad_edge_bias: float32 [512], P(('nodes', 'batch'))
- grad_edge_weight_out: float32 [512, 512], P(('nodes', 'batch'))
- grad_edge_gain: float32 [512], P(('nodes', 'batch'))
- grad_node_weight_in: float32 [1024, 512], P(('nodes', 'batch'))
- grad_node_bias: float32 [512], P(('nodes', 'batch'))
- grad_node_weight_out: float32 [512, 512], P(('nodes', 'batch'))
- grad_node_gain: float32 [512], P(('nodes', 'batch'))
Inputs may be any that keep to these rules, and one draw needn't show every extreme that they name: `senders`: values below 256 are rows of the edge's own device; a value 256 + p * 16 + s names slot s of the list that peer p holds for the edge's device, p never the edge's own device. Most remote edges name the two devices beside the owner in index order (cyclically); the rest name any device. Slots that no edge names carry padding rows. `receivers`: rows of the edge's own device. send_rows[p, d, s] is a row of device p; rows may repeat.
All inputs are finite; a program needn't handle non-finite values.
Results may differ from a plain program's by a relative error of at most 0.012.
Values may be sent and summed in bfloat16 or wider, within the bound.
No kernel may reach another device: no remote copies, remote signals or barrier semaphores. Data moves between devices by JAX's collectives and lax.ppermute only.
A program may use at most 128 MiB of HBM per device.

v0:
```python
import math

import jax
import jax.numpy as jnp
from jax import lax
from jax.sharding import PartitionSpec as P

EPS = 1e-05


def silu_slope(values):
    sigmoid_v = jax.nn.sigmoid(values)
    return sigmoid_v * (1.0 + values * (1.0 - sigmoid_v))


def mlp_forward(layer_input, weight_in, bias_vec, weight_out):
    pre_act = jnp.dot(layer_input, weight_in, preferred_element_type=jnp.float32) + bias_vec
    activation = jax.nn.silu(pre_act).astype(jnp.bfloat16)
    pre_norm = jnp.dot(activation, weight_out, preferred_element_type=jnp.float32)
    row_mean = jnp.mean(pre_norm, axis=-1, keepdims=True)
    centred = pre_norm - row_mean
    inv_scale = lax.rsqrt(jnp.mean(centred * centred, axis=-1, keepdims=True) + EPS)
    return (pre_act, activation, centred * inv_scale, inv_scale)


def mlp_backward(
    layer_input, pre_act, activation, normed, inv_scale, weight_in, weight_out, gain_vec, grad_out
):
    dims_rows = (((0,), (0,)), ((), ()))
    dims_cols = (((1,), (1,)), ((), ()))
    grad_gain = jnp.sum(grad_out * normed, axis=0)
    scaled = grad_out * gain_vec
    grad_norm = (
        (
            scaled
            - jnp.mean(scaled, axis=-1, keepdims=True)
            - normed * jnp.mean(scaled * normed, axis=-1, keepdims=True)
        )
        * inv_scale
    ).astype(jnp.bfloat16)
    grad_second = lax.dot_general(
        activation, grad_norm, dims_rows, preferred_element_type=jnp.float32
    )
    grad_act = lax.dot_general(grad_norm, weight_out, dims_cols, preferred_element_type=jnp.float32)
    grad_pre = (grad_act * silu_slope(pre_act)).astype(jnp.bfloat16)
    grad_bias = jnp.sum(grad_pre.astype(jnp.float32), axis=0)
    grad_first = lax.dot_general(
        layer_input, grad_pre, dims_rows, preferred_element_type=jnp.float32
    )
    grad_input = lax.dot_general(grad_pre, weight_in, dims_cols, preferred_element_type=jnp.float32)
    return (grad_input, grad_first, grad_bias, grad_second, grad_gain)


def shards(
    node_latents,
    edge_latents,
    node_cotangent,
    edge_cotangent,
    senders,
    receivers,
    send_rows,
    edge_weight_in,
    edge_bias,
    edge_weight_out,
    edge_gain,
    node_weight_in,
    node_bias,
    node_weight_out,
    node_gain,
):
    feature_count = node_latents.shape[2]
    node_count = node_latents.shape[1]
    part_count = lax.axis_size("nodes")
    hidden_rows = node_latents[0]
    row_lists = send_rows[0]
    capacity = row_lists.shape[1]
    all_nodes = lax.all_gather(hidden_rows, "nodes", axis=0, tiled=True)
    incoming = lax.all_to_all(row_lists, "nodes", split_axis=0, concat_axis=0, tiled=True)
    own_index = lax.axis_index("nodes")
    halo_slot = jnp.maximum(senders - node_count, 0)
    peer_part = halo_slot // capacity
    listed = incoming[peer_part, halo_slot % capacity]
    global_index = jnp.where(
        senders >= node_count, peer_part * node_count + listed, own_index * node_count + senders
    )
    sender_rows = all_nodes[global_index]
    edge_rows = edge_latents[0]
    edge_cot = edge_cotangent[0].astype(jnp.float32)
    node_cot = node_cotangent[0].astype(jnp.float32)
    edge_input = jnp.concatenate([edge_rows, sender_rows, hidden_rows[receivers]], axis=1)
    edge_pre, edge_act, edge_norm, edge_inv = mlp_forward(
        edge_input, edge_weight_in, edge_bias, edge_weight_out
    )
    message = (edge_norm * edge_gain).astype(jnp.bfloat16)
    onehot = (receivers[:, None] == jnp.arange(node_count, dtype=jnp.int32)[None, :]).astype(
        jnp.bfloat16
    )
    aggregate = lax.dot_general(
        onehot, message, (((0,), (0,)), ((), ())), preferred_element_type=jnp.float32
    ).astype(jnp.bfloat16)
    node_input = jnp.concatenate([hidden_rows, aggregate], axis=1)
    node_pre, node_act, node_norm, node_inv = mlp_forward(
        node_input, node_weight_in, node_bias, node_weight_out
    )
    node_grads = mlp_backward(
        node_input,
        node_pre,
        node_act,
        node_norm,
        node_inv,
        node_weight_in,
        node_weight_out,
        node_gain,
        node_cot,
    )
    node_grad_input = node_grads[0]
    message_grad = edge_cot + node_grad_input[:, feature_count:][receivers]
    edge_grads = mlp_backward(
        edge_input,
        edge_pre,
        edge_act,
        edge_norm,
        edge_inv,
        edge_weight_in,
        edge_weight_out,
        edge_gain,
        message_grad,
    )
    edge_grad_input = edge_grads[0]
    grad_edges = (edge_cot + edge_grad_input[:, :feature_count]).astype(jnp.bfloat16)
    sender_grad = edge_grad_input[:, feature_count : 2 * feature_count]
    node_total = (
        node_cot
        + node_grad_input[:, :feature_count]
        + jax.ops.segment_sum(edge_grad_input[:, 2 * feature_count :], receivers, node_count)
    )
    node_terms = jax.ops.segment_sum(sender_grad, global_index, node_count * part_count)
    node_total = node_total + lax.psum_scatter(
        node_terms.astype(jnp.bfloat16), "nodes", scatter_dimension=0, tiled=True
    ).astype(jnp.float32)
    grad_nodes = node_total.astype(jnp.bfloat16)
    shares = (
        lax.psum_scatter(edge_grads[1], ("nodes", "batch"), scatter_dimension=0, tiled=True),
        lax.psum_scatter(edge_grads[2], ("nodes", "batch"), scatter_dimension=0, tiled=True),
        lax.psum_scatter(edge_grads[3], ("nodes", "batch"), scatter_dimension=0, tiled=True),
        lax.psum_scatter(edge_grads[4], ("nodes", "batch"), scatter_dimension=0, tiled=True),
        lax.psum_scatter(node_grads[1], ("nodes", "batch"), scatter_dimension=0, tiled=True),
        lax.psum_scatter(node_grads[2], ("nodes", "batch"), scatter_dimension=0, tiled=True),
        lax.psum_scatter(node_grads[3], ("nodes", "batch"), scatter_dimension=0, tiled=True),
        lax.psum_scatter(node_grads[4], ("nodes", "batch"), scatter_dimension=0, tiled=True),
    )
    total_edges = senders.shape[0] * part_count
    factor = 1.0 / math.sqrt(lax.axis_size("batch") * total_edges)
    scaled_shares = [item * factor for item in shares]
    return (
        grad_nodes[None],
        grad_edges[None],
        scaled_shares[0],
        scaled_shares[1],
        scaled_shares[2],
        scaled_shares[3],
        scaled_shares[4],
        scaled_shares[5],
        scaled_shares[6],
        scaled_shares[7],
    )


def solution(mesh):
    return jax.shard_map(
        shards,
        mesh=mesh,
        in_specs=(
            P("batch", "nodes", None),
            P("batch", "nodes", None),
            P("batch", "nodes", None),
            P("batch", "nodes", None),
            P("nodes"),
            P("nodes"),
            P("nodes", None, None),
            P(),
            P(),
            P(),
            P(),
            P(),
            P(),
            P(),
            P(),
        ),
        out_specs=(
            P("batch", "nodes", None),
            P("batch", "nodes", None),
            P(("nodes", "batch"), None),
            P(("nodes", "batch")),
            P(("nodes", "batch"), None),
            P(("nodes", "batch")),
            P(("nodes", "batch"), None),
            P(("nodes", "batch")),
            P(("nodes", "batch"), None),
            P(("nodes", "batch")),
        ),
        check_vma=False,
    )
```

profile of v0, /device:TPU:0, one launch (start us, length us, event | category | flops | bytes accessed | tf_op | source)
XLA Modules:
  0.0 1028.3 jit_solution(12242912899697292486)
XLA Ops:
  7.9 1.4 copy.33
  9.3 8.2 all-to-all-start
  19.0 4.0 copy.35
  23.1 9.2 gather_fusion.2
  32.3 14.1 %gather_fusion = s32[2048]{0:T(1024)S(1)} fusion(s32[32,16]{0,1:T(8,128)S(1)} %bitcast.48, s32[2048]{0:T(1024)S(1)} %fusion.31), kind=kCustom, calls=%fused_computation | custom fusion | bytes 32768 | tf_op jit(solution)/shard_map/gather | solution.py:82
  46.4 19.4 %all-gather.3.cloned.1.call-done = bf16[1,8192,512]{2,1,0:T(8,128)(2,1)} async-done(((bf16[1,256,512]{2,1,0:T(8,128)(2,1)}), bf16[1,8192,512]{2,1,0:T(8,128)(2,1)}) %all-gather.3.cloned.1.call-update) | async-done | bytes 8388624 | tf_op jit(solution)/shard_map/all_gather | solution.py:77
  65.8 13.7 %gather_fusion.1 = bf16[2048,512]{1,0:T(8,128)(2,1)} fusion(bf16[8192,512]{1,0:T(8,128)(2,1)} %bitcast.52, s32[2048]{0:T(1024)S(1)} %get-tuple-element.52), kind=kCustom, calls=%fused_computation.1 | custom fusion | bytes 4202496 | tf_op jit(solution)/shard_map/gather | solution.py:86
  79.6 7.3 multiply_convert_fusion.3
  86.9 1.3 fusion.45
  89.1 1.4 fusion.16
  92.5 1.6 fusion.41
  94.6 8.9 gather_fusion.3
  103.5 5.8 copy.36
  109.3 5.8 multiply_reduce_fusion
  116.4 1.6 multiply_convert_fusion.1
  118.0 1.4 copy-done.8
  119.4 2.3 fusion.49
  121.8 1.8 fusion.28
  123.6 5.6 convert_reduce_fusion
  129.2 6.9 fusion.48
  136.1 20.3 %scatter_custom_fusion = f32[8192,512]{1,0:T(8,128)} fusion(s32[2048]{0:T(1024)S(1)} %get-tuple-element.53, f32[]{:T(128)} %constant.61.clone.1, f32[2048,1536]{1,0:T(8,128)} %fusion.48), kind=kCustom, calls=%fused_computation.6 | custom fusion | flops 1048576 | bytes 20972032 | tf_op jit(solution)/shard_map/scatter-add | solution.py:137
  156.4 9.0 convert_element_type.67
  165.5 8.6 fusion.7
  174.1 342.6 %fusion = f32[16,512]{1,0:T(8,128)S(1)} fusion(f32[1536,512]{1,0:T(8,128)} %fusion.7), kind=kCustom, calls=%all-reduce-scatter | all-reduce-scatter fusion | flops 1048577 | bytes 3178496
  516.7 1.3 collective-permute-start.30
  518.0 1.3 collective-permute-start.31
  519.3 1.3 collective-permute-start.29
  520.6 1.3 collective-permute-start.28
  525.8 4.6 slice.32
  530.5 5.4 copy.39
  538.5 12.5 %collective-permute-start.22 = (f32[16,512]{1,0:T(8,128)S(1)}, f32[16,512]{1,0:T(8,128)S(1)}, u32[]{:S(2)}, u32[]{:S(2)}) collective-permute-start(f32[16,512]{1,0:T(8,128)S(1)} %fusion), channel_id=1, source_target_pairs={{0,23},{1,24},{2,25},{3,26},{4,27},{5,28},{6,29},{7,30},{8,31},{9,... | collective-permute-start | bytes 98312
  551.0 3.2 collective-permute-start.21
  554.2 2.2 collective-permute-start.20
  556.4 5.0 fusion.10
  561.4 63.8 %all-reduce.8 = (f32[512]{0:T(512)S(1)}, f32[512]{0:T(512)}, f32[512]{0:T(512)S(1)}, f32[512]{0:T(512)S(1)}) all-reduce(f32[512]{0:T(512)S(1)} %get-tuple-element.60, f32[512]{0:T(512)S(1)} %get-tuple-element.40, f32[512]{0:T(512)S(1)} %get-tuple-element.62, ...), channel_id=5, replica_groups=mesh['nodes'=32,'batch'=4] {'nodes','batch'}, use_global_device_ids=true, to_apply=%region_13.14.clone | all-reduce | flops 2048 | bytes 16384
  625.2 2.6 collective-permute-start.19
  627.8 5.1 collective-permute-start.18
  632.9 4.4 collective-permute-start.17
  637.3 3.1 collective-permute-start.16
  640.4 4.1 collective-permute-start.15
  645.1 3.9 collective-permute-start.14
  649.0 3.6 collective-permute-start.13
  652.6 3.7 collective-permute-start.12
  656.3 1.9 collective-permute-start.11
  658.3 4.8 collective-permute-start.10
  664.3 1.9 collective-permute-start.9
  666.2 2.9 collective-permute-start.8
  669.1 2.5 collective-permute-start.7
  671.6 3.4 collective-permute-start.6
  675.0 2.0 collective-permute-start.5
  677.7 3.3 collective-permute-start.4
  681.0 2.0 collective-permute-start.3
  683.0 5.0 collective-permute-start.2
  688.1 2.6 collective-permute-start.1
  690.7 2.7 collective-permute-start
  694.0 3.9 copy.38
  698.0 45.6 %concatenate.14 = f32[524,512]{1,0:T(8,128)} concatenate(f32[12,512]{1,0:T(8,128)S(1)} %collective-permute-done.31, f32[16,512]{1,0:T(8,128)S(1)} %collective-permute-done.30, f32[16,512]{1,0:T(8,128)S(1)} %collective-permute-done.29, f32[16,512]{1,0:T(8,128)S(1)} %collective-permute-done.28, f32[16,512]{1,0:T(8,128)S(1)} %collective-permute-done.27, ...), dimensions={0} | concatenate | bytes 2146304
  743.5 1.4 dynamic-slice_multiply_fusion
  744.9 1.3 dynamic-slice_multiply_fusion.2
  746.3 1.3 dynamic-slice_multiply_fusion.1
  747.6 167.5 %reduce-scatter.7.cloned.1.call-done = f32[8,512]{1,0:T(8,128)} async-done(((f32[1024,512]{1,0:T(8,128)}), f32[8,512]{1,0:T(8,128)}) %reduce-scatter.7.cloned.1.call-update) | async-done | bytes 16400 | tf_op jit(solution)/shard_map/reduce_scatter | solution.py:147
  915.1 1.3 broadcast_multiply_fusion
  916.4 89.7 %reduce-scatter.5.cloned.1.call-done = bf16[256,512]{1,0:T(8,128)(2,1)} async-done(((bf16[8192,512]{1,0:T(8,128)(2,1)}), bf16[256,512]{1,0:T(8,128)(2,1)}) %reduce-scatter.5.cloned.1.call-update) | async-done | bytes 262160 | tf_op jit(solution)/shard_map/reduce_scatter | solution.py:138
  1007.1 13.7 %scatter_custom_fusion.1 = f32[256,512]{1,0:T(8,128)S(1)} fusion(f32[256,512]{1,0:T(8,128)S(1)} %fusion.26, s32[2048]{0:T(1024)S(1)} %copy-done.26, f32[2048,1536]{1,0:T(8,128)} %fusion.48), kind=kCustom, calls=%fused_computation.12 | custom fusion | flops 1048576 | bytes 4718592 | tf_op jit(solution)/shard_map/scatter-add | solution.py:135
  (138 shorter events, 18.3 us)
Async XLA Ops:
  7.2 72.4 %copy-start = (bf16[1536,512]{1,0:T(8,128)(2,1)S(1)}, bf16[1536,512]{1,0:T(8,128)(2,1)}, u32[]{:S(2)}) copy-start(bf16[1536,512]{1,0:T(8,128)(2,1)} %param.22) | copy-start | bytes 4718596
  7.2 15.9 %copy-start.1 = (bf16[1,256,512]{2,1,0:T(8,128)(2,1)S(1)}, bf16[1,256,512]{2,1,0:T(8,128)(2,1)}, u32[]{:S(2)}) copy-start(bf16[1,256,512]{2,1,0:T(8,128)(2,1)} %param.15) | copy-start | bytes 786436
  7.2 58.6 %all-gather.3.cloned.1.call-start = ((), (), s32[]{:S(2)}) async-start(), calls=%async_computation.5 | async-start | bytes 8650752 | tf_op jit(solution)/shard_map/all_gather | solution.py:77
  9.3 22.9 %all-to-all-start = ((s32[32,1,16]{2,1,0:T(1,128)}), s32[32,1,16]{2,1,0:T(1,128)S(1)}, u32[]{:S(2)}, u32[]{:S(2)}) async-start(s32[32,1,16]{2,1,0:T(1,128)} %bitcast.5), calls=%async_computation | async-start | bytes 32768 | tf_op jit(solution)/shard_map/all_to_all | solution.py:78
  17.6 727.4 %all-reduce.12.cloned.1.call-start = ((), (), s32[]{:S(2)}) async-start(), calls=%async_computation.6 | async-start | bytes 4194304
  32.3 14.1 %copy-start.25 = (s32[2048]{0:T(1024)S(1)}, s32[2048]{0:T(1024)}, u32[]{:S(2)}) copy-start(s32[2048]{0:T(1024)} %param.19) | copy-start | bytes 24580
  65.8 13.8 %copy-start.31 = (f32[512]{0:T(512)S(1)}, f32[512]{0:T(512)}, u32[]{:S(2)}) copy-start(f32[512]{0:T(512)} %param.23) | copy-start | bytes 6148
  79.6 7.4 copy-start.14
  88.3 2.2 copy-start.2
  88.3 2.1 copy-start.9
  88.4 2.1 copy-start.30
  88.9 2.1 copy-start.29
  90.5 2.0 copy-start.15
  92.5 1.6 copy-start.12
  109.3 5.8 copy-start.3
  109.3 6.5 copy-start.4
  109.3 7.1 copy-start.5
  116.4 3.0 copy-start.7
  119.4 2.4 copy-start.13
  119.4 2.4 copy-start.16
  121.7 793.4 %reduce-scatter.7.cloned.1.call-start = ((), (), s32[]{:S(2)}) async-start(), calls=%async_computation.4 | async-start | bytes 2113536 | tf_op jit(solution)/shard_map/reduce_scatter | solution.py:147
  123.6 882.5 %reduce-scatter.5.cloned.1.call-start = ((), (), s32[]{:S(2)}) async-start(), calls=%async_computation.3 | async-start | bytes 8650752 | tf_op jit(solution)/shard_map/reduce_scatter | solution.py:138
  129.2 6.9 copy-start.32
  516.7 7.8 collective-permute-start.30
  518.0 5.2 collective-permute-start.31
  519.3 16.6 %collective-permute-start.29 = (f32[16,512]{1,0:T(8,128)S(1)}, f32[16,512]{1,0:T(8,128)S(1)}, u32[]{:S(2)}, u32[]{:S(2)}) collective-permute-start(f32[16,512]{1,0:T(8,128)S(1)} %fusion), channel_id=1, source_target_pairs={{0,30},{1,31},{2,32},{3,33},{4,34},{5,35},{6,36},{7,37},{8,38},{9,... | collective-permute-start | bytes 98312
  520.6 16.6 %collective-permute-start.28 = (f32[16,512]{1,0:T(8,128)S(1)}, f32[16,512]{1,0:T(8,128)S(1)}, u32[]{:S(2)}, u32[]{:S(2)}) collective-permute-start(f32[16,512]{1,0:T(8,128)S(1)} %fusion), channel_id=1, source_target_pairs={{0,29},{1,30},{2,31},{3,32},{4,33},{5,34},{6,35},{7,36},{8,37},{9,... | collective-permute-start | bytes 98312
  521.9 16.6 %collective-permute-start.27 = (f32[16,512]{1,0:T(8,128)S(1)}, f32[16,512]{1,0:T(8,128)S(1)}, u32[]{:S(2)}, u32[]{:S(2)}) collective-permute-start(f32[16,512]{1,0:T(8,128)S(1)} %fusion), channel_id=1, source_target_pairs={{0,28},{1,29},{2,30},{3,31},{4,32},{5,33},{6,34},{7,35},{8,36},{9,... | collective-permute-start | bytes 98312
  523.2 27.8 %collective-permute-start.26 = (f32[16,512]{1,0:T(8,128)S(1)}, f32[16,512]{1,0:T(8,128)S(1)}, u32[]{:S(2)}, u32[]{:S(2)}) collective-permute-start(f32[16,512]{1,0:T(8,128)S(1)} %fusion), channel_id=1, source_target_pairs={{0,27},{1,28},{2,29},{3,30},{4,31},{5,32},{6,33},{7,34},{8,35},{9,... | collective-permute-start | bytes 98312
  524.5 29.7 %collective-permute-start.25 = (f32[16,512]{1,0:T(8,128)S(1)}, f32[16,512]{1,0:T(8,128)S(1)}, u32[]{:S(2)}, u32[]{:S(2)}) collective-permute-start(f32[16,512]{1,0:T(8,128)S(1)} %fusion), channel_id=1, source_target_pairs={{0,26},{1,27},{2,28},{3,29},{4,30},{5,31},{6,32},{7,33},{8,34},{9,... | collective-permute-start | bytes 98312
  535.9 89.3 %collective-permute-start.24 = (f32[16,512]{1,0:T(8,128)S(1)}, f32[16,512]{1,0:T(8,128)S(1)}, u32[]{:S(2)}, u32[]{:S(2)}) collective-permute-start(f32[16,512]{1,0:T(8,128)S(1)} %fusion), channel_id=1, source_target_pairs={{0,25},{1,26},{2,27},{3,28},{4,29},{5,30},{6,31},{7,32},{8,33},{9,... | collective-permute-start | bytes 98312
  537.2 90.6 %collective-permute-start.23 = (f32[16,512]{1,0:T(8,128)S(1)}, f32[16,512]{1,0:T(8,128)S(1)}, u32[]{:S(2)}, u32[]{:S(2)}) collective-permute-start(f32[16,512]{1,0:T(8,128)S(1)} %fusion), channel_id=1, source_target_pairs={{0,24},{1,25},{2,26},{3,27},{4,28},{5,29},{6,30},{7,31},{8,32},{9,... | collective-permute-start | bytes 98312
  538.5 94.4 %collective-permute-start.22 = (f32[16,512]{1,0:T(8,128)S(1)}, f32[16,512]{1,0:T(8,128)S(1)}, u32[]{:S(2)}, u32[]{:S(2)}) collective-permute-start(f32[16,512]{1,0:T(8,128)S(1)} %fusion), channel_id=1, source_target_pairs={{0,23},{1,24},{2,25},{3,26},{4,27},{5,28},{6,29},{7,30},{8,31},{9,... | collective-permute-start | bytes 98312
  551.0 86.3 %collective-permute-start.21 = (f32[16,512]{1,0:T(8,128)S(1)}, f32[16,512]{1,0:T(8,128)S(1)}, u32[]{:S(2)}, u32[]{:S(2)}) collective-permute-start(f32[16,512]{1,0:T(8,128)S(1)} %fusion), channel_id=1, source_target_pairs={{0,22},{1,23},{2,24},{3,25},{4,26},{5,27},{6,28},{7,29},{8,30},{9,... | collective-permute-start | bytes 98312
  554.2 86.2 %collective-permute-start.20 = (f32[16,512]{1,0:T(8,128)S(1)}, f32[16,512]{1,0:T(8,128)S(1)}, u32[]{:S(2)}, u32[]{:S(2)}) collective-permute-start(f32[16,512]{1,0:T(8,128)S(1)} %fusion), channel_id=1, source_target_pairs={{0,21},{1,22},{2,23},{3,24},{4,25},{5,26},{6,27},{7,28},{8,29},{9,... | collective-permute-start | bytes 98312
  561.4 444.7 %copy-start.11 = (bf16[1,256,512]{2,1,0:T(8,128)(2,1)S(1)}, bf16[1,256,512]{2,1,0:T(8,128)(2,1)}, u32[]{:S(2)}) copy-start(bf16[1,256,512]{2,1,0:T(8,128)(2,1)} %param.17) | copy-start | bytes 786436
  625.2 19.9 %collective-permute-start.19 = (f32[16,512]{1,0:T(8,128)S(1)}, f32[16,512]{1,0:T(8,128)S(1)}, u32[]{:S(2)}, u32[]{:S(2)}) collective-permute-start(f32[16,512]{1,0:T(8,128)S(1)} %fusion), channel_id=1, source_target_pairs={{0,20},{1,21},{2,22},{3,23},{4,24},{5,25},{6,26},{7,27},{8,28},{9,... | collective-permute-start | bytes 98312
  627.8 21.2 %collective-permute-start.18 = (f32[16,512]{1,0:T(8,128)S(1)}, f32[16,512]{1,0:T(8,128)S(1)}, u32[]{:S(2)}, u32[]{:S(2)}) collective-permute-start(f32[16,512]{1,0:T(8,128)S(1)} %fusion), channel_id=1, source_target_pairs={{0,19},{1,20},{2,21},{3,22},{4,23},{5,24},{6,25},{7,26},{8,27},{9,... | collective-permute-start | bytes 98312
  632.9 19.7 %collective-permute-start.17 = (f32[16,512]{1,0:T(8,128)S(1)}, f32[16,512]{1,0:T(8,128)S(1)}, u32[]{:S(2)}, u32[]{:S(2)}) collective-permute-start(f32[16,512]{1,0:T(8,128)S(1)} %fusion), channel_id=1, source_target_pairs={{0,18},{1,19},{2,20},{3,21},{4,22},{5,23},{6,24},{7,25},{8,26},{9,... | collective-permute-start | bytes 98312
  637.3 19.0 %collective-permute-start.16 = (f32[16,512]{1,0:T(8,128)S(1)}, f32[16,512]{1,0:T(8,128)S(1)}, u32[]{:S(2)}, u32[]{:S(2)}) collective-permute-start(f32[16,512]{1,0:T(8,128)S(1)} %fusion), channel_id=1, source_target_pairs={{0,17},{1,18},{2,19},{3,20},{4,21},{5,22},{6,23},{7,24},{8,25},{9,... | collective-permute-start | bytes 98312
  640.4 17.8 %collective-permute-start.15 = (f32[16,512]{1,0:T(8,128)S(1)}, f32[16,512]{1,0:T(8,128)S(1)}, u32[]{:S(2)}, u32[]{:S(2)}) collective-permute-start(f32[16,512]{1,0:T(8,128)S(1)} %fusion), channel_id=1, source_target_pairs={{0,16},{1,17},{2,18},{3,19},{4,20},{5,21},{6,22},{7,23},{8,24},{9,... | collective-permute-start | bytes 98312
  645.1 19.2 %collective-permute-start.14 = (f32[16,512]{1,0:T(8,128)S(1)}, f32[16,512]{1,0:T(8,128)S(1)}, u32[]{:S(2)}, u32[]{:S(2)}) collective-permute-start(f32[16,512]{1,0:T(8,128)S(1)} %fusion), channel_id=1, source_target_pairs={{0,15},{1,16},{2,17},{3,18},{4,19},{5,20},{6,21},{7,22},{8,23},{9,... | collective-permute-start | bytes 98312
  649.0 17.2 %collective-permute-start.13 = (f32[16,512]{1,0:T(8,128)S(1)}, f32[16,512]{1,0:T(8,128)S(1)}, u32[]{:S(2)}, u32[]{:S(2)}) collective-permute-start(f32[16,512]{1,0:T(8,128)S(1)} %fusion), channel_id=1, source_target_pairs={{0,14},{1,15},{2,16},{3,17},{4,18},{5,19},{6,20},{7,21},{8,22},{9,... | collective-permute-start | bytes 98312
  652.6 16.5 %collective-permute-start.12 = (f32[16,512]{1,0:T(8,128)S(1)}, f32[16,512]{1,0:T(8,128)S(1)}, u32[]{:S(2)}, u32[]{:S(2)}) collective-permute-start(f32[16,512]{1,0:T(8,128)S(1)} %fusion), channel_id=1, source_target_pairs={{0,13},{1,14},{2,15},{3,16},{4,17},{5,18},{6,19},{7,20},{8,21},{9,... | collective-permute-start | bytes 98312
  656.3 15.2 %collective-permute-start.11 = (f32[16,512]{1,0:T(8,128)S(1)}, f32[16,512]{1,0:T(8,128)S(1)}, u32[]{:S(2)}, u32[]{:S(2)}) collective-permute-start(f32[16,512]{1,0:T(8,128)S(1)} %fusion), channel_id=1, source_target_pairs={{0,12},{1,13},{2,14},{3,15},{4,16},{5,17},{6,18},{7,19},{8,20},{9,... | collective-permute-start | bytes 98312
  658.3 16.8 %collective-permute-start.10 = (f32[16,512]{1,0:T(8,128)S(1)}, f32[16,512]{1,0:T(8,128)S(1)}, u32[]{:S(2)}, u32[]{:S(2)}) collective-permute-start(f32[16,512]{1,0:T(8,128)S(1)} %fusion), channel_id=1, source_target_pairs={{0,11},{1,12},{2,13},{3,14},{4,15},{5,16},{6,17},{7,18},{8,19},{9,... | collective-permute-start | bytes 98312
  664.3 13.3 %collective-permute-start.9 = (f32[16,512]{1,0:T(8,128)S(1)}, f32[16,512]{1,0:T(8,128)S(1)}, u32[]{:S(2)}, u32[]{:S(2)}) collective-permute-start(f32[16,512]{1,0:T(8,128)S(1)} %fusion), channel_id=1, source_target_pairs={{0,10},{1,11},{2,12},{3,13},{4,14},{5,15},{6,16},{7,17},{8,18},{9,... | collective-permute-start | bytes 98312
  666.2 14.8 %collective-permute-start.8 = (f32[16,512]{1,0:T(8,128)S(1)}, f32[16,512]{1,0:T(8,128)S(1)}, u32[]{:S(2)}, u32[]{:S(2)}) collective-permute-start(f32[16,512]{1,0:T(8,128)S(1)} %fusion), channel_id=1, source_target_pairs={{0,9},{1,10},{2,11},{3,12},{4,13},{5,14},{6,15},{7,16},{8,17},{9,1... | collective-permute-start | bytes 98312
  669.1 21.6 %copy-start.17 = (f32[16,512]{1,0:T(8,128)}, f32[16,512]{1,0:T(8,128)S(1)}, u32[]{:S(2)}) copy-start(f32[16,512]{1,0:T(8,128)S(1)} %collective-permute-done.12) | copy-start | bytes 98308
  669.1 13.9 %collective-permute-start.7 = (f32[16,512]{1,0:T(8,128)S(1)}, f32[16,512]{1,0:T(8,128)S(1)}, u32[]{:S(2)}, u32[]{:S(2)}) collective-permute-start(f32[16,512]{1,0:T(8,128)S(1)} %fusion), channel_id=1, source_target_pairs={{0,8},{1,9},{2,10},{3,11},{4,12},{5,13},{6,14},{7,15},{8,16},{9,17... | collective-permute-start | bytes 98312
  671.6 21.8 %copy-start.18 = (f32[16,512]{1,0:T(8,128)}, f32[16,512]{1,0:T(8,128)S(1)}, u32[]{:S(2)}) copy-start(f32[16,512]{1,0:T(8,128)S(1)} %collective-permute-done.11) | copy-start | bytes 98308
  671.6 16.5 %collective-permute-start.6 = (f32[16,512]{1,0:T(8,128)S(1)}, f32[16,512]{1,0:T(8,128)S(1)}, u32[]{:S(2)}, u32[]{:S(2)}) collective-permute-start(f32[16,512]{1,0:T(8,128)S(1)} %fusion), channel_id=1, source_target_pairs={{0,7},{1,8},{2,9},{3,10},{4,11},{5,12},{6,13},{7,14},{8,15},{9,16}... | collective-permute-start | bytes 98312
  675.0 18.3 %copy-start.19 = (f32[16,512]{1,0:T(8,128)}, f32[16,512]{1,0:T(8,128)S(1)}, u32[]{:S(2)}) copy-start(f32[16,512]{1,0:T(8,128)S(1)} %collective-permute-done.10) | copy-start | bytes 98308
  675.0 15.6 %collective-permute-start.5 = (f32[16,512]{1,0:T(8,128)S(1)}, f32[16,512]{1,0:T(8,128)S(1)}, u32[]{:S(2)}, u32[]{:S(2)}) collective-permute-start(f32[16,512]{1,0:T(8,128)S(1)} %fusion), channel_id=1, source_target_pairs={{0,6},{1,7},{2,8},{3,9},{4,10},{5,11},{6,12},{7,13},{8,14},{9,15},... | collective-permute-start | bytes 98312
  677.7 15.7 %copy-start.20 = (f32[16,512]{1,0:T(8,128)}, f32[16,512]{1,0:T(8,128)S(1)}, u32[]{:S(2)}) copy-start(f32[16,512]{1,0:T(8,128)S(1)} %collective-permute-done.9) | copy-start | bytes 98308
  677.7 20.3 %collective-permute-start.4 = (f32[16,512]{1,0:T(8,128)S(1)}, f32[16,512]{1,0:T(8,128)}, u32[]{:S(2)}, u32[]{:S(2)}) collective-permute-start(f32[16,512]{1,0:T(8,128)S(1)} %fusion), channel_id=1, source_target_pairs={{0,5},{1,6},{2,7},{3,8},{4,9},{5,10},{6,11},{7,12},{8,13},{9,14},{... | collective-permute-start | bytes 98312
  681.0 12.4 %copy-start.21 = (f32[16,512]{1,0:T(8,128)}, f32[16,512]{1,0:T(8,128)S(1)}, u32[]{:S(2)}) copy-start(f32[16,512]{1,0:T(8,128)S(1)} %collective-permute-done.8) | copy-start | bytes 98308
  681.0 17.0 %collective-permute-start.3 = (f32[16,512]{1,0:T(8,128)S(1)}, f32[16,512]{1,0:T(8,128)}, u32[]{:S(2)}, u32[]{:S(2)}) collective-permute-start(f32[16,512]{1,0:T(8,128)S(1)} %fusion), channel_id=1, source_target_pairs={{0,4},{1,5},{2,6},{3,7},{4,8},{5,9},{6,10},{7,11},{8,12},{9,13},{1... | collective-permute-start | bytes 98312
  683.0 10.4 %copy-start.22 = (f32[16,512]{1,0:T(8,128)}, f32[16,512]{1,0:T(8,128)S(1)}, u32[]{:S(2)}) copy-start(f32[16,512]{1,0:T(8,128)S(1)} %collective-permute-done.7) | copy-start | bytes 98308
  683.0 14.9 %collective-permute-start.2 = (f32[16,512]{1,0:T(8,128)S(1)}, f32[16,512]{1,0:T(8,128)}, u32[]{:S(2)}, u32[]{:S(2)}) collective-permute-start(f32[16,512]{1,0:T(8,128)S(1)} %fusion), channel_id=1, source_target_pairs={{0,3},{1,4},{2,5},{3,6},{4,7},{5,8},{6,9},{7,10},{8,11},{9,12},{10... | collective-permute-start | bytes 98312
  688.1 5.3 copy-start.23
  688.1 9.9 collective-permute-start.1
  690.6 2.8 copy-start.24
  690.7 7.3 collective-permute-start
  (6 other events, 6.5 us)
Sparse Core Ops, SparseCore 0:
  10.3 55.4 all-gather.2
  121.8 150.5 all-reduce.11
  274.8 640.2 reduce-scatter.6
  919.1 86.9 reduce-scatter.4
where the time goes:
time: 1040 us; the launch traced here: 1030 us
  blocking collectives  406 us (39%)
  waiting for transfers between devices  277 us (27%)
  local copies, waits for them, and re-layouts  120 us (12%)
  starting transfers between devices  103 us (10%)
  other arithmetic  68.1 us (7%)
  matrix products  38.6 us (4%)
  between operations  14.9 us (1%)
    unnamed x2, blocking collectives  406 us
    reduce_scatter x1, waiting for transfers between devices, shards(): lax.psum_scatter(node_grads[1], ('nodes', 'batch'), scatter_dimension=0,...  167 us
    unnamed x33, starting transfers between devices  94.9 us
    reduce_scatter x1, waiting for transfers between devices, shards(): lax.psum_scatter(node_terms.astype(jnp.bfloat16), 'nodes', scatter_dimens...  89.7 us
    unnamed x72, local copies, waits for them, and re-layouts  63.2 us
  transfers between devices with their start and end apart: 37, of which 3 were waited for; matrix products, arithmetic and copies ran while one was open for 48% of the time, Pallas kernels for 0%

commit v1 on v0

v1 whole, which is shorter than its diff:
```python
import functools
import math

import jax
import jax.numpy as jnp
from jax import lax
from jax.experimental import pallas as pl
from jax.experimental.pallas import tpu as pltpu
from jax.sharding import PartitionSpec as P

EPS = 1e-05
ALL = ("nodes", "batch")
F32 = jnp.float32
BF16 = jnp.bfloat16
TILE = 512
LANES = 128
EDGE_IN, EDGE_OUT, NODE_IN, NODE_OUT = 48, 16, 32, 16
HALO = 16
EDGE_ROWS = HALO + EDGE_IN + EDGE_OUT
NODE_ROWS = NODE_IN + NODE_OUT
SENT_ROWS = 2 * HALO + EDGE_IN + EDGE_OUT + NODE_ROWS
SMALL = 16
VMEM_LIMIT = 48 * 1024 * 1024


def nn(lhs, rhs):
    return lax.dot_general(lhs, rhs, (((1,), (0,)), ((), ())), preferred_element_type=F32)


def nt(lhs, rhs):
    return lax.dot_general(lhs, rhs, (((1,), (1,)), ((), ())), preferred_element_type=F32)


def tn(lhs, rhs):
    return lax.dot_general(lhs, rhs, (((0,), (0,)), ((), ())), preferred_element_type=F32)


def pick_rows(index_column, count, first=0):
    shape = (index_column.shape[0], count)
    columns = lax.broadcasted_iota(jnp.int32, shape, 1) + first
    return jnp.where(index_column == columns, 1.0, 0.0).astype(BF16)


def pick_columns(index_row, count, first=0):
    shape = (count, index_row.shape[1])
    rows = lax.broadcasted_iota(jnp.int32, shape, 0) + first
    return jnp.where(index_row == rows, 1.0, 0.0).astype(BF16)


def activate(pre):
    sig = jax.nn.sigmoid(pre)
    return pre * sig, sig * (1.0 + pre * (1.0 - sig))


def layer_norm(pre_norm):
    centred = pre_norm - jnp.mean(pre_norm, axis=-1, keepdims=True)
    inv = lax.rsqrt(jnp.mean(centred * centred, axis=-1, keepdims=True) + EPS)
    return centred * inv, inv


def norm_backward(scaled, normed, inv):
    mean_scaled = jnp.mean(scaled, axis=-1, keepdims=True)
    mean_product = jnp.mean(scaled * normed, axis=-1, keepdims=True)
    return (scaled - mean_scaled - normed * mean_product) * inv


def put(dst, chip, stride, row, block):
    count = block.shape[0]
    for group in range(4):
        dst[chip, pl.ds(group * stride + row, count), :] = block[
            :, group * LANES : (group + 1) * LANES
        ].astype(BF16)


def gather_kernel(rows_ref, hidden_ref, out_ref):
    out_ref[...] = nn(pick_rows(rows_ref[...], hidden_ref.shape[0]), hidden_ref[...]).astype(BF16)


def local_kernel(
    edge_ref, index_ref, hidden_ref, weight_ref, bias_ref, nweight_ref, nbias_ref,
    part_ref, npart_ref, table
):
    width = hidden_ref.shape[1]
    nodes = hidden_ref.shape[0]

    @pl.when(pl.program_id(0) == 0)
    def _():
        hidden = hidden_ref[...]
        table[:nodes] = nn(hidden, weight_ref[width : 2 * width]).astype(BF16)
        table[nodes:] = nn(hidden, weight_ref[2 * width :]).astype(BF16)
        npart_ref[...] = nn(hidden, nweight_ref[...]) + nbias_ref[...]

    index = index_ref[...]
    picks = jnp.concatenate(
        [pick_rows(index[:, 0:1], nodes), pick_rows(index[:, 1:2], nodes)], axis=1
    )
    part_ref[...] = (
        nn(edge_ref[...], weight_ref[:width]) + nn(picks, table[...]) + bias_ref[...]
    )


def forward_kernel(
    core_ref, part_ref, index_ref, rows_ref, halo_ref, weight_ref, weight_out_ref, gain_ref,
    hidden_ref, npart_ref, nweight_ref, nweight_out_ref, ngain_ref, ncot_ref,
    act_ref, slope_ref, norm_ref, inv_ref, base_ref, agg_grad_ref, nsend_ref, nkeep_ref,
    nsmall_ref, table, aggregate, grad_in, grad_out
):
    step = pl.program_id(0)
    nodes, width = hidden_ref.shape
    slots = halo_ref.shape[0]

    @pl.when(step == 0)
    def _():
        table[...] = nn(halo_ref[...], weight_ref[...]).astype(BF16)
        aggregate[...] = jnp.zeros_like(aggregate)

    pre = part_ref[...] + nn(pick_rows(index_ref[:, 0:1], slots, nodes), table[...])
    act, slope = activate(pre)
    act = act.astype(BF16)
    act_ref[...] = act
    slope_ref[...] = slope.astype(BF16)
    normed, inv = layer_norm(nn(act, weight_out_ref[...]))
    norm_ref[...] = normed.astype(BF16)
    inv_ref[...] = inv
    message = (normed * gain_ref[...]).astype(BF16)
    aggregate[...] += nn(pick_columns(rows_ref[1:2, :], nodes), message)

    @pl.when(step == pl.num_programs(0) - 1)
    def _():
        hidden = hidden_ref[...]
        received = aggregate[...].astype(BF16)
        node_act, node_slope = activate(npart_ref[...] + nn(received, nweight_ref[width:]))
        node_act = node_act.astype(BF16)
        node_norm, node_inv = layer_norm(nn(node_act, nweight_out_ref[...]))
        cot = ncot_ref[...].astype(F32)
        nsmall_ref[1:2] = jnp.sum(cot * node_norm, axis=0, keepdims=True)
        grad_norm = norm_backward(cot * ngain_ref[...], node_norm, node_inv).astype(BF16)
        grad_pre = (nt(grad_norm, nweight_out_ref[...]) * node_slope).astype(BF16)
        nsmall_ref[0:1] = jnp.sum(grad_pre.astype(F32), axis=0, keepdims=True)
        agg_grad_ref[...] = nt(grad_pre, nweight_ref[width:]).astype(BF16)
        base_ref[...] = cot + nt(grad_pre, nweight_ref[:width])
        grad_out[...] = tn(node_act, grad_norm)
        grad_in[:width] = tn(hidden, grad_pre)
        grad_in[width:] = tn(received, grad_pre)
        core = core_ref[0]
        for dst, side in ((nkeep_ref, core), (nsend_ref, 1 - core)):

            def pack(chip, carry):
                piece = chip * 2 + side
                start = pl.multiple_of(piece * NODE_IN, NODE_IN)
                put(dst, chip, NODE_ROWS, 0, grad_in[pl.ds(start, NODE_IN)])
                start = pl.multiple_of(piece * NODE_OUT, NODE_OUT)
                put(dst, chip, NODE_ROWS, NODE_IN, grad_out[pl.ds(start, NODE_OUT)])
                return carry

            lax.fori_loop(0, dst.shape[0], pack, 0)


def backward_kernel(
    core_ref, ecot_ref, index_ref, rows_ref, act_ref, slope_ref, norm_ref, inv_ref, edge_ref,
    agg_grad_ref, gain_ref, weight_out_ref, weight_ref, hidden_ref, halo_ref, base_ref, nsmall_ref,
    pre_grad_ref, esend_ref, ekeep_ref, total_ref,
    grad_in, grad_out, sums, terms, bias_sum, gain_sum
):
    step = pl.program_id(0)
    nodes, width = hidden_ref.shape
    slots = halo_ref.shape[0]

    @pl.when(step == 0)
    def _():
        grad_in[...] = jnp.zeros_like(grad_in)
        grad_out[...] = jnp.zeros_like(grad_out)
        sums[...] = jnp.zeros_like(sums)
        bias_sum[...] = jnp.zeros_like(bias_sum)
        gain_sum[...] = jnp.zeros_like(gain_sum)

    message_grad = ecot_ref[...].astype(F32) + nn(
        pick_rows(index_ref[:, 1:2], nodes), agg_grad_ref[...]
    )
    normed = norm_ref[...].astype(F32)
    gain_sum[...] += jnp.sum(message_grad * normed, axis=0, keepdims=True)
    grad_norm = norm_backward(message_grad * gain_ref[...], normed, inv_ref[...]).astype(BF16)
    grad_pre = nt(grad_norm, weight_out_ref[...]) * slope_ref[...].astype(F32)
    grad_pre = grad_pre.astype(BF16)
    pre_grad_ref[...] = grad_pre
    bias_sum[...] += jnp.sum(grad_pre.astype(F32), axis=0, keepdims=True)
    grad_out[...] += tn(act_ref[...], grad_norm)
    grad_in[:width] += tn(edge_ref[...], grad_pre)
    sums[: nodes + slots] += nn(pick_columns(rows_ref[0:1, :], nodes + slots), grad_pre)
    sums[nodes + slots :] += nn(pick_columns(rows_ref[1:2, :], nodes), grad_pre)

    @pl.when(step == pl.num_programs(0) - 1)
    def _():
        own = sums[:nodes].astype(BF16)
        remote = sums[nodes : nodes + slots].astype(BF16)
        received = sums[nodes + slots :].astype(BF16)
        hidden = hidden_ref[...]
        grad_in[width : 2 * width] = tn(hidden, own) + tn(halo_ref[...], remote)
        grad_in[2 * width :] = tn(hidden, received)
        terms[...] = nt(remote, weight_ref[width : 2 * width])
        total_ref[...] = (
            base_ref[...]
            + nt(own, weight_ref[width : 2 * width])
            + nt(received, weight_ref[2 * width :])
        )
        small = [bias_sum[...], gain_sum[...], nsmall_ref[0:1], nsmall_ref[1:2]]
        small = jnp.concatenate(
            [item[:, g * LANES : (g + 1) * LANES] for item in small for g in range(4)], axis=0
        ).astype(BF16)
        core = core_ref[0]
        for dst, side in ((ekeep_ref, core), (esend_ref, 1 - core)):

            def pack(chip, carry):
                piece = chip * 2 + side
                start = pl.multiple_of(piece * HALO, HALO)
                put(dst, chip, EDGE_ROWS, 0, terms[pl.ds(start, HALO)])
                start = pl.multiple_of(piece * EDGE_IN, EDGE_IN)
                put(dst, chip, EDGE_ROWS, HALO, grad_in[pl.ds(start, EDGE_IN)])
                start = pl.multiple_of(piece * EDGE_OUT, EDGE_OUT)
                put(dst, chip, EDGE_ROWS, HALO + EDGE_IN, grad_out[pl.ds(start, EDGE_OUT)])
                dst[chip, 4 * EDGE_ROWS :, :] = small
                return carry

            lax.fori_loop(0, dst.shape[0], pack, 0)


def pair_kernel(core_ref, ekeep_ref, erecv_ref, nkeep_ref, nrecv_ref, out_ref):
    core = core_ref[0]

    def add(lhs, rhs, start, count):
        rows = slice(start, start + count)
        return (lhs[:, rows, :].astype(F32) + rhs[:, rows, :].astype(F32)).astype(BF16)

    for group in range(4):
        out, edge, node = group * SENT_ROWS, group * EDGE_ROWS, group * NODE_ROWS
        start = pl.multiple_of(out + core * HALO, HALO)
        out_ref[:, pl.ds(start, HALO), :] = ekeep_ref[:, edge : edge + HALO, :]
        start = pl.multiple_of(out + (1 - core) * HALO, HALO)
        out_ref[:, pl.ds(start, HALO), :] = erecv_ref[:, edge : edge + HALO, :]
        out += 2 * HALO
        count = EDGE_IN + EDGE_OUT
        out_ref[:, out : out + count, :] = add(ekeep_ref, erecv_ref, edge + HALO, count)
        out += count
        out_ref[:, out : out + NODE_ROWS, :] = add(nkeep_ref, nrecv_ref, node, NODE_ROWS)
    out_ref[:, 4 * SENT_ROWS :, :] = add(ekeep_ref, erecv_ref, 4 * EDGE_ROWS, SMALL)


def edge_out_kernel(ecot_ref, pre_grad_ref, weight_ref, out_ref):
    out_ref[...] = (
        ecot_ref[...].astype(F32) + nt(pre_grad_ref[...], weight_ref[...])
    ).astype(BF16)


def arrive_kernel(
    batch_ref, arrived_ref, rows_ref, total_ref, nodes_ref, mine_ref, one_ref, two_ref, three_ref, sums
):
    nodes = total_ref.shape[0]
    picks = pick_columns(rows_ref[...], nodes)
    for group in range(4):
        out = group * SENT_ROWS
        halo = arrived_ref[:, out : out + 2 * HALO, :].reshape(-1, LANES)
        lanes = slice(group * LANES, (group + 1) * LANES)
        nodes_ref[:, lanes] = (total_ref[:, lanes] + nn(picks, halo)).astype(BF16)
        weights = jnp.sum(
            arrived_ref[:, out + 2 * HALO : out + SENT_ROWS, :].astype(F32), axis=0
        )
        for state in range(4):
            row, first = group * 28, 0
            for count in (EDGE_IN, EDGE_OUT, NODE_IN, NODE_OUT):
                share = count // 4
                begin = first + state * share
                sums[state, row : row + share, :] = weights[begin : begin + share, :]
                row += share
                first += count
    small = jnp.sum(arrived_ref[:, 4 * SENT_ROWS :, :].astype(F32), axis=0)
    for state in range(4):
        sums[state, 112:, :] = small
    batch = batch_ref[0]
    mine_ref[...] = sums[batch]
    for away, ref in ((1, one_ref), (2, two_ref), (3, three_ref)):
        ref[...] = sums[lax.rem(batch + away, 4)].astype(BF16)


def finish_kernel(
    factor, mine_ref, one_ref, two_ref, three_ref,
    edge_in_ref, edge_out_ref, node_in_ref, node_out_ref, small_ref
):
    total = (
        mine_ref[...]
        + one_ref[...].astype(F32)
        + two_ref[...].astype(F32)
        + three_ref[...].astype(F32)
    ) * factor
    for group in range(4):
        lanes = slice(group * LANES, (group + 1) * LANES)
        row = group * 28
        for ref in (edge_in_ref, edge_out_ref, node_in_ref, node_out_ref):
            count = ref.shape[0]
            ref[:, lanes] = total[row : row + count, :]
            row += count
    small_ref[...] = total[112:, :]


def call(body, outs, grid=None, in_specs=None, out_specs=None, scratch=(), cost=None):
    args = {}
    if grid is not None:
        args = dict(grid=grid, in_specs=in_specs, out_specs=out_specs)
    elif in_specs is not None:
        args = dict(in_specs=in_specs)
    return pl.pallas_call(
        body,
        out_shape=outs,
        scratch_shapes=scratch,
        compiler_params=pltpu.CompilerParams(vmem_limit_bytes=VMEM_LIMIT),
        cost_estimate=cost,
        **args,
    )


def flops(count, moved):
    return pl.CostEstimate(flops=int(count), bytes_accessed=int(moved), transcendentals=0)


def shape(*dims, dtype=BF16):
    return jax.ShapeDtypeStruct(dims, dtype)


def full(*dims):
    return pl.BlockSpec(dims, lambda i: (0,) * len(dims))


def tiled(*dims):
    return pl.BlockSpec(dims, lambda i: (i,) + (0,) * (len(dims) - 1))


SCALAR = pl.BlockSpec(memory_space=pltpu.SMEM)
WHOLE = pl.BlockSpec(memory_space=pltpu.VMEM)


def shards(
    node_latents, edge_latents, node_cotangent, edge_cotangent, senders, receivers, send_rows,
    edge_weight_in, edge_bias, edge_weight_out, edge_gain,
    node_weight_in, node_bias, node_weight_out, node_gain,
):
    nodes, width = node_latents.shape[1:]
    edges = edge_latents.shape[1]
    parts = lax.axis_size("nodes")
    batch_size = lax.axis_size("batch")
    slots = send_rows.shape[1] * send_rows.shape[2]
    chips = parts // 2
    hidden = node_latents[0]
    edge_rows = edge_latents[0]
    ncot = node_cotangent[0]
    ecot = edge_cotangent[0]
    node_index = lax.axis_index("nodes")
    core = jnp.reshape(node_index % 2, (1,)).astype(jnp.int32)
    batch = jnp.reshape(lax.axis_index("batch"), (1,)).astype(jnp.int32)
    tile = min(TILE, edges)
    grid = (edges // tile,)

    row = lambda vector: vector.reshape(1, width)
    index = jnp.stack([senders, receivers], axis=1)
    index_rows = jnp.stack([senders, receivers], axis=0)

    with jax.named_scope("halo_rows"):
        outgoing = call(gather_kernel, shape(slots, width))(send_rows.reshape(slots, 1), hidden)
        halo = lax.all_to_all(
            outgoing.reshape(parts, -1, width), "nodes", 0, 0, tiled=True
        ).reshape(slots, width)
    index_tile = tiled(tile, 2)
    rows_tile = pl.BlockSpec((2, tile), lambda i: (0, i))
    edge_tile = tiled(tile, width)
    with jax.named_scope("edge_pre_local"):
        part, npart = call(
            local_kernel,
            (shape(edges, width, dtype=F32), shape(nodes, width, dtype=F32)),
            grid,
            [
                edge_tile, index_tile, full(nodes, width), full(3 * width, width), full(1, width),
                full(width, width), full(1, width),
            ],
            (edge_tile, full(nodes, width)),
            [pltpu.VMEM((2 * nodes, width), BF16)],
            flops(2 * edges * width * 2 * width, 6 * edges * width),
        )(edge_rows, index, hidden, edge_weight_in, row(edge_bias), node_weight_in, row(node_bias))
    with jax.named_scope("forward"):
        node_pack = shape(chips, 4 * NODE_ROWS, LANES)
        act, slope, norm, inv, base, agg_grad, nsend, nkeep, nsmall = call(
            forward_kernel,
            (
                shape(edges, width), shape(edges, width), shape(edges, width),
                shape(edges, 1, dtype=F32), shape(nodes, width, dtype=F32), shape(nodes, width),
                node_pack, node_pack, shape(2, width, dtype=F32),
            ),
            grid,
            [
                SCALAR, edge_tile, index_tile, rows_tile, full(slots, width),
                pl.BlockSpec((width, width), lambda i: (1, 0)), full(width, width), full(1, width),
                full(nodes, width), full(nodes, width), full(2 * width, width), full(width, width),
                full(1, width), full(nodes, width),
            ],
            (
                edge_tile, edge_tile, edge_tile, tiled(tile, 1), full(nodes, width),
                full(nodes, width), full(*node_pack.shape), full(*node_pack.shape), full(2, width),
            ),
            [
                pltpu.VMEM((slots, width), BF16), pltpu.VMEM((nodes, width), F32),
                pltpu.VMEM((2 * width, width), F32), pltpu.VMEM((width, width), F32),
            ],
            flops(2 * edges * width * 3 * width, 12 * edges * width),
        )(
            core, part, index, index_rows, halo, edge_weight_in, edge_weight_out, row(edge_gain),
            hidden, npart, node_weight_in, node_weight_out, row(node_gain), ncot,
        )
    partner = [(i, i ^ batch_size) for i in range(parts * batch_size)]
    with jax.named_scope("node_weight_pair"):
        nrecv = lax.ppermute(nsend, ALL, partner)
    with jax.named_scope("backward"):
        edge_pack = shape(chips, 4 * EDGE_ROWS + SMALL, LANES)
        pre_grad, esend, ekeep, total = call(
            backward_kernel,
            (shape(edges, width), edge_pack, edge_pack, shape(nodes, width, dtype=F32)),
            grid,
            [
                SCALAR, edge_tile, index_tile, rows_tile, edge_tile, edge_tile, edge_tile,
                tiled(tile, 1), edge_tile, full(nodes, width), full(1, width), full(width, width),
                full(3 * width, width), full(nodes, width), full(slots, width), full(nodes, width),
                full(2, width),
            ],
            (edge_tile, full(*edge_pack.shape), full(*edge_pack.shape), full(nodes, width)),
            [
                pltpu.VMEM((3 * width, width), F32), pltpu.VMEM((width, width), F32),
                pltpu.VMEM((2 * nodes + slots, width), F32), pltpu.VMEM((slots, width), F32),
                pltpu.VMEM((1, width), F32), pltpu.VMEM((1, width), F32),
            ],
            flops(2 * edges * width * 6 * width, 14 * edges * width),
        )(
            core, ecot, index, index_rows, act, slope, norm, inv, edge_rows, agg_grad,
            row(edge_gain), edge_weight_out, edge_weight_in, hidden, halo, base, nsmall,
        )
    with jax.named_scope("edge_weight_pair"):
        erecv = lax.ppermute(esend, ALL, partner)
    with jax.named_scope("pair_sum"):
        sent = call(
            pair_kernel,
            shape(chips, 4 * SENT_ROWS + SMALL, LANES),
            (4,),
            [
                SCALAR, tiled(chips // 4, *edge_pack.shape[1:]), tiled(chips // 4, *edge_pack.shape[1:]),
                tiled(chips // 4, *node_pack.shape[1:]), tiled(chips // 4, *node_pack.shape[1:]),
            ],
            tiled(chips // 4, 4 * SENT_ROWS + SMALL, LANES),
            cost=flops(0, 3 * chips * 4 * SENT_ROWS * LANES),
        )(core, ekeep, erecv, nkeep, nrecv)
    with jax.named_scope("chip_exchange"):
        groups = [[2 * chip + side for chip in range(chips)] for side in range(2)]
        arrived = lax.all_to_all(sent, "nodes", 0, 0, tiled=True, axis_index_groups=groups)
    with jax.named_scope("grad_edges"):
        grad_edges = call(
            edge_out_kernel,
            shape(edges, width),
            grid,
            [edge_tile, edge_tile, full(width, width)],
            edge_tile,
            cost=flops(2 * edges * width * width, 6 * edges * width),
        )(ecot, pre_grad, edge_weight_in)
    with jax.named_scope("arrive"):
        block = (112 + SMALL, LANES)
        grad_nodes, mine, one, two, three = call(
            arrive_kernel,
            (shape(nodes, width), shape(*block, dtype=F32), shape(*block), shape(*block), shape(*block)),
            in_specs=[SCALAR, WHOLE, WHOLE, WHOLE],
            scratch=[pltpu.VMEM((4, *block), F32)],
        )(batch, arrived, send_rows.reshape(1, slots), total)
    with jax.named_scope("state_exchange"):
        places = [
            [(n * batch_size + b, n * batch_size + (b + away) % batch_size)
             for n in range(parts) for b in range(batch_size)]
            for away in (1, 2, 3)
        ]
        got = [lax.ppermute(item, ALL, perm) for item, perm in zip((one, two, three), places)]
    with jax.named_scope("weight_grads"):
        factor = 1.0 / math.sqrt(batch_size * edges * parts)
        edge_in, edge_out, node_in, node_out, small = call(
            functools.partial(finish_kernel, factor),
            (
                shape(12, width, dtype=F32), shape(4, width, dtype=F32), shape(8, width, dtype=F32),
                shape(4, width, dtype=F32), shape(SMALL, LANES, dtype=F32),
            ),
        )(mine, *got)
        place = node_index * batch_size + lax.axis_index("batch")
        small = lax.dynamic_slice(
            small.reshape(4, width), (0, place * 4), (4, 4)
        )
    return (
        grad_nodes[None], grad_edges[None], edge_in, small[0], edge_out, small[1],
        node_in, small[2], node_out, small[3],
    )


def solution(mesh):
    rows = P("batch", "nodes", None)
    split = P(ALL, None)
    return jax.shard_map(
        shards,
        mesh=mesh,
        in_specs=(rows,) * 4 + (P("nodes"), P("nodes"), P("nodes", None, None)) + (P(),) * 8,
        out_specs=(rows, rows) + (split, P(ALL)) * 4,
        check_vma=False,
    )
```

time: 1040 us -> 122 us (0.12); the launches traced: 1030 us -> 121 us
  blocking collectives: 406 us -> 0 us
  waiting for transfers between devices: 277 us -> 44 us
  local copies, waits for them, and re-layouts: 120 us -> 14.7 us
  starting transfers between devices: 103 us -> 19.3 us
  other arithmetic: 68.1 us -> 0.03 us
  Pallas kernels: 0 us -> 41.9 us
  matrix products: 38.6 us -> 0 us
  between operations: 14.9 us -> 0.83 us
    unnamed x2 -> x0, blocking collectives: 406 us -> none
    reduce_scatter x2 -> x0, waiting for transfers between devices: 257 us -> none  [the longest x1 167 us: shards(): lax.psum_scatter(node_grads[1], ('nodes', 'batch'), scatter_dimension=0,...]
    unnamed x33 -> x0, starting transfers between devices: 94.9 us -> none
    gather x5 -> x0, local copies, waits for them, and re-layouts: 51.7 us -> none  [the longest x2 14.7 us: shards(): message_grad = edge_cot + node_grad_input[:, feature_count:][receivers]]
    unnamed x72 -> x49, local copies, waits for them, and re-layouts: 63.2 us -> 13.5 us
    pallas_call x0 -> x8, Pallas kernels: none -> 41.9 us  [the longest x1 15.2 us: shards(): call(backward_kernel, (shape(edges, width), edge_pack, edge_pack, shape(n...]
    all_to_all x1 -> x2, waiting for transfers between devices: 0.01 us -> 40.3 us  [the longest x1 37.8 us: shards(): lax.all_to_all(sent, 'nodes', 0, 0, tiled=True, axis_index_groups=groups)]
    dot_general x13 -> x0, matrix products: 38.6 us -> none  [the longest x2 10.4 us: mlp_backward(): lax.dot_general(layer_input, grad_pre, dims_rows, preferred_element_type=...]
  transfers between devices with their start and end apart: 37 -> 7, of which waited for: 3 -> 3; matrix products, arithmetic and copies ran while one was open for 48% -> 0% of each run, Pallas kernels for 0% -> 8%
where the time goes in v1:
time: 122 us; the launch traced here: 121 us
  waiting for transfers between devices  44 us (36%)
  Pallas kernels  41.9 us (34%)
  starting transfers between devices  19.3 us (16%)
  local copies, waits for them, and re-layouts  14.7 us (12%)
    all_to_all x1, waiting for transfers between devices, shards(): lax.all_to_all(sent, 'nodes', 0, 0, tiled=True, axis_index_groups=groups)  37.8 us
    pallas_call x1, Pallas kernels, shards(): call(backward_kernel, (shape(edges, width), edge_pack, edge_pack, shape(n...  15.2 us
    unnamed x49, local copies, waits for them, and re-layouts  13.5 us
    pallas_call x1, Pallas kernels, shards(): call(forward_kernel, (shape(edges, width), shape(edges, width), shape(edg...  12.2 us
    all_to_all x1, starting transfers between devices, shards(): lax.all_to_all(outgoing.reshape(parts, -1, width), 'nodes', 0, 0, tiled=T...  8.25 us
    pallas_call x1, Pallas kernels, shards(): call(local_kernel, (shape(edges, width, dtype=F32), shape(nodes, width, d...  6.39 us
    ppermute x3, starting transfers between devices, shards(): lax.ppermute(item, ALL, perm)  5.76 us
    all_to_all x1, starting transfers between devices, shards(): lax.all_to_all(sent, 'nodes', 0, 0, tiled=True, axis_index_groups=groups)  4.74 us
  transfers between devices with their start and end apart: 7, of which 3 were waited for; matrix products, arithmetic and copies ran while one was open for 0% of the time, Pallas kernels for 8%

profile of v1, /device:TPU:0, one launch (start us, length us, event | category | flops | bytes accessed | tf_op | source)
XLA Modules:
  0.0 120.8 jit_solution(2517538723469929931)
XLA Ops:
  0.6 0.0 copy-start.2
  0.7 0.9 copy.33
  1.5 0.2 reshape.65.rows_ref
  1.7 0.0 copy-start.9
  1.7 0.9 copy-done.9
  2.7 0.0 copy-start.22
  2.7 0.0 copy-start.23
  2.7 0.0 copy-start.10
  2.7 0.0 copy-start.16
  2.7 0.0 copy-start.17
  2.7 1.1 halo_rows.1
  3.8 8.2 %all-to-all-start = ((bf16[32,16,512]{2,1,0:T(8,128)(2,1)}), bf16[32,16,512]{2,1,0:T(8,128)(2,1)S(1)}, u32[]{:S(2)}, u32[]{:S(2)}) async-start(bf16[32,16,512]{2,1,0:T(8,128)(2,1)} %bitcast.11), calls=%async_computation | async-start | bytes 1048576 | tf_op jit(solution)/shard_map/halo_rows/all_to_all | solution.py:367
  12.1 0.0 copy-done.22
  12.1 0.0 copy-done.23
  12.1 0.4 copy.36.index_ref
  12.5 0.0 copy-start.5
  12.5 0.0 copy-done.2
  12.5 0.0 copy-done.10
  12.5 0.0 copy-done.16
  12.6 0.0 copy-done.17
  12.6 0.0 copy-start.11
  12.6 1.6 %copy-done.11 = bf16[1024,512]{1,0:T(8,128)(2,1)S(1)} copy-done((bf16[1024,512]{1,0:T(8,128)(2,1)S(1)}, bf16[1024,512]{1,0:T(8,128)(2,1)}, u32[]{:S(2)}) %copy-start.11) | copy-done | bytes 1048600
  14.1 0.0 copy-start.18
  14.1 0.0 copy-start.19
  14.1 6.4 %edge_pre_local.1 = (f32[2048,512]{1,0:T(8,128)}, f32[256,512]{1,0:T(8,128)S(1)}) custom-call(bf16[2048,512]{1,0:T(8,128)(2,1)} %bitcast.45, s32[2048,2]{1,0:T(8,128)S(1)} %copy.36.index_ref, bf16[256,512]{1,0:T(8,128)(2,1)S(1)} %bitcast.31, bf16[1536,512]{1,0:T(8,128)(2,1)S(1)} %copy-done.2, f32[1,512]{1,0:T(1,128)S(1)} %bitcast.35, ...), custom_call_target="tpu_custom_call" | custom-call | flops 2147483648 | bytes 6291456 | tf_op jit(solution)/shard_map/edge_pre_local/pallas_call | solution.py:374
  20.5 0.0 copy-done.5
  20.5 0.0 copy-start.20
  20.5 0.8 copy-done.20
  21.4 2.5 %all-to-all-done = bf16[32,16,512]{2,1,0:T(8,128)(2,1)S(1)} async-done(((bf16[32,16,512]{2,1,0:T(8,128)(2,1)}), bf16[32,16,512]{2,1,0:T(8,128)(2,1)S(1)}, u32[]{:S(2)}, u32[]{:S(2)}) %all-to-all-start) | async-done | bytes 524320 | tf_op jit(solution)/shard_map/halo_rows/all_to_all | solution.py:367
  23.8 0.0 copy-done.18
  23.8 0.0 copy-done.19
  23.8 1.0 copy-done.12
  24.9 1.0 copy-done.13
  25.9 0.9 copy-done.15
  26.9 1.0 copy-done.21
  27.9 12.2 %forward.1 = (bf16[2048,512]{1,0:T(8,128)(2,1)}, bf16[2048,512]{1,0:T(8,128)(2,1)}, bf16[2048,512]{1,0:T(8,128)(2,1)}, f32[2048,1]{1,0:T(8,128)S(1)}, f32[256,51...) custom-call(s32[1]{0:T(128)} %bitcast.1.core_ref, ...), custom_call_target="tpu_custom_call" | custom-call | flops 3221225472 | bytes 12582912 | tf_op jit(solution)/shard_map/forward/pallas_call | solution.py:388
  40.1 0.0 copy-done.6
  40.1 0.0 copy-done.14
  40.1 15.2 %backward.1 = (bf16[2048,512]{1,0:T(8,128)(2,1)}, bf16[16,336,128]{2,1,0:T(8,128)(2,1)S(1)}, bf16[16,336,128]{2,1,0:T(8,128)(2,1)}, f32[256,512]{1,0:T(8,128)S(1)}) custom-call(s32[1]{0:T(128)} %bitcast.1.core_ref, bf16[2048,512]{1,0:T(8,128)(2,1)} %bitcast.26, s32[2048,2]{1,0:T(8,128)S(1)} %copy-done.6, s32[2,2048]{1,0:T(2,128)S(1)} %pad_add_fusion.1.rows_ref, ...), custom_call_target="tpu_custom_call" | custom-call | flops 6442450944 | bytes 14680064 | tf_op jit(solution)/shard_map/backward/pallas_call | solution.py:420
  55.3 0.8 copy-done.7
  56.1 0.1 collective-permute-start
  56.2 0.4 collective-permute-start.1
  56.6 3.7 %collective-permute-done.1.nrecv_ref = bf16[16,192,128]{2,1,0:T(8,128)(2,1)S(1)} collective-permute-done((bf16[16,192,128]{2,1,0:T(8,128)(2,1)S(1)}, bf16[16,192,128]{2,1,0:T(8,128)(2,1)S(1)}, u32[]{:S(2)}, u32[]{:S(2)}) %collective-permute-start.1) | collective-permute-done | bytes 786464 | tf_op jit(solution)/shard_map/node_weight_pair/ppermute | solution.py:417
  60.4 0.0 collective-permute-done.erecv_ref
  60.4 1.3 %copy-done.4 = bf16[16,336,128]{2,1,0:T(8,128)(2,1)S(1)} copy-done((bf16[16,336,128]{2,1,0:T(8,128)(2,1)S(1)}, bf16[16,336,128]{2,1,0:T(8,128)(2,1)}, u32[]{:S(2)}) %copy-start.4) | copy-done | bytes 1376280
  61.7 2.1 %pair_sum.1 = bf16[16,592,128]{2,1,0:T(8,128)(2,1)} custom-call(s32[1]{0:T(128)} %bitcast.1.core_ref, bf16[16,336,128]{2,1,0:T(8,128)(2,1)S(1)} %copy-done.4, bf16[16,336,128]{2,1,0:T(8,128)(2,1)S(1)} %collective-permute-done.erecv_ref, bf16[16,192,128]{2,1,0:T(8,128)(2,1)S(1)} %get-tuple-element.46.nkeep_ref, ...), custom_call_target="tpu_custom_call" | custom-call | bytes 3538944 | tf_op jit(solution)/shard_map/pair_sum/pallas_call | solution.py:444
  63.8 4.7 %all-to-all-start.1 = ((bf16[16,592,128]{2,1,0:T(8,128)(2,1)}), bf16[16,592,128]{2,1,0:T(8,128)(2,1)S(1)}, u32[]{:S(2)}, u32[]{:S(2)}) async-start(bf16[16,592,128]{2,1,0:T(8,128)(2,1)} %pair_sum.1), calls=%async_computation.1 | async-start | bytes 4849664 | tf_op jit(solution)/shard_map/chip_exchange/all_to_all | solution.py:457
  68.6 0.1 reshape.63.rows_ref
  68.6 37.8 %all-to-all-done.1.arrived_ref = bf16[16,592,128]{2,1,0:T(8,128)(2,1)S(1)} async-done(((bf16[16,592,128]{2,1,0:T(8,128)(2,1)}), bf16[16,592,128]{2,1,0:T(8,128)(2,1)S(1)}, u32[]{:S(2)}, u32[]{:S(2)}) %all-to-all-start.1) | async-done | bytes 2424864 | tf_op jit(solution)/shard_map/chip_exchange/all_to_all | solution.py:457
  106.5 0.0 copy-done.8
  106.5 1.3 %arrive.1 = (bf16[256,512]{1,0:T(8,128)(2,1)}, f32[128,128]{1,0:T(8,128)S(1)}, bf16[128,128]{1,0:T(8,128)(2,1)S(1)}, bf16[128,128]{1,0:T(8,128)(2,1)S(1)}, bf16[128,128]{1,0:T(8,128)(2,1)S(1)}) custom-call(s32[1]{0:T(128)} %bitcast.batch_ref, bf16[16,592,128]{2,1,0:T(8,128)(2,1)S(1)} %all-to-all-done.1.arrived_ref, s32[1,512]{1,0:T(1,128)S(1)} %reshape.63.rows_ref, ...), custom_call_target="tpu_custom_call" | custom-call | tf_op jit(solution)/shard_map/arrive/pallas_call | solution.py:469
  107.7 1.5 %collective-permute-start.2 = (bf16[128,128]{1,0:T(8,128)(2,1)S(1)}, bf16[128,128]{1,0:T(8,128)(2,1)S(1)}, u32[]{:S(2)}, u32[]{:S(2)}) collective-permute-start(bf16[128,128]{1,0:T(8,128)(2,1)S(1)} %get-tuple-element.52), channel_id=1, source_target_pairs={{0,1},{1,2},{2,3},{3,0},{4,5},{5,6},{6,7},{7,4},{8,9},{9,10},{10,1... | collective-permute-start | bytes 98312 | tf_op jit(solution)/shard_map/state_exchange/ppermute | solution.py:481
  109.2 2.9 %collective-permute-start.3 = (bf16[128,128]{1,0:T(8,128)(2,1)S(1)}, bf16[128,128]{1,0:T(8,128)(2,1)S(1)}, u32[]{:S(2)}, u32[]{:S(2)}) collective-permute-start(bf16[128,128]{1,0:T(8,128)(2,1)S(1)} %get-tuple-element.53), channel_id=1, source_target_pairs={{0,2},{1,3},{2,0},{3,1},{4,6},{5,7},{6,4},{7,5},{8,10},{9,11},{10,... | collective-permute-start | bytes 98312 | tf_op jit(solution)/shard_map/state_exchange/ppermute | solution.py:481
  112.1 1.3 %collective-permute-start.4 = (bf16[128,128]{1,0:T(8,128)(2,1)S(1)}, bf16[128,128]{1,0:T(8,128)(2,1)S(1)}, u32[]{:S(2)}, u32[]{:S(2)}) collective-permute-start(bf16[128,128]{1,0:T(8,128)(2,1)S(1)} %get-tuple-element.54), channel_id=1, source_target_pairs={{0,3},{1,0},{2,1},{3,2},{4,7},{5,4},{6,5},{7,6},{8,11},{9,8},{10,9... | collective-permute-start | bytes 98312 | tf_op jit(solution)/shard_map/state_exchange/ppermute | solution.py:481
  113.5 0.0 copy-done
  113.5 1.6 %copy-done.1 = bf16[2048,512]{1,0:T(8,128)(2,1)S(1)} copy-done((bf16[2048,512]{1,0:T(8,128)(2,1)S(1)}, bf16[2048,512]{1,0:T(8,128)(2,1)}, u32[]{:S(2)}) %copy-start.1) | copy-done | bytes 2097176
  115.1 1.4 %copy-done.3 = bf16[1536,512]{1,0:T(8,128)(2,1)S(1)} copy-done((bf16[1536,512]{1,0:T(8,128)(2,1)S(1)}, bf16[1536,512]{1,0:T(8,128)(2,1)}, u32[]{:S(2)}) %copy-start.3) | copy-done | bytes 1572888
  116.5 3.0 %grad_edges.1 = bf16[2048,512]{1,0:T(8,128)(2,1)} custom-call(bf16[2048,512]{1,0:T(8,128)(2,1)S(1)} %bitcast.27, bf16[2048,512]{1,0:T(8,128)(2,1)S(1)} %copy-done.1, bf16[1536,512]{1,0:T(8,128)(2,1)S(1)} %copy-done.3), custom_call_target="tpu_custom_call" | custom-call | flops 1073741824 | bytes 6291456 | tf_op jit(solution)/shard_map/grad_edges/pallas_call | solution.py:459
  119.5 0.0 collective-permute-done.2.one_ref
  119.5 0.0 collective-permute-done.3.two_ref
  119.5 0.0 collective-permute-done.4.three_ref
  119.5 0.6 weight_grads.1
  120.2 0.1 constant_dynamic-slice_fusion
  120.2 0.5 slice_bitcast_fusion
  (15 shorter events, 0.1 us)
Async XLA Ops:
  0.6 11.9 %copy-start.2 = (bf16[1536,512]{1,0:T(8,128)(2,1)S(1)}, bf16[1536,512]{1,0:T(8,128)(2,1)}, u32[]{:S(2)}) copy-start(bf16[1536,512]{1,0:T(8,128)(2,1)} %weight_ref.7) | copy-start | bytes 4718596
  1.7 1.0 copy-start.9
  2.7 9.4 %copy-start.22 = (s32[2048]{0:T(1024)S(1)}, s32[2048]{0:T(1024)}, u32[]{:S(2)}) copy-start(s32[2048]{0:T(1024)} %param.20) | copy-start | bytes 24580
  2.7 9.4 %copy-start.23 = (s32[2048]{0:T(1024)S(1)}, s32[2048]{0:T(1024)}, u32[]{:S(2)}) copy-start(s32[2048]{0:T(1024)} %param.19) | copy-start | bytes 24580
  2.7 9.9 %copy-start.10 = (bf16[1,256,512]{2,1,0:T(8,128)(2,1)S(1)}, bf16[1,256,512]{2,1,0:T(8,128)(2,1)}, u32[]{:S(2)}) copy-start(bf16[1,256,512]{2,1,0:T(8,128)(2,1)} %param.15) | copy-start | bytes 786436
  2.7 9.9 %copy-start.16 = (f32[512]{0:T(512)S(1)}, f32[512]{0:T(512)}, u32[]{:S(2)}) copy-start(f32[512]{0:T(512)} %param.23) | copy-start | bytes 6148
  2.7 9.9 %copy-start.17 = (f32[512]{0:T(512)S(1)}, f32[512]{0:T(512)}, u32[]{:S(2)}) copy-start(f32[512]{0:T(512)} %param.27) | copy-start | bytes 6148
  3.8 20.0 %all-to-all-start = ((bf16[32,16,512]{2,1,0:T(8,128)(2,1)}), bf16[32,16,512]{2,1,0:T(8,128)(2,1)S(1)}, u32[]{:S(2)}, u32[]{:S(2)}) async-start(bf16[32,16,512]{2,1,0:T(8,128)(2,1)} %bitcast.11), calls=%async_computation | async-start | bytes 1048576 | tf_op jit(solution)/shard_map/halo_rows/all_to_all | solution.py:367
  12.5 8.0 %copy-start.5 = (s32[2048,2]{1,0:T(8,128)}, s32[2048,2]{1,0:T(8,128)S(1)}, u32[]{:S(2)}) copy-start(s32[2048,2]{1,0:T(8,128)S(1)} %copy.36.index_ref) | copy-start | bytes 49156
  12.6 1.6 %copy-start.11 = (bf16[1024,512]{1,0:T(8,128)(2,1)S(1)}, bf16[1024,512]{1,0:T(8,128)(2,1)}, u32[]{:S(2)}) copy-start(bf16[1024,512]{1,0:T(8,128)(2,1)} %nweight_ref.3) | copy-start | bytes 3145732
  14.1 9.7 %copy-start.18 = (f32[512]{0:T(512)S(1)}, f32[512]{0:T(512)}, u32[]{:S(2)}) copy-start(f32[512]{0:T(512)} %param.29) | copy-start | bytes 6148
  14.1 9.7 %copy-start.19 = (f32[512]{0:T(512)S(1)}, f32[512]{0:T(512)}, u32[]{:S(2)}) copy-start(f32[512]{0:T(512)} %param.25) | copy-start | bytes 6148
  20.5 0.8 copy-start.20
  23.8 1.0 copy-start.12
  24.9 1.0 copy-start.13
  25.9 0.9 copy-start.15
  26.9 1.0 copy-start.21
  27.9 12.2 %copy-start.6 = (s32[2048,2]{1,0:T(8,128)S(1)}, s32[2048,2]{1,0:T(8,128)}, u32[]{:S(2)}) copy-start(s32[2048,2]{1,0:T(8,128)} %copy-done.5) | copy-start | bytes 49156
  27.9 12.2 %copy-start.14 = (bf16[512,512]{1,0:T(8,128)(2,1)S(1)}, bf16[512,512]{1,0:T(8,128)(2,1)}, u32[]{:S(2)}) copy-start(bf16[512,512]{1,0:T(8,128)(2,1)} %weight_out_ref.3) | copy-start | bytes 1572868
  55.3 0.8 copy-start.7
  56.1 4.3 %collective-permute-start = (bf16[16,336,128]{2,1,0:T(8,128)(2,1)S(1)}, bf16[16,336,128]{2,1,0:T(8,128)(2,1)S(1)}, u32[]{:S(2)}, u32[]{:S(2)}) collective-permute-start(bf16[16,336,128]{2,1,0:T(8,128)(2,1)S(1)} %get-tuple-element.45), channel_id=1, source_target_pairs={{0,4},{1,5},{2,6},{3,7},{4,0},{5,1},{6,2},{7,3},{8,12},{9,13},{10,... | collective-permute-start | bytes 4128776 | tf_op jit(solution)/shard_map/edge_weight_pair/ppermute | solution.py:442
  56.2 4.2 %collective-permute-start.1 = (bf16[16,192,128]{2,1,0:T(8,128)(2,1)S(1)}, bf16[16,192,128]{2,1,0:T(8,128)(2,1)S(1)}, u32[]{:S(2)}, u32[]{:S(2)}) collective-permute-start(bf16[16,192,128]{2,1,0:T(8,128)(2,1)S(1)} %get-tuple-element.47), channel_id=1, source_target_pairs={{0,4},{1,5},{2,6},{3,7},{4,0},{5,1},{6,2},{7,3},{8,12},{9,13},{10,... | collective-permute-start | bytes 2359304 | tf_op jit(solution)/shard_map/node_weight_pair/ppermute | solution.py:417
  60.4 1.3 %copy-start.4 = (bf16[16,336,128]{2,1,0:T(8,128)(2,1)S(1)}, bf16[16,336,128]{2,1,0:T(8,128)(2,1)}, u32[]{:S(2)}) copy-start(bf16[16,336,128]{2,1,0:T(8,128)(2,1)} %get-tuple-element.44.ekeep_ref) | copy-start | bytes 4128772
  63.8 42.6 %copy-start.8 = (f32[256,512]{1,0:T(8,128)S(1)}, f32[256,512]{1,0:T(8,128)}, u32[]{:S(2)}) copy-start(f32[256,512]{1,0:T(8,128)} %copy-done.7) | copy-start | bytes 1572868
  63.8 42.6 %all-to-all-start.1 = ((bf16[16,592,128]{2,1,0:T(8,128)(2,1)}), bf16[16,592,128]{2,1,0:T(8,128)(2,1)S(1)}, u32[]{:S(2)}, u32[]{:S(2)}) async-start(bf16[16,592,128]{2,1,0:T(8,128)(2,1)} %pair_sum.1), calls=%async_computation.1 | async-start | bytes 4849664 | tf_op jit(solution)/shard_map/chip_exchange/all_to_all | solution.py:457
  106.4 7.0 %copy-start = (bf16[1,2048,512]{2,1,0:T(8,128)(2,1)S(1)}, bf16[1,2048,512]{2,1,0:T(8,128)(2,1)}, u32[]{:S(2)}) copy-start(bf16[1,2048,512]{2,1,0:T(8,128)(2,1)} %param.18) | copy-start | bytes 6291460
  107.7 11.8 %collective-permute-start.2 = (bf16[128,128]{1,0:T(8,128)(2,1)S(1)}, bf16[128,128]{1,0:T(8,128)(2,1)S(1)}, u32[]{:S(2)}, u32[]{:S(2)}) collective-permute-start(bf16[128,128]{1,0:T(8,128)(2,1)S(1)} %get-tuple-element.52), channel_id=1, source_target_pairs={{0,1},{1,2},{2,3},{3,0},{4,5},{5,6},{6,7},{7,4},{8,9},{9,10},{10,1... | collective-permute-start | bytes 98312 | tf_op jit(solution)/shard_map/state_exchange/ppermute | solution.py:481
  109.2 10.3 %collective-permute-start.3 = (bf16[128,128]{1,0:T(8,128)(2,1)S(1)}, bf16[128,128]{1,0:T(8,128)(2,1)S(1)}, u32[]{:S(2)}, u32[]{:S(2)}) collective-permute-start(bf16[128,128]{1,0:T(8,128)(2,1)S(1)} %get-tuple-element.53), channel_id=1, source_target_pairs={{0,2},{1,3},{2,0},{3,1},{4,6},{5,7},{6,4},{7,5},{8,10},{9,11},{10,... | collective-permute-start | bytes 98312 | tf_op jit(solution)/shard_map/state_exchange/ppermute | solution.py:481
  112.1 7.4 %collective-permute-start.4 = (bf16[128,128]{1,0:T(8,128)(2,1)S(1)}, bf16[128,128]{1,0:T(8,128)(2,1)S(1)}, u32[]{:S(2)}, u32[]{:S(2)}) collective-permute-start(bf16[128,128]{1,0:T(8,128)(2,1)S(1)} %get-tuple-element.54), channel_id=1, source_target_pairs={{0,3},{1,0},{2,1},{3,2},{4,7},{5,4},{6,5},{7,6},{8,11},{9,8},{10,9... | collective-permute-start | bytes 98312 | tf_op jit(solution)/shard_map/state_exchange/ppermute | solution.py:481
  113.5 1.6 %copy-start.1 = (bf16[2048,512]{1,0:T(8,128)(2,1)S(1)}, bf16[2048,512]{1,0:T(8,128)(2,1)}, u32[]{:S(2)}) copy-start(bf16[2048,512]{1,0:T(8,128)(2,1)} %get-tuple-element.50.pre_grad_ref) | copy-start | bytes 6291460
  115.1 1.4 %copy-start.3 = (bf16[1536,512]{1,0:T(8,128)(2,1)S(1)}, bf16[1536,512]{1,0:T(8,128)(2,1)}, u32[]{:S(2)}) copy-start(bf16[1536,512]{1,0:T(8,128)(2,1)} %weight_ref.7) | copy-start | bytes 4718596

commit v2 on v1

v2 whole, which is shorter than its diff:
```python
import functools
import math

import jax
import jax.numpy as jnp
from jax import lax
from jax.experimental import pallas as pl
from jax.experimental.pallas import tpu as pltpu
from jax.sharding import PartitionSpec as P

EPS = 1e-05
ALL = ("nodes", "batch")
F32 = jnp.float32
BF16 = jnp.bfloat16
TILE = 512
EDGE_IN, EDGE_OUT = 48, 16
SHARE_EDGE_IN, SHARE_EDGE_OUT, SHARE_NODE_IN, SHARE_NODE_OUT = 12, 4, 8, 4
EDGE_BLOCK = EDGE_IN + EDGE_OUT
SHARE_EDGE = SHARE_EDGE_IN + SHARE_EDGE_OUT
SHARE_NODE = 192
SHARE_ROWS = 16 * SHARE_EDGE + SHARE_NODE
SMALL = 16
STATES = 4
VMEM_FEW = 24 * 1024 * 1024
VMEM_MOST = 62 * 1024 * 1024


def nn(lhs, rhs):
    return lax.dot_general(lhs, rhs, (((1,), (0,)), ((), ())), preferred_element_type=F32)


def nt(lhs, rhs):
    return lax.dot_general(lhs, rhs, (((1,), (1,)), ((), ())), preferred_element_type=F32)


def tn(lhs, rhs):
    return lax.dot_general(lhs, rhs, (((0,), (0,)), ((), ())), preferred_element_type=F32)


def pick_rows(index_column, count, first=0):
    shape = (index_column.shape[0], count)
    columns = lax.broadcasted_iota(jnp.int32, shape, 1) + first
    return jnp.where(index_column == columns, 1.0, 0.0).astype(BF16)


def pick_columns(index_row, count, first=0):
    shape = (count, index_row.shape[1])
    rows = lax.broadcasted_iota(jnp.int32, shape, 0) + first
    return jnp.where(index_row == rows, 1.0, 0.0).astype(BF16)


def activate(pre):
    sig = jax.nn.sigmoid(pre)
    return pre * sig, sig * (1.0 + pre * (1.0 - sig))


def layer_norm(pre_norm):
    centred = pre_norm - jnp.mean(pre_norm, axis=-1, keepdims=True)
    inv = lax.rsqrt(jnp.mean(centred * centred, axis=-1, keepdims=True) + EPS)
    return centred * inv, inv


def norm_backward(scaled, normed, inv):
    mean_scaled = jnp.mean(scaled, axis=-1, keepdims=True)
    mean_product = jnp.mean(scaled * normed, axis=-1, keepdims=True)
    return (scaled - mean_scaled - normed * mean_product) * inv


def permutation(count, shares, rows):
    source = lax.broadcasted_iota(jnp.int32, (count, count), 0)
    place = lax.broadcasted_iota(jnp.int32, (count, count), 1)
    row = place % rows
    chip = (place // rows) % shares
    core = (place // (rows * shares)) % 2
    state = place // (rows * shares * 2)
    wanted = ((chip * 2 + core) * STATES + state) * rows + row
    return jnp.where(source == wanted, 1.0, 0.0).astype(BF16)


def gather_kernel(rows_ref, hidden_ref, out_ref):
    slots, peers = rows_ref.shape
    lists = rows_ref[...].astype(F32).astype(BF16)
    place = lax.broadcasted_iota(jnp.int32, (peers * slots, slots), 0)
    slot = lax.broadcasted_iota(jnp.int32, (peers * slots, slots), 1)
    spread = nn(jnp.where(place % slots == slot, 1.0, 0.0).astype(BF16), lists)
    place = lax.broadcasted_iota(jnp.int32, (peers * slots, peers), 0)
    peer = lax.broadcasted_iota(jnp.int32, (peers * slots, peers), 1)
    column = jnp.sum(
        jnp.where(place // slots == peer, spread, 0.0), axis=1, keepdims=True
    ).astype(jnp.int32)
    out_ref[...] = nn(pick_rows(column, hidden_ref.shape[0]), hidden_ref[...]).astype(BF16)


def local_kernel(
    edge_ref, rows_ref, hidden_ref, weight_ref, bias_ref, nweight_ref, nbias_ref,
    part_ref, npart_ref, ordered_ref, table
):
    width = hidden_ref.shape[1]
    nodes = hidden_ref.shape[0]

    @pl.when(pl.program_id(0) == 0)
    def _():
        hidden = hidden_ref[...]
        table[:nodes] = nn(hidden, weight_ref[width : 2 * width]).astype(BF16)
        table[nodes:] = nn(hidden, weight_ref[2 * width :]).astype(BF16)
        npart_ref[...] = nn(hidden, nweight_ref[...]) + nbias_ref[...]
        ordered_ref[...] = nn(hidden, permutation(width, 8, SHARE_NODE_IN)).astype(BF16)

    picks = jnp.concatenate(
        [pick_columns(rows_ref[0:1, :], nodes), pick_columns(rows_ref[1:2, :], nodes)], axis=0
    )
    part_ref[...] = (
        nn(edge_ref[...], weight_ref[:width]) + tn(picks, table[...]) + bias_ref[...]
    )


def forward_kernel(
    core_ref, rows_ref, gain_ref, ngain_ref, part_hbm, halo_hbm, weight_hbm, weight_out_hbm,
    ordered_hbm, npart_hbm, nweight_hbm, nweight_out_hbm, ncot_hbm,
    act_ref, slope_ref, norm_ref, inv_ref, base_ref, agg_grad_ref, send_ref, keep_ref,
    table, aggregate, grads, small, part, halo, weight_ref, weight_out_ref,
    ordered_ref, npart_ref, nweight_ref, nweight_out_ref, ncot_ref, sems
):
    step = pl.program_id(0)
    nodes, width = ordered_ref.shape
    slots = halo.shape[0]
    tiles, tile = part.shape[:2]

    def fetch(number, src, dst):
        return pltpu.make_async_copy(src, dst, sems.at[number])

    def part_fetch(number):
        start = pl.multiple_of(number * tile, tile)
        return fetch(number, part_hbm.at[pl.ds(start, tile), :], part.at[number])

    first = [
        fetch(tiles, halo_hbm, halo),
        fetch(tiles + 1, weight_hbm.at[pl.ds(width, width), :], weight_ref),
        fetch(tiles + 2, weight_out_hbm, weight_out_ref),
    ]
    late = [
        fetch(tiles + 3, ordered_hbm, ordered_ref),
        fetch(tiles + 4, npart_hbm, npart_ref),
        fetch(tiles + 5, nweight_hbm, nweight_ref),
        fetch(tiles + 6, nweight_out_hbm, nweight_out_ref),
        fetch(tiles + 7, ncot_hbm, ncot_ref),
    ]

    @pl.when(step == 0)
    def _():
        first[0].start()
        first[1].start()
        part_fetch(0).start()
        first[2].start()
        for number in range(1, tiles):
            part_fetch(number).start()
        for copy in late:
            copy.start()
        aggregate[...] = jnp.zeros_like(aggregate)
        first[0].wait()
        first[1].wait()
        table[...] = nn(halo[...], weight_ref[...]).astype(BF16)
        first[2].wait()

    part_fetch(step).wait()
    pre = part[step] + tn(pick_columns(rows_ref[0:1, :], slots, nodes), table[...])
    act, slope = activate(pre)
    act = act.astype(BF16)
    act_ref[...] = act
    slope_ref[...] = slope.astype(BF16)
    normed, inv = layer_norm(nn(act, weight_out_ref[...]))
    norm_ref[...] = normed.astype(BF16)
    inv_ref[...] = inv
    message = (normed * gain_ref[...]).astype(BF16)
    aggregate[...] += nn(pick_columns(rows_ref[1:2, :], nodes), message)

    @pl.when(step == pl.num_programs(0) - 1)
    def _():
        for copy in late:
            copy.wait()
        received = aggregate[...].astype(BF16)
        node_act, node_slope = activate(npart_ref[...] + nn(received, nweight_ref[width:]))
        node_act = node_act.astype(BF16)
        node_norm, node_inv = layer_norm(nn(node_act, nweight_out_ref[...]))
        cot = ncot_ref[...].astype(F32)
        small[...] = jnp.zeros_like(small)
        small[3:4] = jnp.sum(cot * node_norm, axis=0, keepdims=True)
        grad_norm = norm_backward(cot * ngain_ref[...], node_norm, node_inv).astype(BF16)
        grad_pre = (nt(grad_norm, nweight_out_ref[...]) * node_slope).astype(BF16)
        small[2:3] = jnp.sum(grad_pre.astype(F32), axis=0, keepdims=True)
        agg_grad_ref[...] = nt(grad_pre, nweight_ref[width:]).astype(BF16)
        base_ref[...] = cot + nt(grad_pre, nweight_ref[:width])
        received = nn(received, permutation(width, 8, SHARE_NODE_IN)).astype(BF16)
        node_act = nn(node_act, permutation(width, 16, SHARE_NODE_OUT)).astype(BF16)
        grads[0] = tn(ordered_ref[...], grad_pre).reshape(STATES, 2, 64, width)
        grads[1] = tn(received, grad_pre).reshape(STATES, 2, 64, width)
        grads[2] = tn(node_act, grad_norm).reshape(STATES, 2, 64, width)
        for dst, side in ((send_ref, 1 - core_ref[0]), (keep_ref, core_ref[0])):
            for state in range(STATES):
                for kind in range(3):
                    row = state * SHARE_NODE + kind * 64
                    dst[row : row + 64, :] = grads[kind, state, side].astype(BF16)
            dst[STATES * SHARE_NODE :, :] = small[...].astype(BF16)


def backward_kernel(
    core_ref, ecot_ref, rows_ref, act_ref, slope_ref, norm_ref, inv_ref, edge_ref,
    agg_grad_ref, gain_ref, weight_out_ref, hidden_ref, halo_hbm, weight_hbm,
    pre_grad_hbm, send_ref, keep_ref, sums_ref, terms_ref,
    grad_in, grad_out, sums, small, halo_ref, weight_ref, held, sems
):
    step = pl.program_id(0)
    nodes, width = hidden_ref.shape
    slots = halo_ref.shape[0]
    tiles, tile = held.shape[:2]
    halo_fetch = pltpu.make_async_copy(halo_hbm, halo_ref, sems.at[tiles])
    weight_fetch = pltpu.make_async_copy(
        weight_hbm.at[pl.ds(width, width), :], weight_ref, sems.at[tiles + 1]
    )

    def push(number):
        start = pl.multiple_of(number * tile, tile)
        return pltpu.make_async_copy(
            held.at[number], pre_grad_hbm.at[pl.ds(start, tile), :], sems.at[number]
        )

    @pl.when(step == 0)
    def _():
        halo_fetch.start()
        weight_fetch.start()
        grad_in[...] = jnp.zeros_like(grad_in)
        grad_out[...] = jnp.zeros_like(grad_out)
        sums[...] = jnp.zeros_like(sums)
        small[...] = jnp.zeros_like(small)

    receivers = pick_columns(rows_ref[1:2, :], nodes)
    message_grad = ecot_ref[...].astype(F32) + tn(receivers, agg_grad_ref[...])
    normed = norm_ref[...].astype(F32)
    small[1:2] += jnp.sum(message_grad * normed, axis=0, keepdims=True)
    grad_norm = norm_backward(message_grad * gain_ref[...], normed, inv_ref[...]).astype(BF16)
    grad_pre = nt(grad_norm, weight_out_ref[...]) * slope_ref[...].astype(F32)
    grad_pre = grad_pre.astype(BF16)
    held[step] = grad_pre
    push(step).start()
    small[0:1] += jnp.sum(grad_pre.astype(F32), axis=0, keepdims=True)
    grad_out[...] += tn(act_ref[...], grad_norm)
    grad_in[:width] += tn(edge_ref[...], grad_pre)
    sums[: nodes + slots] += nn(pick_columns(rows_ref[0:1, :], nodes + slots), grad_pre)
    sums[nodes + slots :] += nn(receivers, grad_pre)

    @pl.when(step == pl.num_programs(0) - 1)
    def _():
        halo_fetch.wait()
        weight_fetch.wait()
        own = sums[:nodes].astype(BF16)
        remote = sums[nodes : nodes + slots].astype(BF16)
        received = sums[nodes + slots :].astype(BF16)
        sums_ref[:nodes] = own
        sums_ref[nodes:] = received
        terms_ref[...] = nt(remote, weight_ref[...]).astype(BF16)
        hidden = hidden_ref[...]
        grad_in[width : 2 * width] = tn(hidden, own) + tn(halo_ref[...], remote)
        grad_in[2 * width :] = tn(hidden, received)
        core = core_ref[0]
        for dst, side in ((send_ref, 1 - core), (keep_ref, core)):

            def pack(chip, carry):
                piece = chip * 2 + side
                row = pl.multiple_of(chip * EDGE_BLOCK, EDGE_BLOCK)
                start = pl.multiple_of(piece * EDGE_IN, EDGE_IN)
                dst[pl.ds(row, EDGE_IN), :] = grad_in[pl.ds(start, EDGE_IN), :].astype(BF16)
                row = pl.multiple_of(row + EDGE_IN, EDGE_OUT)
                start = pl.multiple_of(piece * EDGE_OUT, EDGE_OUT)
                dst[pl.ds(row, EDGE_OUT), :] = grad_out[pl.ds(start, EDGE_OUT), :].astype(BF16)
                return carry

            lax.fori_loop(0, 16, pack, 0, unroll=4)
            dst[16 * EDGE_BLOCK :, :] = small[...].astype(BF16)
        for number in range(tiles):
            push(number).wait()


def pair_kernel(
    batch_ref, keep_ref, recv_ref, nkeep_ref, nrecv_ref,
    mine_ref, one_ref, two_ref, three_ref, states
):
    def both(start, count):
        rows = slice(start, start + count)
        return keep_ref[rows, :].astype(F32) + recv_ref[rows, :].astype(F32)

    def node_both(start, count):
        rows = slice(start, start + count)
        return nkeep_ref[rows, :].astype(F32) + nrecv_ref[rows, :].astype(F32)

    for chip in range(16):
        start = chip * EDGE_BLOCK
        into, out = both(start, EDGE_IN), both(start + EDGE_IN, EDGE_OUT)
        row = chip * SHARE_EDGE
        for state in range(STATES):
            states[state, row : row + SHARE_EDGE_IN, :] = into[
                state * SHARE_EDGE_IN : (state + 1) * SHARE_EDGE_IN
            ]
            states[state, row + SHARE_EDGE_IN : row + SHARE_EDGE, :] = out[
                state * SHARE_EDGE_OUT : (state + 1) * SHARE_EDGE_OUT
            ]
    small = both(16 * EDGE_BLOCK, SMALL) + node_both(STATES * SHARE_NODE, SMALL)
    for state in range(STATES):
        states[state, 16 * SHARE_EDGE : SHARE_ROWS, :] = node_both(state * SHARE_NODE, SHARE_NODE)
        states[state, SHARE_ROWS:, :] = small
    for away, ref in enumerate((mine_ref, one_ref, two_ref, three_ref)):
        ref[...] = states[lax.rem(batch_ref[0] + away, STATES)].astype(BF16)


def merge_kernel(mine_ref, one_ref, two_ref, three_ref, out_ref, block):
    total = (
        mine_ref[...].astype(F32)
        + one_ref[...].astype(F32)
        + two_ref[...].astype(F32)
        + three_ref[...].astype(F32)
    )
    chips, _, width = block.shape
    block[:, :16, :] = total[:256].reshape(chips, 16, width)
    block[:, 16:24, :] = total[256:384].reshape(chips, 8, width)
    for chip in range(chips):
        block[chip, 24:28, :] = total[384 + chip * 4 : 388 + chip * 4]
        block[chip, 28:32, :] = total[SHARE_ROWS : SHARE_ROWS + 4]
    out_ref[...] = block[...].astype(BF16)


def edge_out_kernel(ecot_ref, pre_grad_ref, weight_ref, out_ref):
    out_ref[...] = (
        ecot_ref[...].astype(F32) + nt(pre_grad_ref[...], weight_ref[...])
    ).astype(BF16)


def nodes_kernel(halo_ref, rows_ref, sums_ref, weight_ref, base_ref, out_ref):
    nodes, width = base_ref.shape
    picks = pick_columns(rows_ref[...], nodes)
    out_ref[...] = (
        base_ref[...]
        + nt(sums_ref[:nodes], weight_ref[width : 2 * width])
        + nt(sums_ref[nodes:], weight_ref[2 * width :])
        + nn(picks, halo_ref[...])
    ).astype(BF16)


def finish_kernel(factor, arrived_ref, edge_in_ref, edge_out_ref, node_in_ref, node_out_ref, small_ref):
    total = jnp.sum(arrived_ref[...].astype(F32), axis=0) * factor
    row = 0
    for ref in (edge_in_ref, edge_out_ref, node_in_ref, node_out_ref, small_ref):
        count = ref.shape[0]
        ref[...] = total[row : row + count, :]
        row += count


def call(body, outs, grid=None, in_specs=None, out_specs=None, scratch=(), cost=None, limit=None):
    args = {}
    if grid is not None:
        args = dict(grid=grid, in_specs=in_specs, out_specs=out_specs)
    elif in_specs is not None:
        args = dict(in_specs=in_specs)
    return pl.pallas_call(
        body,
        out_shape=outs,
        scratch_shapes=scratch,
        compiler_params=pltpu.CompilerParams(vmem_limit_bytes=limit or VMEM_MOST),
        cost_estimate=cost,
        **args,
    )


def flops(count, moved):
    return pl.CostEstimate(flops=int(count), bytes_accessed=int(moved), transcendentals=0)


def shape(*dims, dtype=BF16):
    return jax.ShapeDtypeStruct(dims, dtype)


def far(*dims, dtype=BF16):
    return pltpu.HBM(dims, dtype)


def keep_far(*arrays):
    return [pltpu.with_memory_space_constraint(item, pltpu.HBM) for item in arrays]


def full(*dims):
    return pl.BlockSpec(dims, lambda i: (0,) * len(dims))


def tiled(*dims):
    return pl.BlockSpec(dims, lambda i: (i,) + (0,) * (len(dims) - 1))


SCALAR = pl.BlockSpec(memory_space=pltpu.SMEM)
FAR = pl.BlockSpec(memory_space=pltpu.HBM)
WHOLE = pl.BlockSpec(memory_space=pltpu.VMEM)


def shards(
    node_latents, edge_latents, node_cotangent, edge_cotangent, senders, receivers, send_rows,
    edge_weight_in, edge_bias, edge_weight_out, edge_gain,
    node_weight_in, node_bias, node_weight_out, node_gain,
):
    nodes, width = node_latents.shape[1:]
    edges = edge_latents.shape[1]
    parts = lax.axis_size("nodes")
    batch_size = lax.axis_size("batch")
    slots = send_rows.shape[1] * send_rows.shape[2]
    hidden = node_latents[0]
    edge_rows = edge_latents[0]
    ncot = node_cotangent[0]
    ecot = edge_cotangent[0]
    node_index = lax.axis_index("nodes")
    core = jnp.reshape(node_index % 2, (1,)).astype(jnp.int32)
    batch = jnp.reshape(lax.axis_index("batch"), (1,)).astype(jnp.int32)
    tile = min(TILE, edges)
    grid = (edges // tile,)

    row = lambda vector: vector.reshape(1, width)
    index_rows = jnp.stack([senders, receivers], axis=0)

    partner = [(i, i ^ batch_size) for i in range(parts * batch_size)]
    places = [
        [(n * batch_size + b, n * batch_size + (b + away) % batch_size)
         for n in range(parts) for b in range(batch_size)]
        for away in (1, 2, 3)
    ]

    with jax.named_scope("halo_rows"):
        outgoing = call(gather_kernel, shape(slots, width))(send_rows[0].T, hidden)
        halo = lax.all_to_all(
            outgoing.reshape(parts, -1, width), "nodes", 0, 0, tiled=True
        ).reshape(slots, width)
    rows_tile = pl.BlockSpec((2, tile), lambda i: (0, i))
    edge_tile = tiled(tile, width)
    node_full = full(nodes, width)
    node_f32 = shape(nodes, width, dtype=F32)
    with jax.named_scope("edge_pre_local"):
        part, npart, ordered = call(
            local_kernel,
            (far(edges, width, dtype=F32), far(nodes, width, dtype=F32), far(nodes, width)),
            grid,
            [
                edge_tile, rows_tile, node_full, full(3 * width, width), full(1, width),
                full(width, width), full(1, width),
            ],
            (edge_tile, node_full, node_full),
            [pltpu.VMEM((2 * nodes, width), BF16)],
            flops(2 * edges * width * 2 * width, 6 * edges * width),
        )(edge_rows, index_rows, hidden, edge_weight_in, row(edge_bias), node_weight_in, row(node_bias))
    with jax.named_scope("forward"):
        node_pair = shape(STATES * SHARE_NODE + SMALL, width)
        act, slope, norm, inv, base, agg_grad, nsend, nkeep = call(
            forward_kernel,
            (
                shape(edges, width), shape(edges, width), shape(edges, width),
                shape(edges, 1, dtype=F32), far(nodes, width, dtype=F32), shape(nodes, width),
                node_pair, far(*node_pair.shape),
            ),
            grid,
            [SCALAR, rows_tile, full(1, width), full(1, width)] + [FAR] * 9,
            (edge_tile, edge_tile, edge_tile, tiled(tile, 1), node_full, node_full)
            + (full(*node_pair.shape),) * 2,
            [
                pltpu.VMEM((slots, width), BF16), pltpu.VMEM((nodes, width), F32),
                pltpu.VMEM((3, STATES, 2, 64, width), F32), pltpu.VMEM((SMALL, width), F32),
                pltpu.VMEM((edges // tile, tile, width), F32), pltpu.VMEM((slots, width), BF16),
                pltpu.VMEM((width, width), BF16), pltpu.VMEM((width, width), BF16),
                pltpu.VMEM((nodes, width), BF16), pltpu.VMEM((nodes, width), F32),
                pltpu.VMEM((2 * width, width), BF16), pltpu.VMEM((width, width), BF16),
                pltpu.VMEM((nodes, width), BF16), pltpu.SemaphoreType.DMA((edges // tile + 8,)),
            ],
            flops(2 * edges * width * 3 * width, 12 * edges * width),
            VMEM_FEW,
        )(
            core, index_rows, row(edge_gain), row(node_gain),
            *keep_far(
                part, halo, edge_weight_in, edge_weight_out, ordered, npart, node_weight_in,
                node_weight_out, ncot,
            ),
        )
    with jax.named_scope("node_weight_pair"):
        nrecv = lax.ppermute(nsend, ALL, partner)
    with jax.named_scope("backward"):
        edge_pair = shape(16 * EDGE_BLOCK + SMALL, width)
        pre_grad, esend, ekeep, sums, terms = call(
            backward_kernel,
            (
                far(edges, width), edge_pair, far(*edge_pair.shape), far(2 * nodes, width),
                far(slots, width),
            ),
            grid,
            [
                SCALAR, edge_tile, rows_tile, edge_tile, edge_tile, edge_tile,
                tiled(tile, 1), edge_tile, node_full, full(1, width), full(width, width),
                node_full, FAR, FAR,
            ],
            (
                FAR, full(*edge_pair.shape), full(*edge_pair.shape),
                full(2 * nodes, width), full(slots, width),
            ),
            [
                pltpu.VMEM((3 * width, width), F32), pltpu.VMEM((width, width), F32),
                pltpu.VMEM((2 * nodes + slots, width), F32), pltpu.VMEM((SMALL, width), F32),
                pltpu.VMEM((slots, width), BF16), pltpu.VMEM((width, width), BF16),
                pltpu.VMEM((edges // tile, tile, width), BF16),
                pltpu.SemaphoreType.DMA((edges // tile + 2,)),
            ],
            flops(2 * edges * width * 6 * width, 14 * edges * width),
            VMEM_FEW,
        )(
            core, ecot, index_rows, act, slope, norm, inv, edge_rows, agg_grad,
            row(edge_gain), edge_weight_out, hidden, *keep_far(halo, edge_weight_in),
        )
    with jax.named_scope("edge_weight_pair"):
        erecv = lax.ppermute(esend, ALL, partner)
    with jax.named_scope("halo_back"):
        back = lax.all_to_all(
            terms.reshape(parts, -1, width), "nodes", 0, 0, tiled=True
        ).reshape(slots, width)
    with jax.named_scope("pair_sum"):
        block = shape(SHARE_ROWS + SMALL, width)
        blocks = call(
            pair_kernel, (block,) * STATES, in_specs=[SCALAR] + [WHOLE] * 4,
            scratch=[pltpu.VMEM((STATES, *block.shape), F32)],
            cost=flops(0, 8 * edges * width), limit=VMEM_FEW,
        )(batch, *keep_far(ekeep), erecv, *keep_far(nkeep), nrecv)
    with jax.named_scope("weight_states"):
        got = [lax.ppermute(item, ALL, perm) for item, perm in zip(blocks[1:], places)]
    with jax.named_scope("grad_edges"):
        grad_edges = call(
            edge_out_kernel,
            shape(edges, width),
            grid,
            [edge_tile, edge_tile, full(width, width)],
            edge_tile,
            cost=flops(2 * edges * width * width, 6 * edges * width), limit=VMEM_FEW,
        )(*keep_far(ecot, pre_grad, edge_weight_in))
    with jax.named_scope("merge"):
        got, grad_edges = lax.optimization_barrier((got, grad_edges))
        sent = call(
            merge_kernel, shape(16, 32, width),
            scratch=[pltpu.VMEM((16, 32, width), F32)], limit=VMEM_FEW,
        )(blocks[0], *got)
    with jax.named_scope("chip_exchange"):
        chips = parts // 2
        groups = [[2 * chip + side for chip in range(chips)] for side in range(2)]
        arrived = lax.all_to_all(sent, "nodes", 0, 0, tiled=True, axis_index_groups=groups)
    with jax.named_scope("grad_nodes"):
        grad_nodes = call(nodes_kernel, shape(nodes, width), limit=VMEM_FEW)(
            back, send_rows.reshape(1, slots), *keep_far(sums, edge_weight_in, base)
        )
    with jax.named_scope("weight_grads"):
        factor = 1.0 / math.sqrt(batch_size * edges * parts)
        edge_in, edge_out, node_in, node_out, small = call(
            functools.partial(finish_kernel, factor),
            (
                shape(12, width, dtype=F32), shape(4, width, dtype=F32), shape(8, width, dtype=F32),
                shape(4, width, dtype=F32), shape(4, width, dtype=F32),
            ),
            limit=VMEM_FEW,
        )(arrived)
        place = node_index * batch_size + lax.axis_index("batch")
        small = lax.dynamic_slice(small, (0, place * 4), (4, 4))
    return (
        grad_nodes[None], grad_edges[None], edge_in, small[0], edge_out, small[1],
        node_in, small[2], node_out, small[3],
    )


def solution(mesh):
    rows = P("batch", "nodes", None)
    split = P(ALL, None)
    return jax.shard_map(
        shards,
        mesh=mesh,
        in_specs=(rows,) * 4 + (P("nodes"), P("nodes"), P("nodes", None, None)) + (P(),) * 8,
        out_specs=(rows, rows) + (split, P(ALL)) * 4,
        check_vma=False,
    )
```

time: 122 us -> 102 us (0.84)
  waiting for transfers between devices: 44 us -> 25.7 us
  local copies, waits for them, and re-layouts: 14.7 us -> 1.6 us
  starting transfers between devices: 19.3 us -> 25.9 us
  Pallas kernels: 41.9 us -> 45.8 us
  other arithmetic: 0.03 us -> 1.34 us
    all_to_all x1, waiting for transfers between devices: 37.8 us -> 7.86 us  [shards(): lax.all_to_all(sent, 'nodes', 0, 0, tiled=True, axis_index_groups=groups)]
    ppermute x3, waiting for transfers between devices: 0.01 us -> 14.7 us  [shards(): lax.ppermute(item, ALL, perm)]
    unnamed x49 -> x19, local copies, waits for them, and re-layouts: 13.5 us -> 0.91 us
    all_to_all x0 -> x1, starting transfers between devices: none -> 4.23 us  [shards(): lax.all_to_all(terms.reshape(parts, -1, width), 'nodes', 0, 0, tiled=True)]
    ppermute x1, waiting for transfers between devices: 3.74 us -> 0.01 us  [shards(): nrecv = lax.ppermute(nsend, ALL, partner)]
    pallas_call x5 -> x6, Pallas kernels: 26.1 us -> 28.4 us  [the longest x1 12.5 us: shards(): call(backward_kernel, (far(edges, width), edge_pair, far(*edge_pair.shape...]
    all_to_all x1, starting transfers between devices: 4.74 us -> 6.97 us  [shards(): lax.all_to_all(sent, 'nodes', 0, 0, tiled=True, axis_index_groups=groups)]
    pallas_call x1, Pallas kernels: 3.01 us -> 5.16 us  [shards(): call(edge_out_kernel, shape(edges, width), grid, [edge_tile, edge_tile, f...]
  transfers between devices with their start and end apart: 7 -> 8, of which waited for: 3 -> 4; matrix products, arithmetic and copies ran while one was open for 0% -> 1% of each run, Pallas kernels for 8% -> 19%
where the time goes in v2:
time: 102 us; the launch traced here: 101 us
  Pallas kernels  45.8 us (45%)
  starting transfers between devices  25.9 us (25%)
  waiting for transfers between devices  25.7 us (25%)
  local copies, waits for them, and re-layouts  1.6 us (2%)
  other arithmetic  1.34 us (1%)
    ppermute x3, waiting for transfers between devices, shards(): lax.ppermute(item, ALL, perm)  14.7 us
    pallas_call x1, Pallas kernels, shards(): call(backward_kernel, (far(edges, width), edge_pair, far(*edge_pair.shape...  12.5 us
    pallas_call x1, Pallas kernels, shards(): call(forward_kernel, (shape(edges, width), shape(edges, width), shape(edg...  11.6 us
    all_to_all x1, starting transfers between devices, shards(): lax.all_to_all(outgoing.reshape(parts, -1, width), 'nodes', 0, 0, tiled=T...  8.24 us
    all_to_all x1, waiting for transfers between devices, shards(): lax.all_to_all(sent, 'nodes', 0, 0, tiled=True, axis_index_groups=groups)  7.86 us
    pallas_call x1, Pallas kernels, shards(): call(local_kernel, (far(edges, width, dtype=F32), far(nodes, width, dtype...  7.24 us
    all_to_all x1, starting transfers between devices, shards(): lax.all_to_all(sent, 'nodes', 0, 0, tiled=True, axis_index_groups=groups)  6.97 us
    ppermute x3, starting transfers between devices, shards(): lax.ppermute(item, ALL, perm)  5.9 us
  transfers between devices with their start and end apart: 8, of which 4 were waited for; matrix products, arithmetic and copies ran while one was open for 1% of the time, Pallas kernels for 19%

profile of v2, /device:TPU:0, one launch (start us, length us, event | category | flops | bytes accessed | tf_op | source)
XLA Modules:
  0.0 101.2 jit_solution(1871274137979959321)
XLA Ops:
  0.6 2.3 %halo_rows.1 = bf16[512,512]{1,0:T(8,128)(2,1)} custom-call(s32[16,32]{1,0:T(8,128)} %bitcast.46, bf16[256,512]{1,0:T(8,128)(2,1)} %bitcast.32), custom_call_target="tpu_custom_call" | custom-call | tf_op jit(solution)/shard_map/halo_rows/pallas_call | solution.py:432
  2.9 8.2 %all-to-all-start = ((bf16[32,16,512]{2,1,0:T(8,128)(2,1)}), bf16[32,16,512]{2,1,0:T(8,128)(2,1)S(1)}, u32[]{:S(2)}, u32[]{:S(2)}) async-start(bf16[32,16,512]{2,1,0:T(8,128)(2,1)} %bitcast.40), calls=%async_computation | async-start | bytes 1048576 | tf_op jit(solution)/shard_map/halo_rows/all_to_all | solution.py:433
  11.2 1.3 %pad_add_fusion.rows_ref = s32[2,2048]{1,0:T(2,128)} fusion(s32[1,2048]{1,0:T(1,128)} %bitcast.47, s32[1,2048]{1,0:T(1,128)} %bitcast.48), kind=kLoop, calls=%fused_computation | loop fusion | flops 4096 | bytes 32768 | tf_op jit(solution)/shard_map/stack | solution.py:422
  12.5 0.0 copy-start.2
  12.5 0.0 copy-start.5
  12.5 0.0 copy-start.6
  12.5 7.2 %edge_pre_local.1 = (f32[2048,512]{1,0:T(8,128)}, f32[256,512]{1,0:T(8,128)}, bf16[256,512]{1,0:T(8,128)(2,1)}) custom-call(bf16[2048,512]{1,0:T(8,128)(2,1)} %bitcast.35, s32[2,2048]{1,0:T(2,128)} %pad_add_fusion.rows_ref, bf16[256,512]{1,0:T(8,128)(2,1)} %bitcast.33, bf16[1536,512]{1,0:T(8,128)(2,1)} %weight_ref.5, f32[1,512]{1,0:T(1,128)} %bitcast.50, ...), custom_call_target="tpu_custom_call" | custom-call | flops 2147483648 | bytes 6291456 | tf_op jit(solution)/shard_map/edge_pre_local/pallas_call | solution.py:441
  19.7 3.2 %all-to-all-done = bf16[32,16,512]{2,1,0:T(8,128)(2,1)S(1)} async-done(((bf16[32,16,512]{2,1,0:T(8,128)(2,1)}), bf16[32,16,512]{2,1,0:T(8,128)(2,1)S(1)}, u32[]{:S(2)}, u32[]{:S(2)}) %all-to-all-start) | async-done | bytes 524320 | tf_op jit(solution)/shard_map/halo_rows/all_to_all | solution.py:433
  22.9 0.0 copy-start.7
  22.9 0.8 copy-done.7
  23.7 0.0 copy-done.2
  23.7 0.0 copy-done.5
  23.7 0.0 copy-done.6
  23.7 0.0 copy-start
  23.7 0.0 copy-start.1
  23.7 0.0 copy-start.3
  23.7 0.0 copy-start.4
  23.8 11.6 %forward.1 = (bf16[2048,512]{1,0:T(8,128)(2,1)S(1)}, bf16[2048,512]{1,0:T(8,128)(2,1)S(1)}, bf16[2048,512]{1,0:T(8,128)(2,1)S(1)}, f32[2048,1]{1,0:T(8,128)S(1)}...) custom-call(s32[1]{0:T(128)} %bitcast.core_ref, ...), custom_call_target="tpu_custom_call" | custom-call | flops 3221225472 | bytes 12582912 | tf_op jit(solution)/shard_map/forward/pallas_call | solution.py:455
  35.4 0.0 copy-done
  35.4 0.0 copy-done.1
  35.4 0.0 copy-done.3
  35.4 0.0 copy-done.4
  35.4 12.5 %backward.1 = (bf16[2048,512]{1,0:T(8,128)(2,1)}, bf16[1040,512]{1,0:T(8,128)(2,1)}, bf16[1040,512]{1,0:T(8,128)(2,1)}, bf16[512,512]{1,0:T(8,128)(2,1)}, bf16[512,512]{1,0:T(8,128)(2,1)}) custom-call(s32[1]{0:T(128)} %bitcast.core_ref, bf16[2048,512]{1,0:T(8,128)(2,1)S(1)} %bitcast.31, s32[2,2048]{1,0:T(2,128)S(1)} %copy-done.2, ...), custom_call_target="tpu_custom_call" | custom-call | flops 6442450944 | bytes 14680064 | tf_op jit(solution)/shard_map/backward/pallas_call | solution.py:488
  47.9 0.1 collective-permute-start
  48.1 0.4 collective-permute-start.1
  48.5 4.2 %all-to-all-start.1 = ((bf16[32,16,512]{2,1,0:T(8,128)(2,1)}), bf16[32,16,512]{2,1,0:T(8,128)(2,1)S(1)}, u32[]{:S(2)}, u32[]{:S(2)}) async-start(bf16[32,16,512]{2,1,0:T(8,128)(2,1)} %bitcast.42), calls=%async_computation.1 | async-start | bytes 1048576 | tf_op jit(solution)/shard_map/halo_back/all_to_all | solution.py:520
  52.7 0.0 collective-permute-done.1.nrecv_ref
  52.8 0.0 collective-permute-done.recv_ref
  52.8 2.1 %pair_sum.1 = (bf16[464,512]{1,0:T(8,128)(2,1)S(1)}, bf16[464,512]{1,0:T(8,128)(2,1)S(1)}, bf16[464,512]{1,0:T(8,128)(2,1)S(1)}, bf16[464,512]{1,0:T(8,128)(2,1)S(1)}) custom-call(s32[1]{0:T(128)} %bitcast.18.batch_ref, bf16[1040,512]{1,0:T(8,128)(2,1)} %get-tuple-element.50.keep_ref, bf16[1040,512]{1,0:T(8,128)(2,1)S(1)} %collective-permute-done.recv_ref, ...), custom_call_target="tpu_custom_call" | custom-call | bytes 8388608 | tf_op jit(solution)/shard_map/pair_sum/pallas_call | solution.py:525
  54.9 1.6 %collective-permute-start.2 = (bf16[464,512]{1,0:T(8,128)(2,1)S(1)}, bf16[464,512]{1,0:T(8,128)(2,1)S(1)}, u32[]{:S(2)}, u32[]{:S(2)}) collective-permute-start(bf16[464,512]{1,0:T(8,128)(2,1)S(1)} %get-tuple-element.54), channel_id=1, source_target_pairs={{0,1},{1,2},{2,3},{3,0},{4,5},{5,6},{6,7},{7,4},{8,9},{9,10},{10,1... | collective-permute-start | bytes 1425416 | tf_op jit(solution)/shard_map/weight_states/ppermute | solution.py:531
  56.6 2.9 %collective-permute-start.3 = (bf16[464,512]{1,0:T(8,128)(2,1)S(1)}, bf16[464,512]{1,0:T(8,128)(2,1)S(1)}, u32[]{:S(2)}, u32[]{:S(2)}) collective-permute-start(bf16[464,512]{1,0:T(8,128)(2,1)S(1)} %get-tuple-element.55), channel_id=1, source_target_pairs={{0,2},{1,3},{2,0},{3,1},{4,6},{5,7},{6,4},{7,5},{8,10},{9,11},{10,... | collective-permute-start | bytes 1425416 | tf_op jit(solution)/shard_map/weight_states/ppermute | solution.py:531
  59.5 1.3 %collective-permute-start.4 = (bf16[464,512]{1,0:T(8,128)(2,1)S(1)}, bf16[464,512]{1,0:T(8,128)(2,1)S(1)}, u32[]{:S(2)}, u32[]{:S(2)}) collective-permute-start(bf16[464,512]{1,0:T(8,128)(2,1)S(1)} %get-tuple-element.56), channel_id=1, source_target_pairs={{0,3},{1,0},{2,1},{3,2},{4,7},{5,4},{6,5},{7,6},{8,11},{9,8},{10,9... | collective-permute-start | bytes 1425416 | tf_op jit(solution)/shard_map/weight_states/ppermute | solution.py:531
  60.8 5.2 %grad_edges.1 = bf16[2048,512]{1,0:T(8,128)(2,1)} custom-call(bf16[2048,512]{1,0:T(8,128)(2,1)} %bitcast.30, bf16[2048,512]{1,0:T(8,128)(2,1)} %get-tuple-element.57.pre_grad_ref, bf16[1536,512]{1,0:T(8,128)(2,1)} %weight_ref.5), custom_call_target="tpu_custom_call" | custom-call | flops 1073741824 | bytes 6291456 | tf_op jit(solution)/shard_map/grad_edges/pallas_call | solution.py:533
  66.0 0.0 copy-start.8
  66.0 3.3 %collective-permute-done.2.one_ref = bf16[464,512]{1,0:T(8,128)(2,1)S(1)} collective-permute-done((bf16[464,512]{1,0:T(8,128)(2,1)S(1)}, bf16[464,512]{1,0:T(8,128)(2,1)S(1)}, u32[]{:S(2)}, u32[]{:S(2)}) %collective-permute-start.2) | collective-permute-done | bytes 475168 | tf_op jit(solution)/shard_map/weight_states/ppermute | solution.py:531
  69.3 11.4 %collective-permute-done.3.two_ref = bf16[464,512]{1,0:T(8,128)(2,1)S(1)} collective-permute-done((bf16[464,512]{1,0:T(8,128)(2,1)S(1)}, bf16[464,512]{1,0:T(8,128)(2,1)S(1)}, u32[]{:S(2)}, u32[]{:S(2)}) %collective-permute-start.3) | collective-permute-done | bytes 475168 | tf_op jit(solution)/shard_map/weight_states/ppermute | solution.py:531
  80.7 0.0 collective-permute-done.4.three_ref
  80.7 1.2 %merge.1 = bf16[16,32,512]{2,1,0:T(8,128)(2,1)} custom-call(bf16[464,512]{1,0:T(8,128)(2,1)S(1)} %get-tuple-element.59.mine_ref, bf16[464,512]{1,0:T(8,128)(2,1)S(1)} %collective-permute-done.2.one_ref, bf16[464,512]{1,0:T(8,128)(2,1)S(1)} %collective-permute-done.3.two_ref, bf16[464,512]{1,0:T(8,128)(2,1)S(1)} %collective-permute-done.4.three_ref), custom_call_target="tpu_custom_call" | custom-call | tf_op jit(solution)/shard_map/merge/pallas_call | solution.py:543
  81.9 0.0 all-to-all-done.1
  81.9 7.0 %all-to-all-start.2 = ((bf16[16,32,512]{2,1,0:T(8,128)(2,1)}), bf16[16,32,512]{2,1,0:T(8,128)(2,1)S(1)}, u32[]{:S(2)}, u32[]{:S(2)}) async-start(bf16[16,32,512]{2,1,0:T(8,128)(2,1)} %merge.1), calls=%async_computation.2 | async-start | bytes 1048576 | tf_op jit(solution)/shard_map/chip_exchange/all_to_all | solution.py:550
  88.9 0.0 copy-done.8
  88.9 0.1 copy.26
  89.0 0.1 reshape.63.rows_ref
  89.1 3.0 %grad_nodes.1 = bf16[256,512]{1,0:T(8,128)(2,1)} custom-call(bf16[512,512]{1,0:T(8,128)(2,1)S(1)} %bitcast.29, s32[1,512]{1,0:T(1,128)S(1)} %reshape.63.rows_ref, bf16[512,512]{1,0:T(8,128)(2,1)} %get-tuple-element.48.sums_ref, bf16[1536,512]{1,0:T(8,128)(2,1)} %weight_ref.5, f32[256,512]{1,0:T(8,128)} %get-tuple-element.49.base_ref), custom_call_target="tpu_custom_call" | custom-call | tf_op jit(solution)/shard_map/grad_nodes/pallas_call | solution.py:552
  92.1 7.9 %all-to-all-done.2.arrived_ref = bf16[16,32,512]{2,1,0:T(8,128)(2,1)S(1)} async-done(((bf16[16,32,512]{2,1,0:T(8,128)(2,1)}), bf16[16,32,512]{2,1,0:T(8,128)(2,1)S(1)}, u32[]{:S(2)}, u32[]{:S(2)}) %all-to-all-start.2) | async-done | bytes 524320 | tf_op jit(solution)/shard_map/chip_exchange/all_to_all | solution.py:550
  99.9 0.7 weight_grads.1
  100.6 0.1 constant_dynamic-slice_fusion
  100.7 0.5 slice_bitcast_fusion
Async XLA Ops:
  2.9 20.0 %all-to-all-start = ((bf16[32,16,512]{2,1,0:T(8,128)(2,1)}), bf16[32,16,512]{2,1,0:T(8,128)(2,1)S(1)}, u32[]{:S(2)}, u32[]{:S(2)}) async-start(bf16[32,16,512]{2,1,0:T(8,128)(2,1)} %bitcast.40), calls=%async_computation | async-start | bytes 1048576 | tf_op jit(solution)/shard_map/halo_rows/all_to_all | solution.py:433
  12.5 11.2 %copy-start.2 = (s32[2,2048]{1,0:T(2,128)S(1)}, s32[2,2048]{1,0:T(2,128)}, u32[]{:S(2)}) copy-start(s32[2,2048]{1,0:T(2,128)} %pad_add_fusion.rows_ref) | copy-start | bytes 49156
  12.5 11.2 %copy-start.5 = (f32[512]{0:T(512)S(1)}, f32[512]{0:T(512)}, u32[]{:S(2)}) copy-start(f32[512]{0:T(512)} %param.29) | copy-start | bytes 6148
  12.5 11.2 %copy-start.6 = (f32[512]{0:T(512)S(1)}, f32[512]{0:T(512)}, u32[]{:S(2)}) copy-start(f32[512]{0:T(512)} %param.25) | copy-start | bytes 6148
  22.9 0.8 copy-start.7
  23.7 11.7 %copy-start = (bf16[1,2048,512]{2,1,0:T(8,128)(2,1)S(1)}, bf16[1,2048,512]{2,1,0:T(8,128)(2,1)}, u32[]{:S(2)}) copy-start(bf16[1,2048,512]{2,1,0:T(8,128)(2,1)} %param.18) | copy-start | bytes 6291460
  23.7 11.7 %copy-start.1 = (bf16[1,256,512]{2,1,0:T(8,128)(2,1)S(1)}, bf16[1,256,512]{2,1,0:T(8,128)(2,1)}, u32[]{:S(2)}) copy-start(bf16[1,256,512]{2,1,0:T(8,128)(2,1)} %param.15) | copy-start | bytes 786436
  23.7 11.7 %copy-start.3 = (bf16[1,2048,512]{2,1,0:T(8,128)(2,1)S(1)}, bf16[1,2048,512]{2,1,0:T(8,128)(2,1)}, u32[]{:S(2)}) copy-start(bf16[1,2048,512]{2,1,0:T(8,128)(2,1)} %param.16) | copy-start | bytes 6291460
  23.7 11.7 %copy-start.4 = (bf16[512,512]{1,0:T(8,128)(2,1)S(1)}, bf16[512,512]{1,0:T(8,128)(2,1)}, u32[]{:S(2)}) copy-start(bf16[512,512]{1,0:T(8,128)(2,1)} %weight_out_ref.1) | copy-start | bytes 1572868
  47.9 4.8 %collective-permute-start = (bf16[1040,512]{1,0:T(8,128)(2,1)}, bf16[1040,512]{1,0:T(8,128)(2,1)S(1)}, u32[]{:S(2)}, u32[]{:S(2)}) collective-permute-start(bf16[1040,512]{1,0:T(8,128)(2,1)} %get-tuple-element.51), channel_id=1, source_target_pairs={{0,4},{1,5},{2,6},{3,7},{4,0},{5,1},{6,2},{7,3},{8,12},{9,13},{10,... | collective-permute-start | bytes 3194888 | tf_op jit(solution)/shard_map/edge_weight_pair/ppermute | solution.py:518
  48.1 4.7 %collective-permute-start.1 = (bf16[784,512]{1,0:T(8,128)(2,1)}, bf16[784,512]{1,0:T(8,128)(2,1)S(1)}, u32[]{:S(2)}, u32[]{:S(2)}) collective-permute-start(bf16[784,512]{1,0:T(8,128)(2,1)} %get-tuple-element.53), channel_id=1, source_target_pairs={{0,4},{1,5},{2,6},{3,7},{4,0},{5,1},{6,2},{7,3},{8,12},{9,13},{10,... | collective-permute-start | bytes 2408456 | tf_op jit(solution)/shard_map/node_weight_pair/ppermute | solution.py:485
  48.5 33.4 %all-to-all-start.1 = ((bf16[32,16,512]{2,1,0:T(8,128)(2,1)}), bf16[32,16,512]{2,1,0:T(8,128)(2,1)S(1)}, u32[]{:S(2)}, u32[]{:S(2)}) async-start(bf16[32,16,512]{2,1,0:T(8,128)(2,1)} %bitcast.42), calls=%async_computation.1 | async-start | bytes 1048576 | tf_op jit(solution)/shard_map/halo_back/all_to_all | solution.py:520
  54.9 14.4 %collective-permute-start.2 = (bf16[464,512]{1,0:T(8,128)(2,1)S(1)}, bf16[464,512]{1,0:T(8,128)(2,1)S(1)}, u32[]{:S(2)}, u32[]{:S(2)}) collective-permute-start(bf16[464,512]{1,0:T(8,128)(2,1)S(1)} %get-tuple-element.54), channel_id=1, source_target_pairs={{0,1},{1,2},{2,3},{3,0},{4,5},{5,6},{6,7},{7,4},{8,9},{9,10},{10,1... | collective-permute-start | bytes 1425416 | tf_op jit(solution)/shard_map/weight_states/ppermute | solution.py:531
  56.6 24.1 %collective-permute-start.3 = (bf16[464,512]{1,0:T(8,128)(2,1)S(1)}, bf16[464,512]{1,0:T(8,128)(2,1)S(1)}, u32[]{:S(2)}, u32[]{:S(2)}) collective-permute-start(bf16[464,512]{1,0:T(8,128)(2,1)S(1)} %get-tuple-element.55), channel_id=1, source_target_pairs={{0,2},{1,3},{2,0},{3,1},{4,6},{5,7},{6,4},{7,5},{8,10},{9,11},{10,... | collective-permute-start | bytes 1425416 | tf_op jit(solution)/shard_map/weight_states/ppermute | solution.py:531
  59.5 21.2 %collective-permute-start.4 = (bf16[464,512]{1,0:T(8,128)(2,1)S(1)}, bf16[464,512]{1,0:T(8,128)(2,1)S(1)}, u32[]{:S(2)}, u32[]{:S(2)}) collective-permute-start(bf16[464,512]{1,0:T(8,128)(2,1)S(1)} %get-tuple-element.56), channel_id=1, source_target_pairs={{0,3},{1,0},{2,1},{3,2},{4,7},{5,4},{6,5},{7,6},{8,11},{9,8},{10,9... | collective-permute-start | bytes 1425416 | tf_op jit(solution)/shard_map/weight_states/ppermute | solution.py:531
  66.0 22.9 %copy-start.8 = (s32[1,32,16]{1,2,0:T(8,128)S(1)}, s32[1,32,16]{1,2,0:T(8,128)}, u32[]{:S(2)}) copy-start(s32[1,32,16]{1,2,0:T(8,128)} %param.21) | copy-start | bytes 6148
  81.9 18.0 %all-to-all-start.2 = ((bf16[16,32,512]{2,1,0:T(8,128)(2,1)}), bf16[16,32,512]{2,1,0:T(8,128)(2,1)S(1)}, u32[]{:S(2)}, u32[]{:S(2)}) async-start(bf16[16,32,512]{2,1,0:T(8,128)(2,1)} %merge.1), calls=%async_computation.2 | async-start | bytes 1048576 | tf_op jit(solution)/shard_map/chip_exchange/all_to_all | solution.py:550

commit v3 on v2

--- a/solution.py
+++ b/solution.py
@@ -12,7 +12,7 @@
 ALL = ("nodes", "batch")
 F32 = jnp.float32
 BF16 = jnp.bfloat16
-TILE = 512
+TILE = 1024
 EDGE_IN, EDGE_OUT = 48, 16
 SHARE_EDGE_IN, SHARE_EDGE_OUT, SHARE_NODE_IN, SHARE_NODE_OUT = 12, 4, 8, 4
 EDGE_BLOCK = EDGE_IN + EDGE_OUT
@@ -121,7 +121,6 @@
     table, aggregate, grads, small, part, halo, weight_ref, weight_out_ref,
     ordered_ref, npart_ref, nweight_ref, nweight_out_ref, ncot_ref, sems
 ):
-    step = pl.program_id(0)
     nodes, width = ordered_ref.shape
     slots = halo.shape[0]
     tiles, tile = part.shape[:2]
@@ -130,8 +129,7 @@
         return pltpu.make_async_copy(src, dst, sems.at[number])
 
     def part_fetch(number):
-        start = pl.multiple_of(number * tile, tile)
-        return fetch(number, part_hbm.at[pl.ds(start, tile), :], part.at[number])
+        return fetch(number, part_hbm.at[pl.ds(number * tile, tile), :], part.at[number])
 
     first = [
         fetch(tiles, halo_hbm, halo),
@@ -146,61 +144,61 @@
         fetch(tiles + 7, ncot_hbm, ncot_ref),
     ]
 
-    @pl.when(step == 0)
-    def _():
-        first[0].start()
-        first[1].start()
-        part_fetch(0).start()
-        first[2].start()
-        for number in range(1, tiles):
-            part_fetch(number).start()
-        for copy in late:
-            copy.start()
-        aggregate[...] = jnp.zeros_like(aggregate)
-        first[0].wait()
-        first[1].wait()
-        table[...] = nn(halo[...], weight_ref[...]).astype(BF16)
-        first[2].wait()
-
-    part_fetch(step).wait()
-    pre = part[step] + tn(pick_columns(rows_ref[0:1, :], slots, nodes), table[...])
-    act, slope = activate(pre)
-    act = act.astype(BF16)
-    act_ref[...] = act
-    slope_ref[...] = slope.astype(BF16)
-    normed, inv = layer_norm(nn(act, weight_out_ref[...]))
-    norm_ref[...] = normed.astype(BF16)
-    inv_ref[...] = inv
-    message = (normed * gain_ref[...]).astype(BF16)
-    aggregate[...] += nn(pick_columns(rows_ref[1:2, :], nodes), message)
-
-    @pl.when(step == pl.num_programs(0) - 1)
-    def _():
-        for copy in late:
-            copy.wait()
-        received = aggregate[...].astype(BF16)
-        node_act, node_slope = activate(npart_ref[...] + nn(received, nweight_ref[width:]))
-        node_act = node_act.astype(BF16)
-        node_norm, node_inv = layer_norm(nn(node_act, nweight_out_ref[...]))
-        cot = ncot_ref[...].astype(F32)
-        small[...] = jnp.zeros_like(small)
-        small[3:4] = jnp.sum(cot * node_norm, axis=0, keepdims=True)
-        grad_norm = norm_backward(cot * ngain_ref[...], node_norm, node_inv).astype(BF16)
-        grad_pre = (nt(grad_norm, nweight_out_ref[...]) * node_slope).astype(BF16)
-        small[2:3] = jnp.sum(grad_pre.astype(F32), axis=0, keepdims=True)
-        agg_grad_ref[...] = nt(grad_pre, nweight_ref[width:]).astype(BF16)
-        base_ref[...] = cot + nt(grad_pre, nweight_ref[:width])
-        received = nn(received, permutation(width, 8, SHARE_NODE_IN)).astype(BF16)
-        node_act = nn(node_act, permutation(width, 16, SHARE_NODE_OUT)).astype(BF16)
-        grads[0] = tn(ordered_ref[...], grad_pre).reshape(STATES, 2, 64, width)
-        grads[1] = tn(received, grad_pre).reshape(STATES, 2, 64, width)
-        grads[2] = tn(node_act, grad_norm).reshape(STATES, 2, 64, width)
-        for dst, side in ((send_ref, 1 - core_ref[0]), (keep_ref, core_ref[0])):
-            for state in range(STATES):
-                for kind in range(3):
-                    row = state * SHARE_NODE + kind * 64
-                    dst[row : row + 64, :] = grads[kind, state, side].astype(BF16)
-            dst[STATES * SHARE_NODE :, :] = small[...].astype(BF16)
+    first[0].start()
+    first[1].start()
+    part_fetch(0).start()
+    first[2].start()
+    for number in range(1, tiles):
+        part_fetch(number).start()
+    for copy in late:
+        copy.start()
+    first[0].wait()
+    first[1].wait()
+    table[...] = nn(halo[...], weight_ref[...]).astype(BF16)
+    for step in range(tiles):
+        rows = slice(step * tile, (step + 1) * tile)
+        part_fetch(step).wait()
+        pre = part[step] + tn(pick_columns(rows_ref[0:1, rows], slots, nodes), table[...])
+        act, slope = activate(pre)
+        act = act.astype(BF16)
+        act_ref[rows, :] = act
+        slope_ref[rows, :] = slope.astype(BF16)
+        if step == 0:
+            first[2].wait()
+        normed, inv = layer_norm(nn(act, weight_out_ref[...]))
+        norm_ref[rows, :] = normed.astype(BF16)
+        inv_ref[rows, :] = inv
+        message = (normed * gain_ref[...]).astype(BF16)
+        added = nn(pick_columns(rows_ref[1:2, rows], nodes), message)
+        if step == 0:
+            aggregate[...] = added
+        else:
+            aggregate[...] += added
+    for copy in late:
+        copy.wait()
+    received = aggregate[...].astype(BF16)
+    node_act, node_slope = activate(npart_ref[...] + nn(received, nweight_ref[width:]))
+    node_act = node_act.astype(BF16)
+    node_norm, node_inv = layer_norm(nn(node_act, nweight_out_ref[...]))
+    cot = ncot_ref[...].astype(F32)
+    small[...] = jnp.zeros_like(small)
+    small[3:4] = jnp.sum(cot * node_norm, axis=0, keepdims=True)
+    grad_norm = norm_backward(cot * ngain_ref[...], node_norm, node_inv).astype(BF16)
+    grad_pre = (nt(grad_norm, nweight_out_ref[...]) * node_slope).astype(BF16)
+    small[2:3] = jnp.sum(grad_pre.astype(F32), axis=0, keepdims=True)
+    agg_grad_ref[...] = nt(grad_pre, nweight_ref[width:]).astype(BF16)
+    base_ref[...] = cot + nt(grad_pre, nweight_ref[:width])
+    received = nn(received, permutation(width, 8, SHARE_NODE_IN)).astype(BF16)
+    node_act = nn(node_act, permutation(width, 16, SHARE_NODE_OUT)).astype(BF16)
+    grads[0] = tn(ordered_ref[...], grad_pre).reshape(STATES, 2, 64, width)
+    grads[1] = tn(received, grad_pre).reshape(STATES, 2, 64, width)
+    grads[2] = tn(node_act, grad_norm).reshape(STATES, 2, 64, width)
+    for dst, side in ((send_ref, 1 - core_ref[0]), (keep_ref, core_ref[0])):
+        for state in range(STATES):
+            for kind in range(3):
+                row = state * SHARE_NODE + kind * 64
+                dst[row : row + 64, :] = grads[kind, state, side].astype(BF16)
+        dst[STATES * SHARE_NODE :, :] = small[...].astype(BF16)
 
 
 def backward_kernel(
@@ -209,7 +207,6 @@
     pre_grad_hbm, send_ref, keep_ref, sums_ref, terms_ref,
     grad_in, grad_out, sums, small, halo_ref, weight_ref, held, sems
 ):
-    step = pl.program_id(0)
     nodes, width = hidden_ref.shape
     slots = halo_ref.shape[0]
     tiles, tile = held.shape[:2]
@@ -219,65 +216,67 @@
     )
 
     def push(number):
-        start = pl.multiple_of(number * tile, tile)
         return pltpu.make_async_copy(
-            held.at[number], pre_grad_hbm.at[pl.ds(start, tile), :], sems.at[number]
+            held.at[number], pre_grad_hbm.at[pl.ds(number * tile, tile), :], sems.at[number]
         )
 
-    @pl.when(step == 0)
-    def _():
-        halo_fetch.start()
-        weight_fetch.start()
-        grad_in[...] = jnp.zeros_like(grad_in)
-        grad_out[...] = jnp.zeros_like(grad_out)
-        sums[...] = jnp.zeros_like(sums)
-        small[...] = jnp.zeros_like(small)
-
-    receivers = pick_columns(rows_ref[1:2, :], nodes)
-    message_grad = ecot_ref[...].astype(F32) + tn(receivers, agg_grad_ref[...])
-    normed = norm_ref[...].astype(F32)
-    small[1:2] += jnp.sum(message_grad * normed, axis=0, keepdims=True)
-    grad_norm = norm_backward(message_grad * gain_ref[...], normed, inv_ref[...]).astype(BF16)
-    grad_pre = nt(grad_norm, weight_out_ref[...]) * slope_ref[...].astype(F32)
-    grad_pre = grad_pre.astype(BF16)
-    held[step] = grad_pre
-    push(step).start()
-    small[0:1] += jnp.sum(grad_pre.astype(F32), axis=0, keepdims=True)
-    grad_out[...] += tn(act_ref[...], grad_norm)
-    grad_in[:width] += tn(edge_ref[...], grad_pre)
-    sums[: nodes + slots] += nn(pick_columns(rows_ref[0:1, :], nodes + slots), grad_pre)
-    sums[nodes + slots :] += nn(receivers, grad_pre)
-
-    @pl.when(step == pl.num_programs(0) - 1)
-    def _():
-        halo_fetch.wait()
-        weight_fetch.wait()
-        own = sums[:nodes].astype(BF16)
-        remote = sums[nodes : nodes + slots].astype(BF16)
-        received = sums[nodes + slots :].astype(BF16)
-        sums_ref[:nodes] = own
-        sums_ref[nodes:] = received
-        terms_ref[...] = nt(remote, weight_ref[...]).astype(BF16)
-        hidden = hidden_ref[...]
-        grad_in[width : 2 * width] = tn(hidden, own) + tn(halo_ref[...], remote)
-        grad_in[2 * width :] = tn(hidden, received)
-        core = core_ref[0]
-        for dst, side in ((send_ref, 1 - core), (keep_ref, core)):
-
-            def pack(chip, carry):
-                piece = chip * 2 + side
-                row = pl.multiple_of(chip * EDGE_BLOCK, EDGE_BLOCK)
-                start = pl.multiple_of(piece * EDGE_IN, EDGE_IN)
-                dst[pl.ds(row, EDGE_IN), :] = grad_in[pl.ds(start, EDGE_IN), :].astype(BF16)
-                row = pl.multiple_of(row + EDGE_IN, EDGE_OUT)
-                start = pl.multiple_of(piece * EDGE_OUT, EDGE_OUT)
-                dst[pl.ds(row, EDGE_OUT), :] = grad_out[pl.ds(start, EDGE_OUT), :].astype(BF16)
-                return carry
-
-            lax.fori_loop(0, 16, pack, 0, unroll=4)
-            dst[16 * EDGE_BLOCK :, :] = small[...].astype(BF16)
-        for number in range(tiles):
-            push(number).wait()
+    halo_fetch.start()
+    weight_fetch.start()
+    small[...] = jnp.zeros_like(small)
+    for step in range(tiles):
+        rows = slice(step * tile, (step + 1) * tile)
+
+        def add(ref, place, value):
+            if step == 0:
+                ref[place] = value
+            else:
+                ref[place] += value
+
+        receivers = pick_columns(rows_ref[1:2, rows], nodes)
+        message_grad = ecot_ref[rows, :].astype(F32) + tn(receivers, agg_grad_ref[...])
+        normed = norm_ref[rows, :].astype(F32)
+        small[1:2] += jnp.sum(message_grad * normed, axis=0, keepdims=True)
+        grad_norm = norm_backward(
+            message_grad * gain_ref[...], normed, inv_ref[rows, :]
+        ).astype(BF16)
+        grad_pre = nt(grad_norm, weight_out_ref[...]) * slope_ref[rows, :].astype(F32)
+        grad_pre = grad_pre.astype(BF16)
+        held[step] = grad_pre
+        push(step).start()
+        small[0:1] += jnp.sum(grad_pre.astype(F32), axis=0, keepdims=True)
+        add(grad_out, slice(None), tn(act_ref[rows, :], grad_norm))
+        add(grad_in, slice(0, width), tn(edge_ref[rows, :], grad_pre))
+        senders = pick_columns(rows_ref[0:1, rows], nodes + slots)
+        add(sums, slice(0, nodes + slots), nn(senders, grad_pre))
+        add(sums, slice(nodes + slots, None), nn(receivers, grad_pre))
+    halo_fetch.wait()
+    weight_fetch.wait()
+    own = sums[:nodes].astype(BF16)
+    remote = sums[nodes : nodes + slots].astype(BF16)
+    received = sums[nodes + slots :].astype(BF16)
+    sums_ref[:nodes] = own
+    sums_ref[nodes:] = received
+    terms_ref[...] = nt(remote, weight_ref[...]).astype(BF16)
+    hidden = hidden_ref[...]
+    grad_in[width : 2 * width] = tn(hidden, own) + tn(halo_ref[...], remote)
+    grad_in[2 * width :] = tn(hidden, received)
+    core = core_ref[0]
+    for dst, side in ((send_ref, 1 - core), (keep_ref, core)):
+
+        def pack(chip, carry):
+            piece = chip * 2 + side
+            row = pl.multiple_of(chip * EDGE_BLOCK, EDGE_BLOCK)
+            start = pl.multiple_of(piece * EDGE_IN, EDGE_IN)
+            dst[pl.ds(row, EDGE_IN), :] = grad_in[pl.ds(start, EDGE_IN), :].astype(BF16)
+            row = pl.multiple_of(row + EDGE_IN, EDGE_OUT)
+            start = pl.multiple_of(piece * EDGE_OUT, EDGE_OUT)
+            dst[pl.ds(row, EDGE_OUT), :] = grad_out[pl.ds(start, EDGE_OUT), :].astype(BF16)
+            return carry
+
+        lax.fori_loop(0, 16, pack, 0, unroll=4)
+        dst[16 * EDGE_BLOCK :, :] = small[...].astype(BF16)
+    for number in range(tiles):
+        push(number).wait()
 
 
 def pair_kernel(
@@ -359,6 +358,8 @@
         args = dict(grid=grid, in_specs=in_specs, out_specs=out_specs)
     elif in_specs is not None:
         args = dict(in_specs=in_specs)
+        if out_specs is not None:
+            args["out_specs"] = tuple(out_specs)
     return pl.pallas_call(
         body,
         out_shape=outs,
@@ -459,10 +460,9 @@
                 shape(edges, 1, dtype=F32), far(nodes, width, dtype=F32), shape(nodes, width),
                 node_pair, far(*node_pair.shape),
             ),
-            grid,
-            [SCALAR, rows_tile, full(1, width), full(1, width)] + [FAR] * 9,
-            (edge_tile, edge_tile, edge_tile, tiled(tile, 1), node_full, node_full)
-            + (full(*node_pair.shape),) * 2,
+            None,
+            [SCALAR, WHOLE, WHOLE, WHOLE] + [FAR] * 9,
+            None,
             [
                 pltpu.VMEM((slots, width), BF16), pltpu.VMEM((nodes, width), F32),
                 pltpu.VMEM((3, STATES, 2, 64, width), F32), pltpu.VMEM((SMALL, width), F32),
@@ -491,16 +491,9 @@
                 far(edges, width), edge_pair, far(*edge_pair.shape), far(2 * nodes, width),
                 far(slots, width),
             ),
-            grid,
-            [
-                SCALAR, edge_tile, rows_tile, edge_tile, edge_tile, edge_tile,
-                tiled(tile, 1), edge_tile, node_full, full(1, width), full(width, width),
-                node_full, FAR, FAR,
-            ],
-            (
-                FAR, full(*edge_pair.shape), full(*edge_pair.shape),
-                full(2 * nodes, width), full(slots, width),
-            ),
+            None,
+            [SCALAR] + [WHOLE] * 11 + [FAR, FAR],
+            [FAR] + [WHOLE] * 4,
             [
                 pltpu.VMEM((3 * width, width), F32), pltpu.VMEM((width, width), F32),
                 pltpu.VMEM((2 * nodes + slots, width), F32), pltpu.VMEM((SMALL, width), F32),

time: 102 us -> 99.4 us (0.975)
  Pallas kernels: 45.8 us -> 42.2 us
  waiting for transfers between devices: 25.7 us -> 27.2 us
    pallas_call x1, Pallas kernels: 12.5 us -> 11.3 us  [shards(): call(backward_kernel, (far(edges, width), edge_pair, far(*edge_pair.shape...]
  transfers between devices with their start and end apart: 8 -> 8, of which waited for: 4 -> 4; matrix products, arithmetic and copies ran while one was open for 1% -> 2% of each run, Pallas kernels for 19% -> 17%
where the time goes in v3:
time: 99.4 us; the launch traced here: 98.9 us
  Pallas kernels  42.2 us (42%)
  waiting for transfers between devices  27.2 us (27%)
  starting transfers between devices  25.7 us (26%)
  local copies, waits for them, and re-layouts  1.6 us (2%)
  other arithmetic  1.34 us (1%)
    ppermute x3, waiting for transfers between devices, shards(): lax.ppermute(item, ALL, perm)  15.6 us
    pallas_call x1, Pallas kernels, shards(): call(backward_kernel, (far(edges, width), edge_pair, far(*edge_pair.shape...  11.3 us
    pallas_call x1, Pallas kernels, shards(): call(forward_kernel, (shape(edges, width), shape(edges, width), shape(edg...  10.8 us
    all_to_all x1, starting transfers between devices, shards(): lax.all_to_all(outgoing.reshape(parts, -1, width), 'nodes', 0, 0, tiled=T...  8.25 us
    all_to_all x1, waiting for transfers between devices, shards(): lax.all_to_all(sent, 'nodes', 0, 0, tiled=True, axis_index_groups=groups)  7.87 us
    all_to_all x1, starting transfers between devices, shards(): lax.all_to_all(sent, 'nodes', 0, 0, tiled=True, axis_index_groups=groups)  7.08 us
    pallas_call x1, Pallas kernels, shards(): call(local_kernel, (far(edges, width, dtype=F32), far(nodes, width, dtype...  6.64 us
    ppermute x3, starting transfers between devices, shards(): lax.ppermute(item, ALL, perm)  5.86 us
  transfers between devices with their start and end apart: 8, of which 4 were waited for; matrix products, arithmetic and copies ran while one was open for 2% of the time, Pallas kernels for 17%

profile of v3, /device:TPU:0, one launch (start us, length us, event | category | flops | bytes accessed | tf_op | source)
XLA Modules:
  0.0 98.9 jit_solution(3700262783387897938)
XLA Ops:
  0.6 2.3 %halo_rows.1 = bf16[512,512]{1,0:T(8,128)(2,1)} custom-call(s32[16,32]{1,0:T(8,128)} %bitcast.46, bf16[256,512]{1,0:T(8,128)(2,1)} %bitcast.32), custom_call_target="tpu_custom_call" | custom-call | tf_op jit(solution)/shard_map/halo_rows/pallas_call | solution.py:433
  2.9 8.3 %all-to-all-start = ((bf16[32,16,512]{2,1,0:T(8,128)(2,1)}), bf16[32,16,512]{2,1,0:T(8,128)(2,1)S(1)}, u32[]{:S(2)}, u32[]{:S(2)}) async-start(bf16[32,16,512]{2,1,0:T(8,128)(2,1)} %bitcast.40), calls=%async_computation | async-start | bytes 1048576 | tf_op jit(solution)/shard_map/halo_rows/all_to_all | solution.py:434
  11.2 1.3 %pad_add_fusion.rows_ref = s32[2,2048]{1,0:T(2,128)} fusion(s32[1,2048]{1,0:T(1,128)} %bitcast.47, s32[1,2048]{1,0:T(1,128)} %bitcast.48), kind=kLoop, calls=%fused_computation | loop fusion | flops 4096 | bytes 32768 | tf_op jit(solution)/shard_map/stack | solution.py:423
  12.5 0.0 copy-start.2
  12.5 0.0 copy-start.5
  12.5 0.0 copy-start.6
  12.5 6.6 %edge_pre_local.1 = (f32[2048,512]{1,0:T(8,128)}, f32[256,512]{1,0:T(8,128)}, bf16[256,512]{1,0:T(8,128)(2,1)}) custom-call(bf16[2048,512]{1,0:T(8,128)(2,1)} %bitcast.35, s32[2,2048]{1,0:T(2,128)} %pad_add_fusion.rows_ref, bf16[256,512]{1,0:T(8,128)(2,1)} %bitcast.33, bf16[1536,512]{1,0:T(8,128)(2,1)} %weight_ref.5, f32[1,512]{1,0:T(1,128)} %bitcast.50, ...), custom_call_target="tpu_custom_call" | custom-call | flops 2147483648 | bytes 6291456 | tf_op jit(solution)/shard_map/edge_pre_local/pallas_call | solution.py:442
  19.1 3.8 %all-to-all-done = bf16[32,16,512]{2,1,0:T(8,128)(2,1)S(1)} async-done(((bf16[32,16,512]{2,1,0:T(8,128)(2,1)}), bf16[32,16,512]{2,1,0:T(8,128)(2,1)S(1)}, u32[]{:S(2)}, u32[]{:S(2)}) %all-to-all-start) | async-done | bytes 524320 | tf_op jit(solution)/shard_map/halo_rows/all_to_all | solution.py:434
  22.9 0.0 copy-start.7
  22.9 0.8 copy-done.7
  23.7 0.0 copy-done.2
  23.7 0.0 copy-done.5
  23.7 0.0 copy-done.6
  23.7 0.0 copy-start
  23.7 0.0 copy-start.1
  23.7 0.0 copy-start.3
  23.8 0.0 copy-start.4
  23.8 10.8 %forward.1 = (bf16[2048,512]{1,0:T(8,128)(2,1)S(1)}, bf16[2048,512]{1,0:T(8,128)(2,1)S(1)}, bf16[2048,512]{1,0:T(8,128)(2,1)S(1)}, f32[2048,1]{1,0:T(8,128)S(1)}...) custom-call(s32[1]{0:T(128)} %bitcast.core_ref, ...), custom_call_target="tpu_custom_call" | custom-call | flops 3221225472 | bytes 12582912 | tf_op jit(solution)/shard_map/forward/pallas_call | solution.py:456
  34.6 0.0 copy-done
  34.6 0.0 copy-done.1
  34.6 0.0 copy-done.3
  34.6 0.0 copy-done.4
  34.6 11.3 %backward.1 = (bf16[2048,512]{1,0:T(8,128)(2,1)}, bf16[1040,512]{1,0:T(8,128)(2,1)}, bf16[1040,512]{1,0:T(8,128)(2,1)}, bf16[512,512]{1,0:T(8,128)(2,1)}, bf16[512,512]{1,0:T(8,128)(2,1)}) custom-call(s32[1]{0:T(128)} %bitcast.core_ref, bf16[2048,512]{1,0:T(8,128)(2,1)S(1)} %bitcast.31, s32[2,2048]{1,0:T(2,128)S(1)} %copy-done.2, ...), custom_call_target="tpu_custom_call" | custom-call | flops 6442450944 | bytes 14680064 | tf_op jit(solution)/shard_map/backward/pallas_call | solution.py:488
  45.9 0.1 collective-permute-start
  46.1 0.4 collective-permute-start.1
  46.5 3.9 %all-to-all-start.1 = ((bf16[32,16,512]{2,1,0:T(8,128)(2,1)}), bf16[32,16,512]{2,1,0:T(8,128)(2,1)S(1)}, u32[]{:S(2)}, u32[]{:S(2)}) async-start(bf16[32,16,512]{2,1,0:T(8,128)(2,1)} %bitcast.42), calls=%async_computation.1 | async-start | bytes 1048576 | tf_op jit(solution)/shard_map/halo_back/all_to_all | solution.py:513
  50.4 0.0 collective-permute-done.1.nrecv_ref
  50.4 0.0 collective-permute-done.recv_ref
  50.5 2.1 %pair_sum.1 = (bf16[464,512]{1,0:T(8,128)(2,1)S(1)}, bf16[464,512]{1,0:T(8,128)(2,1)S(1)}, bf16[464,512]{1,0:T(8,128)(2,1)S(1)}, bf16[464,512]{1,0:T(8,128)(2,1)S(1)}) custom-call(s32[1]{0:T(128)} %bitcast.18.batch_ref, bf16[1040,512]{1,0:T(8,128)(2,1)} %get-tuple-element.50.keep_ref, bf16[1040,512]{1,0:T(8,128)(2,1)S(1)} %collective-permute-done.recv_ref, ...), custom_call_target="tpu_custom_call" | custom-call | bytes 8388608 | tf_op jit(solution)/shard_map/pair_sum/pallas_call | solution.py:518
  52.6 1.6 %collective-permute-start.2 = (bf16[464,512]{1,0:T(8,128)(2,1)S(1)}, bf16[464,512]{1,0:T(8,128)(2,1)S(1)}, u32[]{:S(2)}, u32[]{:S(2)}) collective-permute-start(bf16[464,512]{1,0:T(8,128)(2,1)S(1)} %get-tuple-element.54), channel_id=1, source_target_pairs={{0,1},{1,2},{2,3},{3,0},{4,5},{5,6},{6,7},{7,4},{8,9},{9,10},{10,1... | collective-permute-start | bytes 1425416 | tf_op jit(solution)/shard_map/weight_states/ppermute | solution.py:524
  54.2 2.9 %collective-permute-start.3 = (bf16[464,512]{1,0:T(8,128)(2,1)S(1)}, bf16[464,512]{1,0:T(8,128)(2,1)S(1)}, u32[]{:S(2)}, u32[]{:S(2)}) collective-permute-start(bf16[464,512]{1,0:T(8,128)(2,1)S(1)} %get-tuple-element.55), channel_id=1, source_target_pairs={{0,2},{1,3},{2,0},{3,1},{4,6},{5,7},{6,4},{7,5},{8,10},{9,11},{10,... | collective-permute-start | bytes 1425416 | tf_op jit(solution)/shard_map/weight_states/ppermute | solution.py:524
  57.1 1.3 %collective-permute-start.4 = (bf16[464,512]{1,0:T(8,128)(2,1)S(1)}, bf16[464,512]{1,0:T(8,128)(2,1)S(1)}, u32[]{:S(2)}, u32[]{:S(2)}) collective-permute-start(bf16[464,512]{1,0:T(8,128)(2,1)S(1)} %get-tuple-element.56), channel_id=1, source_target_pairs={{0,3},{1,0},{2,1},{3,2},{4,7},{5,4},{6,5},{7,6},{8,11},{9,8},{10,9... | collective-permute-start | bytes 1425416 | tf_op jit(solution)/shard_map/weight_states/ppermute | solution.py:524
  58.5 4.1 %grad_edges.1 = bf16[2048,512]{1,0:T(8,128)(2,1)} custom-call(bf16[2048,512]{1,0:T(8,128)(2,1)} %bitcast.30, bf16[2048,512]{1,0:T(8,128)(2,1)} %get-tuple-element.57.pre_grad_ref, bf16[1536,512]{1,0:T(8,128)(2,1)} %weight_ref.5), custom_call_target="tpu_custom_call" | custom-call | flops 1073741824 | bytes 6291456 | tf_op jit(solution)/shard_map/grad_edges/pallas_call | solution.py:526
  62.6 0.0 copy-start.8
  62.6 4.2 %collective-permute-done.2.one_ref = bf16[464,512]{1,0:T(8,128)(2,1)S(1)} collective-permute-done((bf16[464,512]{1,0:T(8,128)(2,1)S(1)}, bf16[464,512]{1,0:T(8,128)(2,1)S(1)}, u32[]{:S(2)}, u32[]{:S(2)}) %collective-permute-start.2) | collective-permute-done | bytes 475168 | tf_op jit(solution)/shard_map/weight_states/ppermute | solution.py:524
  66.8 11.4 %collective-permute-done.3.two_ref = bf16[464,512]{1,0:T(8,128)(2,1)S(1)} collective-permute-done((bf16[464,512]{1,0:T(8,128)(2,1)S(1)}, bf16[464,512]{1,0:T(8,128)(2,1)S(1)}, u32[]{:S(2)}, u32[]{:S(2)}) %collective-permute-start.3) | collective-permute-done | bytes 475168 | tf_op jit(solution)/shard_map/weight_states/ppermute | solution.py:524
  78.2 0.0 collective-permute-done.4.three_ref
  78.2 1.2 %merge.1 = bf16[16,32,512]{2,1,0:T(8,128)(2,1)} custom-call(bf16[464,512]{1,0:T(8,128)(2,1)S(1)} %get-tuple-element.59.mine_ref, bf16[464,512]{1,0:T(8,128)(2,1)S(1)} %collective-permute-done.2.one_ref, bf16[464,512]{1,0:T(8,128)(2,1)S(1)} %collective-permute-done.3.two_ref, bf16[464,512]{1,0:T(8,128)(2,1)S(1)} %collective-permute-done.4.three_ref), custom_call_target="tpu_custom_call" | custom-call | tf_op jit(solution)/shard_map/merge/pallas_call | solution.py:536
  79.5 0.0 all-to-all-done.1
  79.5 7.1 %all-to-all-start.2 = ((bf16[16,32,512]{2,1,0:T(8,128)(2,1)}), bf16[16,32,512]{2,1,0:T(8,128)(2,1)S(1)}, u32[]{:S(2)}, u32[]{:S(2)}) async-start(bf16[16,32,512]{2,1,0:T(8,128)(2,1)} %merge.1), calls=%async_computation.2 | async-start | bytes 1048576 | tf_op jit(solution)/shard_map/chip_exchange/all_to_all | solution.py:543
  86.6 0.0 copy-done.8
  86.6 0.1 copy.26
  86.6 0.1 reshape.63.rows_ref
  86.7 3.0 %grad_nodes.1 = bf16[256,512]{1,0:T(8,128)(2,1)} custom-call(bf16[512,512]{1,0:T(8,128)(2,1)S(1)} %bitcast.29, s32[1,512]{1,0:T(1,128)S(1)} %reshape.63.rows_ref, bf16[512,512]{1,0:T(8,128)(2,1)} %get-tuple-element.48.sums_ref, bf16[1536,512]{1,0:T(8,128)(2,1)} %weight_ref.5, f32[256,512]{1,0:T(8,128)} %get-tuple-element.49.base_ref), custom_call_target="tpu_custom_call" | custom-call | tf_op jit(solution)/shard_map/grad_nodes/pallas_call | solution.py:545
  89.7 7.9 %all-to-all-done.2.arrived_ref = bf16[16,32,512]{2,1,0:T(8,128)(2,1)S(1)} async-done(((bf16[16,32,512]{2,1,0:T(8,128)(2,1)}), bf16[16,32,512]{2,1,0:T(8,128)(2,1)S(1)}, u32[]{:S(2)}, u32[]{:S(2)}) %all-to-all-start.2) | async-done | bytes 524320 | tf_op jit(solution)/shard_map/chip_exchange/all_to_all | solution.py:543
  97.6 0.7 weight_grads.1
  98.3 0.1 constant_dynamic-slice_fusion
  98.3 0.5 slice_bitcast_fusion
Async XLA Ops:
  2.9 20.0 %all-to-all-start = ((bf16[32,16,512]{2,1,0:T(8,128)(2,1)}), bf16[32,16,512]{2,1,0:T(8,128)(2,1)S(1)}, u32[]{:S(2)}, u32[]{:S(2)}) async-start(bf16[32,16,512]{2,1,0:T(8,128)(2,1)} %bitcast.40), calls=%async_computation | async-start | bytes 1048576 | tf_op jit(solution)/shard_map/halo_rows/all_to_all | solution.py:434
  12.5 11.2 %copy-start.2 = (s32[2,2048]{1,0:T(2,128)S(1)}, s32[2,2048]{1,0:T(2,128)}, u32[]{:S(2)}) copy-start(s32[2,2048]{1,0:T(2,128)} %pad_add_fusion.rows_ref) | copy-start | bytes 49156
  12.5 11.2 %copy-start.5 = (f32[512]{0:T(512)S(1)}, f32[512]{0:T(512)}, u32[]{:S(2)}) copy-start(f32[512]{0:T(512)} %param.29) | copy-start | bytes 6148
  12.5 11.2 %copy-start.6 = (f32[512]{0:T(512)S(1)}, f32[512]{0:T(512)}, u32[]{:S(2)}) copy-start(f32[512]{0:T(512)} %param.25) | copy-start | bytes 6148
  22.9 0.8 copy-start.7
  23.7 10.9 %copy-start = (bf16[1,2048,512]{2,1,0:T(8,128)(2,1)S(1)}, bf16[1,2048,512]{2,1,0:T(8,128)(2,1)}, u32[]{:S(2)}) copy-start(bf16[1,2048,512]{2,1,0:T(8,128)(2,1)} %param.18) | copy-start | bytes 6291460
  23.7 10.9 %copy-start.1 = (bf16[1,256,512]{2,1,0:T(8,128)(2,1)S(1)}, bf16[1,256,512]{2,1,0:T(8,128)(2,1)}, u32[]{:S(2)}) copy-start(bf16[1,256,512]{2,1,0:T(8,128)(2,1)} %param.15) | copy-start | bytes 786436
  23.7 10.9 %copy-start.3 = (bf16[1,2048,512]{2,1,0:T(8,128)(2,1)S(1)}, bf16[1,2048,512]{2,1,0:T(8,128)(2,1)}, u32[]{:S(2)}) copy-start(bf16[1,2048,512]{2,1,0:T(8,128)(2,1)} %param.16) | copy-start | bytes 6291460
  23.8 10.9 %copy-start.4 = (bf16[512,512]{1,0:T(8,128)(2,1)S(1)}, bf16[512,512]{1,0:T(8,128)(2,1)}, u32[]{:S(2)}) copy-start(bf16[512,512]{1,0:T(8,128)(2,1)} %weight_out_ref.1) | copy-start | bytes 1572868
  45.9 4.5 %collective-permute-start = (bf16[1040,512]{1,0:T(8,128)(2,1)}, bf16[1040,512]{1,0:T(8,128)(2,1)S(1)}, u32[]{:S(2)}, u32[]{:S(2)}) collective-permute-start(bf16[1040,512]{1,0:T(8,128)(2,1)} %get-tuple-element.51), channel_id=1, source_target_pairs={{0,4},{1,5},{2,6},{3,7},{4,0},{5,1},{6,2},{7,3},{8,12},{9,13},{10,... | collective-permute-start | bytes 3194888 | tf_op jit(solution)/shard_map/edge_weight_pair/ppermute | solution.py:511
  46.1 4.3 %collective-permute-start.1 = (bf16[784,512]{1,0:T(8,128)(2,1)}, bf16[784,512]{1,0:T(8,128)(2,1)S(1)}, u32[]{:S(2)}, u32[]{:S(2)}) collective-permute-start(bf16[784,512]{1,0:T(8,128)(2,1)} %get-tuple-element.53), channel_id=1, source_target_pairs={{0,4},{1,5},{2,6},{3,7},{4,0},{5,1},{6,2},{7,3},{8,12},{9,13},{10,... | collective-permute-start | bytes 2408456 | tf_op jit(solution)/shard_map/node_weight_pair/ppermute | solution.py:485
  46.5 32.9 %all-to-all-start.1 = ((bf16[32,16,512]{2,1,0:T(8,128)(2,1)}), bf16[32,16,512]{2,1,0:T(8,128)(2,1)S(1)}, u32[]{:S(2)}, u32[]{:S(2)}) async-start(bf16[32,16,512]{2,1,0:T(8,128)(2,1)} %bitcast.42), calls=%async_computation.1 | async-start | bytes 1048576 | tf_op jit(solution)/shard_map/halo_back/all_to_all | solution.py:513
  52.6 14.2 %collective-permute-start.2 = (bf16[464,512]{1,0:T(8,128)(2,1)S(1)}, bf16[464,512]{1,0:T(8,128)(2,1)S(1)}, u32[]{:S(2)}, u32[]{:S(2)}) collective-permute-start(bf16[464,512]{1,0:T(8,128)(2,1)S(1)} %get-tuple-element.54), channel_id=1, source_target_pairs={{0,1},{1,2},{2,3},{3,0},{4,5},{5,6},{6,7},{7,4},{8,9},{9,10},{10,1... | collective-permute-start | bytes 1425416 | tf_op jit(solution)/shard_map/weight_states/ppermute | solution.py:524
  54.2 24.0 %collective-permute-start.3 = (bf16[464,512]{1,0:T(8,128)(2,1)S(1)}, bf16[464,512]{1,0:T(8,128)(2,1)S(1)}, u32[]{:S(2)}, u32[]{:S(2)}) collective-permute-start(bf16[464,512]{1,0:T(8,128)(2,1)S(1)} %get-tuple-element.55), channel_id=1, source_target_pairs={{0,2},{1,3},{2,0},{3,1},{4,6},{5,7},{6,4},{7,5},{8,10},{9,11},{10,... | collective-permute-start | bytes 1425416 | tf_op jit(solution)/shard_map/weight_states/ppermute | solution.py:524
  57.1 21.1 %collective-permute-start.4 = (bf16[464,512]{1,0:T(8,128)(2,1)S(1)}, bf16[464,512]{1,0:T(8,128)(2,1)S(1)}, u32[]{:S(2)}, u32[]{:S(2)}) collective-permute-start(bf16[464,512]{1,0:T(8,128)(2,1)S(1)} %get-tuple-element.56), channel_id=1, source_target_pairs={{0,3},{1,0},{2,1},{3,2},{4,7},{5,4},{6,5},{7,6},{8,11},{9,8},{10,9... | collective-permute-start | bytes 1425416 | tf_op jit(solution)/shard_map/weight_states/ppermute | solution.py:524
  62.6 23.9 %copy-start.8 = (s32[1,32,16]{1,2,0:T(8,128)S(1)}, s32[1,32,16]{1,2,0:T(8,128)}, u32[]{:S(2)}) copy-start(s32[1,32,16]{1,2,0:T(8,128)} %param.21) | copy-start | bytes 6148
  79.5 18.1 %all-to-all-start.2 = ((bf16[16,32,512]{2,1,0:T(8,128)(2,1)}), bf16[16,32,512]{2,1,0:T(8,128)(2,1)S(1)}, u32[]{:S(2)}, u32[]{:S(2)}) async-start(bf16[16,32,512]{2,1,0:T(8,128)(2,1)} %merge.1), calls=%async_computation.2 | async-start | bytes 1048576 | tf_op jit(solution)/shard_map/chip_exchange/all_to_all | solution.py:543

commit v4 on v3

--- a/solution.py
+++ b/solution.py
@@ -117,7 +117,7 @@
 def forward_kernel(
     core_ref, rows_ref, gain_ref, ngain_ref, part_hbm, halo_hbm, weight_hbm, weight_out_hbm,
     ordered_hbm, npart_hbm, nweight_hbm, nweight_out_hbm, ncot_hbm,
-    act_ref, slope_ref, norm_ref, inv_ref, base_ref, agg_grad_ref, send_ref, keep_ref,
+    act_ref, slope_ref, norm_ref, inv_ref, grad_pre_ref, agg_grad_ref, send_ref, keep_ref,
     table, aggregate, grads, small, part, halo, weight_ref, weight_out_ref,
     ordered_ref, npart_ref, nweight_ref, nweight_out_ref, ncot_ref, sems
 ):
@@ -187,7 +187,7 @@
     grad_pre = (nt(grad_norm, nweight_out_ref[...]) * node_slope).astype(BF16)
     small[2:3] = jnp.sum(grad_pre.astype(F32), axis=0, keepdims=True)
     agg_grad_ref[...] = nt(grad_pre, nweight_ref[width:]).astype(BF16)
-    base_ref[...] = cot + nt(grad_pre, nweight_ref[:width])
+    grad_pre_ref[...] = grad_pre
     received = nn(received, permutation(width, 8, SHARE_NODE_IN)).astype(BF16)
     node_act = nn(node_act, permutation(width, 16, SHARE_NODE_OUT)).astype(BF16)
     grads[0] = tn(ordered_ref[...], grad_pre).reshape(STATES, 2, 64, width)
@@ -332,11 +332,14 @@
     ).astype(BF16)
 
 
-def nodes_kernel(halo_ref, rows_ref, sums_ref, weight_ref, base_ref, out_ref):
-    nodes, width = base_ref.shape
+def nodes_kernel(
+    halo_ref, rows_ref, sums_ref, weight_ref, grad_pre_ref, nweight_ref, cot_ref, out_ref
+):
+    nodes, width = cot_ref.shape
     picks = pick_columns(rows_ref[...], nodes)
     out_ref[...] = (
-        base_ref[...]
+        cot_ref[...].astype(F32)
+        + nt(grad_pre_ref[...], nweight_ref[...])
         + nt(sums_ref[:nodes], weight_ref[width : 2 * width])
         + nt(sums_ref[nodes:], weight_ref[2 * width :])
         + nn(picks, halo_ref[...])
@@ -430,7 +433,9 @@
     ]
 
     with jax.named_scope("halo_rows"):
-        outgoing = call(gather_kernel, shape(slots, width))(send_rows[0].T, hidden)
+        outgoing = call(gather_kernel, shape(slots, width), limit=VMEM_FEW)(
+            *keep_far(send_rows[0].T, hidden)
+        )
         halo = lax.all_to_all(
             outgoing.reshape(parts, -1, width), "nodes", 0, 0, tiled=True
         ).reshape(slots, width)
@@ -453,11 +458,11 @@
         )(edge_rows, index_rows, hidden, edge_weight_in, row(edge_bias), node_weight_in, row(node_bias))
     with jax.named_scope("forward"):
         node_pair = shape(STATES * SHARE_NODE + SMALL, width)
-        act, slope, norm, inv, base, agg_grad, nsend, nkeep = call(
+        act, slope, norm, inv, node_grad_pre, agg_grad, nsend, nkeep = call(
             forward_kernel,
             (
                 shape(edges, width), shape(edges, width), shape(edges, width),
-                shape(edges, 1, dtype=F32), far(nodes, width, dtype=F32), shape(nodes, width),
+                shape(edges, 1, dtype=F32), far(nodes, width), shape(nodes, width),
                 node_pair, far(*node_pair.shape),
             ),
             None,
@@ -542,8 +547,17 @@
         groups = [[2 * chip + side for chip in range(chips)] for side in range(2)]
         arrived = lax.all_to_all(sent, "nodes", 0, 0, tiled=True, axis_index_groups=groups)
     with jax.named_scope("grad_nodes"):
-        grad_nodes = call(nodes_kernel, shape(nodes, width), limit=VMEM_FEW)(
-            back, send_rows.reshape(1, slots), *keep_far(sums, edge_weight_in, base)
+        near_weight = pl.BlockSpec((width, width), lambda i: (0, 0))
+        grad_nodes = call(
+            nodes_kernel, shape(nodes, width), (1,),
+            [
+                full(slots, width), full(1, slots), full(2 * nodes, width), full(3 * width, width),
+                full(nodes, width), near_weight, full(nodes, width),
+            ],
+            full(nodes, width), limit=VMEM_FEW,
+        )(
+            back, send_rows.reshape(1, slots),
+            *keep_far(sums, edge_weight_in, node_grad_pre, node_weight_in, ncot),
         )
     with jax.named_scope("weight_grads"):
         factor = 1.0 / math.sqrt(batch_size * edges * parts)

time: 99.4 us -> 99.3 us (level)
  transfers between devices with their start and end apart: 8 -> 8, of which waited for: 4 -> 4; matrix products, arithmetic and copies ran while one was open for 2% -> 2% of each run, Pallas kernels for 17% -> 18%
where the time goes in v4:
time: 99.3 us; the launch traced here: 98.7 us
  Pallas kernels  42.4 us (43%)
  waiting for transfers between devices  26.9 us (27%)
  starting transfers between devices  25.7 us (26%)
  local copies, waits for them, and re-layouts  1.59 us (2%)
  other arithmetic  1.34 us (1%)
    ppermute x3, waiting for transfers between devices, shards(): lax.ppermute(item, ALL, perm)  15.6 us
    pallas_call x1, Pallas kernels, shards(): call(backward_kernel, (far(edges, width), edge_pair, far(*edge_pair.shape...  11.3 us
    pallas_call x1, Pallas kernels, shards(): call(forward_kernel, (shape(edges, width), shape(edges, width), shape(edg...  10.6 us
    all_to_all x1, starting transfers between devices, shards(): lax.all_to_all(outgoing.reshape(parts, -1, width), 'nodes', 0, 0, tiled=T...  8.25 us
    all_to_all x1, waiting for transfers between devices, shards(): lax.all_to_all(sent, 'nodes', 0, 0, tiled=True, axis_index_groups=groups)  7.59 us
    all_to_all x1, starting transfers between devices, shards(): lax.all_to_all(sent, 'nodes', 0, 0, tiled=True, axis_index_groups=groups)  7.08 us
    pallas_call x1, Pallas kernels, shards(): call(local_kernel, (far(edges, width, dtype=F32), far(nodes, width, dtype...  6.68 us
    ppermute x3, starting transfers between devices, shards(): lax.ppermute(item, ALL, perm)  5.86 us
  transfers between devices with their start and end apart: 8, of which 4 were waited for; matrix products, arithmetic and copies ran while one was open for 2% of the time, Pallas kernels for 18%

profile of v4, /device:TPU:0, one launch (start us, length us, event | category | flops | bytes accessed | tf_op | source)
XLA Modules:
  0.0 98.7 jit_solution(17554103133788881184)
XLA Ops:
  0.6 2.3 %halo_rows.1 = bf16[512,512]{1,0:T(8,128)(2,1)} custom-call(s32[16,32]{1,0:T(8,128)} %bitcast.47, bf16[256,512]{1,0:T(8,128)(2,1)} %bitcast.32), custom_call_target="tpu_custom_call" | custom-call | tf_op jit(solution)/shard_map/halo_rows/pallas_call | solution.py:436
  2.9 8.3 %all-to-all-start = ((bf16[32,16,512]{2,1,0:T(8,128)(2,1)}), bf16[32,16,512]{2,1,0:T(8,128)(2,1)S(1)}, u32[]{:S(2)}, u32[]{:S(2)}) async-start(bf16[32,16,512]{2,1,0:T(8,128)(2,1)} %bitcast.12), calls=%async_computation | async-start | bytes 1048576 | tf_op jit(solution)/shard_map/halo_rows/all_to_all | solution.py:439
  11.2 1.3 %pad_add_fusion.rows_ref = s32[2,2048]{1,0:T(2,128)} fusion(s32[1,2048]{1,0:T(1,128)} %bitcast.48, s32[1,2048]{1,0:T(1,128)} %bitcast.49), kind=kLoop, calls=%fused_computation | loop fusion | flops 4096 | bytes 32768 | tf_op jit(solution)/shard_map/stack | solution.py:426
  12.5 0.0 copy-start.2
  12.5 0.0 copy-start.5
  12.5 0.0 copy-start.6
  12.5 6.7 %edge_pre_local.1 = (f32[2048,512]{1,0:T(8,128)}, f32[256,512]{1,0:T(8,128)}, bf16[256,512]{1,0:T(8,128)(2,1)}) custom-call(bf16[2048,512]{1,0:T(8,128)(2,1)} %bitcast.35, s32[2,2048]{1,0:T(2,128)} %pad_add_fusion.rows_ref, bf16[256,512]{1,0:T(8,128)(2,1)} %bitcast.33, bf16[1536,512]{1,0:T(8,128)(2,1)} %weight_ref.5, f32[1,512]{1,0:T(1,128)} %bitcast.50, ...), custom_call_target="tpu_custom_call" | custom-call | flops 2147483648 | bytes 6291456 | tf_op jit(solution)/shard_map/edge_pre_local/pallas_call | solution.py:447
  19.2 3.7 %all-to-all-done = bf16[32,16,512]{2,1,0:T(8,128)(2,1)S(1)} async-done(((bf16[32,16,512]{2,1,0:T(8,128)(2,1)}), bf16[32,16,512]{2,1,0:T(8,128)(2,1)S(1)}, u32[]{:S(2)}, u32[]{:S(2)}) %all-to-all-start) | async-done | bytes 524320 | tf_op jit(solution)/shard_map/halo_rows/all_to_all | solution.py:439
  22.9 0.0 copy-start.7
  22.9 0.8 copy-done.7
  23.7 0.0 copy-done.2
  23.7 0.0 copy-done.5
  23.7 0.0 copy-done.6
  23.7 0.0 copy-start
  23.7 0.0 copy-start.1
  23.7 0.0 copy-start.3
  23.7 0.0 copy-start.4
  23.8 10.6 %forward.1 = (bf16[2048,512]{1,0:T(8,128)(2,1)S(1)}, bf16[2048,512]{1,0:T(8,128)(2,1)S(1)}, bf16[2048,512]{1,0:T(8,128)(2,1)S(1)}, f32[2048,1]{1,0:T(8,128)S(1)}...) custom-call(s32[1]{0:T(128)} %bitcast.core_ref, ...), custom_call_target="tpu_custom_call" | custom-call | flops 3221225472 | bytes 12582912 | tf_op jit(solution)/shard_map/forward/pallas_call | solution.py:461
  34.4 0.0 copy-done
  34.4 0.0 copy-done.1
  34.4 0.0 copy-done.3
  34.4 0.0 copy-done.4
  34.5 11.3 %backward.1 = (bf16[2048,512]{1,0:T(8,128)(2,1)}, bf16[1040,512]{1,0:T(8,128)(2,1)}, bf16[1040,512]{1,0:T(8,128)(2,1)}, bf16[512,512]{1,0:T(8,128)(2,1)}, bf16[512,512]{1,0:T(8,128)(2,1)}) custom-call(s32[1]{0:T(128)} %bitcast.core_ref, bf16[2048,512]{1,0:T(8,128)(2,1)S(1)} %bitcast.30, s32[2,2048]{1,0:T(2,128)S(1)} %copy-done.2, ...), custom_call_target="tpu_custom_call" | custom-call | flops 6442450944 | bytes 14680064 | tf_op jit(solution)/shard_map/backward/pallas_call | solution.py:493
  45.8 0.1 collective-permute-start
  45.9 0.4 collective-permute-start.1
  46.4 3.9 %all-to-all-start.1 = ((bf16[32,16,512]{2,1,0:T(8,128)(2,1)}), bf16[32,16,512]{2,1,0:T(8,128)(2,1)S(1)}, u32[]{:S(2)}, u32[]{:S(2)}) async-start(bf16[32,16,512]{2,1,0:T(8,128)(2,1)} %bitcast.41), calls=%async_computation.1 | async-start | bytes 1048576 | tf_op jit(solution)/shard_map/halo_back/all_to_all | solution.py:518
  50.3 0.0 collective-permute-done.1.nrecv_ref
  50.3 0.0 collective-permute-done.recv_ref
  50.3 2.1 %pair_sum.1 = (bf16[464,512]{1,0:T(8,128)(2,1)S(1)}, bf16[464,512]{1,0:T(8,128)(2,1)S(1)}, bf16[464,512]{1,0:T(8,128)(2,1)S(1)}, bf16[464,512]{1,0:T(8,128)(2,1)S(1)}) custom-call(s32[1]{0:T(128)} %bitcast.18.batch_ref, bf16[1040,512]{1,0:T(8,128)(2,1)} %get-tuple-element.50.keep_ref, bf16[1040,512]{1,0:T(8,128)(2,1)S(1)} %collective-permute-done.recv_ref, ...), custom_call_target="tpu_custom_call" | custom-call | bytes 8388608 | tf_op jit(solution)/shard_map/pair_sum/pallas_call | solution.py:523
  52.5 1.6 %collective-permute-start.2 = (bf16[464,512]{1,0:T(8,128)(2,1)S(1)}, bf16[464,512]{1,0:T(8,128)(2,1)S(1)}, u32[]{:S(2)}, u32[]{:S(2)}) collective-permute-start(bf16[464,512]{1,0:T(8,128)(2,1)S(1)} %get-tuple-element.54), channel_id=1, source_target_pairs={{0,1},{1,2},{2,3},{3,0},{4,5},{5,6},{6,7},{7,4},{8,9},{9,10},{10,1... | collective-permute-start | bytes 1425416 | tf_op jit(solution)/shard_map/weight_states/ppermute | solution.py:529
  54.1 2.9 %collective-permute-start.3 = (bf16[464,512]{1,0:T(8,128)(2,1)S(1)}, bf16[464,512]{1,0:T(8,128)(2,1)S(1)}, u32[]{:S(2)}, u32[]{:S(2)}) collective-permute-start(bf16[464,512]{1,0:T(8,128)(2,1)S(1)} %get-tuple-element.55), channel_id=1, source_target_pairs={{0,2},{1,3},{2,0},{3,1},{4,6},{5,7},{6,4},{7,5},{8,10},{9,11},{10,... | collective-permute-start | bytes 1425416 | tf_op jit(solution)/shard_map/weight_states/ppermute | solution.py:529
  57.0 1.3 %collective-permute-start.4 = (bf16[464,512]{1,0:T(8,128)(2,1)S(1)}, bf16[464,512]{1,0:T(8,128)(2,1)S(1)}, u32[]{:S(2)}, u32[]{:S(2)}) collective-permute-start(bf16[464,512]{1,0:T(8,128)(2,1)S(1)} %get-tuple-element.56), channel_id=1, source_target_pairs={{0,3},{1,0},{2,1},{3,2},{4,7},{5,4},{6,5},{7,6},{8,11},{9,8},{10,9... | collective-permute-start | bytes 1425416 | tf_op jit(solution)/shard_map/weight_states/ppermute | solution.py:529
  58.3 4.2 %grad_edges.1 = bf16[2048,512]{1,0:T(8,128)(2,1)} custom-call(bf16[2048,512]{1,0:T(8,128)(2,1)} %bitcast.29, bf16[2048,512]{1,0:T(8,128)(2,1)} %get-tuple-element.57.pre_grad_ref, bf16[1536,512]{1,0:T(8,128)(2,1)} %weight_ref.5), custom_call_target="tpu_custom_call" | custom-call | flops 1073741824 | bytes 6291456 | tf_op jit(solution)/shard_map/grad_edges/pallas_call | solution.py:531
  62.5 0.0 copy-start.8
  62.5 4.2 %collective-permute-done.2.one_ref = bf16[464,512]{1,0:T(8,128)(2,1)S(1)} collective-permute-done((bf16[464,512]{1,0:T(8,128)(2,1)S(1)}, bf16[464,512]{1,0:T(8,128)(2,1)S(1)}, u32[]{:S(2)}, u32[]{:S(2)}) %collective-permute-start.2) | collective-permute-done | bytes 475168 | tf_op jit(solution)/shard_map/weight_states/ppermute | solution.py:529
  66.7 11.4 %collective-permute-done.3.two_ref = bf16[464,512]{1,0:T(8,128)(2,1)S(1)} collective-permute-done((bf16[464,512]{1,0:T(8,128)(2,1)S(1)}, bf16[464,512]{1,0:T(8,128)(2,1)S(1)}, u32[]{:S(2)}, u32[]{:S(2)}) %collective-permute-start.3) | collective-permute-done | bytes 475168 | tf_op jit(solution)/shard_map/weight_states/ppermute | solution.py:529
  78.1 0.0 collective-permute-done.4.three_ref
  78.1 1.2 %merge.1 = bf16[16,32,512]{2,1,0:T(8,128)(2,1)} custom-call(bf16[464,512]{1,0:T(8,128)(2,1)S(1)} %get-tuple-element.59.mine_ref, bf16[464,512]{1,0:T(8,128)(2,1)S(1)} %collective-permute-done.2.one_ref, bf16[464,512]{1,0:T(8,128)(2,1)S(1)} %collective-permute-done.3.two_ref, bf16[464,512]{1,0:T(8,128)(2,1)S(1)} %collective-permute-done.4.three_ref), custom_call_target="tpu_custom_call" | custom-call | tf_op jit(solution)/shard_map/merge/pallas_call | solution.py:541
  79.3 0.0 all-to-all-done.1
  79.3 7.1 %all-to-all-start.2 = ((bf16[16,32,512]{2,1,0:T(8,128)(2,1)}), bf16[16,32,512]{2,1,0:T(8,128)(2,1)S(1)}, u32[]{:S(2)}, u32[]{:S(2)}) async-start(bf16[16,32,512]{2,1,0:T(8,128)(2,1)} %merge.1), calls=%async_computation.2 | async-start | bytes 1048576 | tf_op jit(solution)/shard_map/chip_exchange/all_to_all | solution.py:548
  86.4 0.0 copy-done.8
  86.4 0.1 copy.26
  86.5 0.1 reshape.63.rows_ref
  86.6 3.3 %grad_nodes.1 = bf16[256,512]{1,0:T(8,128)(2,1)} custom-call(bf16[512,512]{1,0:T(8,128)(2,1)S(1)} %bitcast.31, s32[1,512]{1,0:T(1,128)S(1)} %reshape.63.rows_ref, bf16[512,512]{1,0:T(8,128)(2,1)} %get-tuple-element.48.sums_ref, bf16[1536,512]{1,0:T(8,128)(2,1)} %weight_ref.5, bf16[256,512]{1,0:T(8,128)(2,1)} %get-tuple-element.49.grad_pre_ref, ...), custom_call_target="tpu_custom_call" | custom-call | tf_op jit(solution)/shard_map/grad_nodes/pallas_call | solution.py:551
  89.8 7.6 %all-to-all-done.2.arrived_ref = bf16[16,32,512]{2,1,0:T(8,128)(2,1)S(1)} async-done(((bf16[16,32,512]{2,1,0:T(8,128)(2,1)}), bf16[16,32,512]{2,1,0:T(8,128)(2,1)S(1)}, u32[]{:S(2)}, u32[]{:S(2)}) %all-to-all-start.2) | async-done | bytes 524320 | tf_op jit(solution)/shard_map/chip_exchange/all_to_all | solution.py:548
  97.4 0.7 weight_grads.1
  98.1 0.1 constant_dynamic-slice_fusion
  98.2 0.5 slice_bitcast_fusion
Async XLA Ops:
  2.9 20.0 %all-to-all-start = ((bf16[32,16,512]{2,1,0:T(8,128)(2,1)}), bf16[32,16,512]{2,1,0:T(8,128)(2,1)S(1)}, u32[]{:S(2)}, u32[]{:S(2)}) async-start(bf16[32,16,512]{2,1,0:T(8,128)(2,1)} %bitcast.12), calls=%async_computation | async-start | bytes 1048576 | tf_op jit(solution)/shard_map/halo_rows/all_to_all | solution.py:439
  12.5 11.2 %copy-start.2 = (s32[2,2048]{1,0:T(2,128)S(1)}, s32[2,2048]{1,0:T(2,128)}, u32[]{:S(2)}) copy-start(s32[2,2048]{1,0:T(2,128)} %pad_add_fusion.rows_ref) | copy-start | bytes 49156
  12.5 11.2 %copy-start.5 = (f32[512]{0:T(512)S(1)}, f32[512]{0:T(512)}, u32[]{:S(2)}) copy-start(f32[512]{0:T(512)} %param.29) | copy-start | bytes 6148
  12.5 11.2 %copy-start.6 = (f32[512]{0:T(512)S(1)}, f32[512]{0:T(512)}, u32[]{:S(2)}) copy-start(f32[512]{0:T(512)} %param.25) | copy-start | bytes 6148
  22.9 0.8 copy-start.7
  23.7 10.7 %copy-start = (bf16[1,2048,512]{2,1,0:T(8,128)(2,1)S(1)}, bf16[1,2048,512]{2,1,0:T(8,128)(2,1)}, u32[]{:S(2)}) copy-start(bf16[1,2048,512]{2,1,0:T(8,128)(2,1)} %param.18) | copy-start | bytes 6291460
  23.7 10.7 %copy-start.1 = (bf16[1,256,512]{2,1,0:T(8,128)(2,1)S(1)}, bf16[1,256,512]{2,1,0:T(8,128)(2,1)}, u32[]{:S(2)}) copy-start(bf16[1,256,512]{2,1,0:T(8,128)(2,1)} %param.15) | copy-start | bytes 786436
  23.7 10.7 %copy-start.3 = (bf16[1,2048,512]{2,1,0:T(8,128)(2,1)S(1)}, bf16[1,2048,512]{2,1,0:T(8,128)(2,1)}, u32[]{:S(2)}) copy-start(bf16[1,2048,512]{2,1,0:T(8,128)(2,1)} %param.16) | copy-start | bytes 6291460
  23.7 10.7 %copy-start.4 = (bf16[512,512]{1,0:T(8,128)(2,1)S(1)}, bf16[512,512]{1,0:T(8,128)(2,1)}, u32[]{:S(2)}) copy-start(bf16[512,512]{1,0:T(8,128)(2,1)} %weight_out_ref.1) | copy-start | bytes 1572868
  45.8 4.5 %collective-permute-start = (bf16[1040,512]{1,0:T(8,128)(2,1)}, bf16[1040,512]{1,0:T(8,128)(2,1)S(1)}, u32[]{:S(2)}, u32[]{:S(2)}) collective-permute-start(bf16[1040,512]{1,0:T(8,128)(2,1)} %get-tuple-element.51), channel_id=1, source_target_pairs={{0,4},{1,5},{2,6},{3,7},{4,0},{5,1},{6,2},{7,3},{8,12},{9,13},{10,... | collective-permute-start | bytes 3194888 | tf_op jit(solution)/shard_map/edge_weight_pair/ppermute | solution.py:516
  45.9 4.3 %collective-permute-start.1 = (bf16[784,512]{1,0:T(8,128)(2,1)}, bf16[784,512]{1,0:T(8,128)(2,1)S(1)}, u32[]{:S(2)}, u32[]{:S(2)}) collective-permute-start(bf16[784,512]{1,0:T(8,128)(2,1)} %get-tuple-element.53), channel_id=1, source_target_pairs={{0,4},{1,5},{2,6},{3,7},{4,0},{5,1},{6,2},{7,3},{8,12},{9,13},{10,... | collective-permute-start | bytes 2408456 | tf_op jit(solution)/shard_map/node_weight_pair/ppermute | solution.py:490
  46.4 32.9 %all-to-all-start.1 = ((bf16[32,16,512]{2,1,0:T(8,128)(2,1)}), bf16[32,16,512]{2,1,0:T(8,128)(2,1)S(1)}, u32[]{:S(2)}, u32[]{:S(2)}) async-start(bf16[32,16,512]{2,1,0:T(8,128)(2,1)} %bitcast.41), calls=%async_computation.1 | async-start | bytes 1048576 | tf_op jit(solution)/shard_map/halo_back/all_to_all | solution.py:518
  52.5 14.2 %collective-permute-start.2 = (bf16[464,512]{1,0:T(8,128)(2,1)S(1)}, bf16[464,512]{1,0:T(8,128)(2,1)S(1)}, u32[]{:S(2)}, u32[]{:S(2)}) collective-permute-start(bf16[464,512]{1,0:T(8,128)(2,1)S(1)} %get-tuple-element.54), channel_id=1, source_target_pairs={{0,1},{1,2},{2,3},{3,0},{4,5},{5,6},{6,7},{7,4},{8,9},{9,10},{10,1... | collective-permute-start | bytes 1425416 | tf_op jit(solution)/shard_map/weight_states/ppermute | solution.py:529
  54.1 24.0 %collective-permute-start.3 = (bf16[464,512]{1,0:T(8,128)(2,1)S(1)}, bf16[464,512]{1,0:T(8,128)(2,1)S(1)}, u32[]{:S(2)}, u32[]{:S(2)}) collective-permute-start(bf16[464,512]{1,0:T(8,128)(2,1)S(1)} %get-tuple-element.55), channel_id=1, source_target_pairs={{0,2},{1,3},{2,0},{3,1},{4,6},{5,7},{6,4},{7,5},{8,10},{9,11},{10,... | collective-permute-start | bytes 1425416 | tf_op jit(solution)/shard_map/weight_states/ppermute | solution.py:529
  57.0 21.1 %collective-permute-start.4 = (bf16[464,512]{1,0:T(8,128)(2,1)S(1)}, bf16[464,512]{1,0:T(8,128)(2,1)S(1)}, u32[]{:S(2)}, u32[]{:S(2)}) collective-permute-start(bf16[464,512]{1,0:T(8,128)(2,1)S(1)} %get-tuple-element.56), channel_id=1, source_target_pairs={{0,3},{1,0},{2,1},{3,2},{4,7},{5,4},{6,5},{7,6},{8,11},{9,8},{10,9... | collective-permute-start | bytes 1425416 | tf_op jit(solution)/shard_map/weight_states/ppermute | solution.py:529
  62.5 23.9 %copy-start.8 = (s32[1,32,16]{1,2,0:T(8,128)S(1)}, s32[1,32,16]{1,2,0:T(8,128)}, u32[]{:S(2)}) copy-start(s32[1,32,16]{1,2,0:T(8,128)} %param.21) | copy-start | bytes 6148
  79.3 18.1 %all-to-all-start.2 = ((bf16[16,32,512]{2,1,0:T(8,128)(2,1)}), bf16[16,32,512]{2,1,0:T(8,128)(2,1)S(1)}, u32[]{:S(2)}, u32[]{:S(2)}) async-start(bf16[16,32,512]{2,1,0:T(8,128)(2,1)} %merge.1), calls=%async_computation.2 | async-start | bytes 1048576 | tf_op jit(solution)/shard_map/chip_exchange/all_to_all | solution.py:548
